TPU v7x, 32 devices: a whole 2x2x4 slice. The times are simulated.
32 devices in a mesh: dp: 8 (over z, y), grp: 4 (over x, core).
Axes of the slice: x: 2, y: 2, z: 4, core: 2. Of those that a mesh axis runs over, the one named last changes fastest.
Arguments:
- patches: bfloat16 [27648, 1728], P(('dp', 'grp')), may hold values from -6 to 6
- segments: int32 [27648], P(('dp', 'grp')), may hold values from -1 to 73, as said below
- visible: int32 [3072], P(('dp', 'grp')), may hold values from 0 to 3455, as said below
- enc_params: float32 [66048, 128], P('dp')
- enc_first: float32 [66048, 128], P('dp'), may hold values from -8.34465e-07 to 8.34465e-07
- enc_second: float32 [66048, 128], P('dp'), may hold values from 3.0982314e-15 to 1.23929255e-14
- enc_average: float32 [66048, 128], P('dp')
- dec_params: float32 [34816, 128], P('dp')
- dec_first: float32 [34816, 128], P('dp'), may hold values from -8.34465e-07 to 8.34465e-07
- dec_second: float32 [34816, 128], P('dp'), may hold values from 3.0982314e-15 to 1.23929255e-14
- step_count: int32 [1], replicated, may hold values from 1 to 20
Outputs:
- new_enc_params: float32 [66048, 128], P('dp')
- new_enc_first: float32 [66048, 128], P('dp')
- new_enc_second: float32 [66048, 128], P('dp')
- new_enc_copy: bfloat16 [66048, 128], P('dp')
- new_dec_params: float32 [34816, 128], P('dp')
- new_dec_first: float32 [34816, 128], P('dp')
- new_dec_second: float32 [34816, 128], P('dp')
- new_dec_copy: bfloat16 [34816, 128], P('dp')
- new_enc_average: float32 [66048, 128], P('dp')
- grad_norm: float32 [], replicated
- loss: float32 [], replicated
- count: float32 [], replicated
Inputs may be any that keep to these rules, and one draw needn't show every extreme that they name: `segments`: within a group, each of the 2 sequences holds whole tiles of 48 to 192 slots from its start, and padding (-1) only after its last tile. The tiles of sequence s are numbered consecutively, ending with (s + 1) * 37 - 1. `visible`: slots of the device's group, distinct over the group, never padding. Each device has exactly 96 encoder rows; at most 48 of one device's rows name slots held by one device of its group, and in every group some such pair has exactly 48; every device of a group holds exactly 96 named slots.
All inputs are finite; a program needn't handle non-finite values.
Results may differ from a plain program's by a relative error of at most 0.00065.
The roundings to bfloat16 on the way count: a program that leaves them out, or rounds other values in their place, can miss the bound.
Values may be sent and summed in bfloat16 or wider, within the bound.
No kernel may reach another device: no remote copies, remote signals or barrier semaphores. Data moves between devices by JAX's collectives and lax.ppermute only.
A program may use at most 320 MiB of HBM per device.

v0:
```python
import math

import jax
import jax.numpy as jnp
from jax import lax
from jax.sharding import PartitionSpec as P

D = 768
H = 12
F = 3072
E = 512
EH = 16
FE = 2048
PATCH = 1728
L = 1728
TILE_HI = 192
ER = 66048
DR = 34816


NORM_EPS = 1e-06
MASK_FILL = -1e30
CLIP_LIMIT = 0.0002
LEARN_RATE = 0.02
BETA_ONE = 0.5
BETA_TWO = 0.5
ADAM_EPS = 1e-08
WEIGHT_DECAY = 0.05
EMA_RATE = 0.9


def for_sending(x):

    def short(part):
        return part.astype(jnp.bfloat16) if part.dtype == jnp.float32 else part

    return jax.tree.map(short, x)


def extended(cells, sides, width):
    for axis, dim in sides:
        count = lax.axis_size(axis)
        ends = count - 1
        head = lax.slice_in_dim(cells, 0, width, axis=dim)
        tail = lax.slice_in_dim(cells, cells.shape[dim] - width, cells.shape[dim], axis=dim)
        cells = jnp.concatenate(
            [
                lax.ppermute(tail, axis, [(i, (i + 1) % count) for i in range(ends)]),
                cells,
                lax.ppermute(head, axis, [((i + 1) % count, i) for i in range(ends)]),
            ],
            axis=dim,
        )
    return cells


def passed_along(block, axis, distance):
    devices = range(lax.axis_size(axis))
    route = [(i - distance, i) for i in devices if i - distance in devices]
    return lax.ppermute(block, axis, route)


def enc_pieces():
    return [
        ("patch_w", (PATCH, D)),
        ("qkv_w", (D, 3 * D)),
        ("out_w", (D, D)),
        ("up_w", (D, F)),
        ("down_w", (F, D)),
        ("patch_b", (D,)),
        ("out_b", (D,)),
        ("up_b", (F,)),
        ("down_b", (D,)),
        ("norm_g", (3, D)),
        ("norm_b", (3, D)),
    ]


def dec_pieces():
    return [
        ("embed_w", (D, E)),
        ("qkv_w", (E, 3 * E)),
        ("out_w", (E, E)),
        ("up_w", (E, FE)),
        ("down_w", (FE, E)),
        ("pix_w", (E, PATCH)),
        ("embed_b", (E,)),
        ("mask_token", (E,)),
        ("out_b", (E,)),
        ("up_b", (FE,)),
        ("down_b", (E,)),
        ("pix_b", (PATCH,)),
        ("norm_g", (3, E)),
        ("norm_b", (3, E)),
    ]


def unpack(flat_vec, pieces):
    table = {}
    offset = 0
    for piece_name, piece_dims in pieces:
        amount = math.prod(piece_dims)
        table[piece_name] = flat_vec[offset : offset + amount].reshape(piece_dims)
        offset += amount
    return table


def pack(table, pieces, total_rows):
    joined = jnp.concatenate([table[piece_name].reshape(-1) for piece_name, piece_dims in pieces])
    return jnp.pad(joined, (0, total_rows * 128 - joined.shape[0])).reshape(total_rows, 128)


def matmul(left, right):
    return jnp.dot(left, right, preferred_element_type=jnp.float32)


def mul_trans(left, right):
    return lax.dot_general(
        left, right, (((1,), (1,)), ((), ())), preferred_element_type=jnp.float32
    )


def trans_mul(left, right):
    return lax.dot_general(
        left, right, (((0,), (0,)), ((), ())), preferred_element_type=jnp.float32
    )


def sincos(positions, width):
    half_width = width // 2
    freq_row = jnp.exp(
        jnp.arange(half_width, dtype=jnp.float32) * (-2.0 * math.log(10000.0) / width)
    )
    angles = positions.astype(jnp.float32)[:, None] * freq_row[None, :]
    return jnp.concatenate([jnp.sin(angles), jnp.cos(angles)], axis=1)


def layer_norm(inputs, gain, shift):
    center = inputs - jnp.mean(inputs, axis=-1, keepdims=True)
    return (
        center * lax.rsqrt(jnp.mean(center * center, axis=-1, keepdims=True) + NORM_EPS) * gain
        + shift
    )


def norm_back(inputs, gain, shift, grad_out):
    outputs, pull = jax.vjp(layer_norm, inputs, gain, shift)
    return pull(grad_out)


def exact_gelu(values):
    return jax.nn.gelu(values, approximate=False)


def head_scores(query, keys, index, width, allowed, scale):
    query_head = lax.dynamic_slice_in_dim(query, index * width, width, 1)
    key_head = lax.dynamic_slice_in_dim(keys, index * width, width, 1)
    scores = mul_trans(query_head, key_head) * scale
    return (jnp.where(allowed, scores, MASK_FILL), query_head, key_head)


def attend(query, keys, values, allowed, heads):
    width = query.shape[1] // heads
    scale = width ** (-0.5)

    def one_head(index):
        scores, query_head, key_head = head_scores(query, keys, index, width, allowed, scale)
        value_head = lax.dynamic_slice_in_dim(values, index * width, width, 1)
        largest = jnp.max(scores, axis=1, keepdims=True)
        log_total = largest + jnp.log(jnp.sum(jnp.exp(scores - largest), axis=1, keepdims=True))
        probs = jnp.exp(scores - log_total).astype(jnp.bfloat16)
        return (matmul(probs, value_head), log_total[:, 0])

    outputs, log_totals = lax.map(one_head, jnp.arange(heads, dtype=jnp.int32))
    return (outputs.transpose(1, 0, 2).reshape(query.shape[0], -1).astype(jnp.bfloat16), log_totals)


def attend_back(query, keys, values, allowed, heads, log_totals, out_grad):
    width = query.shape[1] // heads
    scale = width ** (-0.5)

    def one_head(index):
        scores, query_head, key_head = head_scores(query, keys, index, width, allowed, scale)
        value_head = lax.dynamic_slice_in_dim(values, index * width, width, 1)
        grad_head = lax.dynamic_slice_in_dim(out_grad, index * width, width, 1)
        probs = jnp.exp(scores - log_totals[index][:, None])
        value_grad = trans_mul(probs.astype(jnp.bfloat16), grad_head)
        prob_grad = mul_trans(grad_head, value_head)
        score_grad = (
            probs * (prob_grad - jnp.sum(probs * prob_grad, axis=1, keepdims=True))
        ).astype(jnp.bfloat16)
        query_grad = matmul(score_grad, key_head) * scale
        key_grad = trans_mul(score_grad, query_head) * scale
        return (query_grad, key_grad, value_grad)

    members = lax.map(one_head, jnp.arange(heads, dtype=jnp.int32))
    return tuple((member.transpose(1, 0, 2).reshape(member.shape[1], -1) for member in members))


def block_forward(inputs, table, heads, allowed, share_keys):
    gains = table["norm_g"].astype(jnp.float32)
    shifts = table["norm_b"].astype(jnp.float32)
    width = inputs.shape[1]
    normed_one = layer_norm(inputs, gains[0], shifts[0]).astype(jnp.bfloat16)
    qkv = matmul(normed_one, table["qkv_w"]).astype(jnp.bfloat16)
    query = qkv[:, :width]
    all_keys, all_values = share_keys((qkv[:, width : 2 * width], qkv[:, 2 * width :]))
    attended, log_totals = attend(query, all_keys, all_values, allowed, heads)
    mixed = inputs + (matmul(attended, table["out_w"]) + table["out_b"].astype(jnp.float32))
    normed_two = layer_norm(mixed, gains[1], shifts[1]).astype(jnp.bfloat16)
    hidden = matmul(normed_two, table["up_w"]) + table["up_b"].astype(jnp.float32)
    activated = exact_gelu(hidden).astype(jnp.bfloat16)
    result = mixed + (matmul(activated, table["down_w"]) + table["down_b"].astype(jnp.float32))
    saved = (
        inputs,
        normed_one,
        query,
        all_keys,
        all_values,
        attended,
        log_totals,
        mixed,
        normed_two,
        hidden,
        activated,
    )
    return (result, saved)


def block_backward(grad_out, table, heads, allowed, saved, return_keys):
    (
        inputs,
        normed_one,
        query,
        all_keys,
        all_values,
        attended,
        log_totals,
        mixed,
        normed_two,
        hidden,
        activated,
    ) = saved
    gains = table["norm_g"].astype(jnp.float32)
    shifts = table["norm_b"].astype(jnp.float32)
    grads = {}
    down_grad = grad_out.astype(jnp.bfloat16)
    grads["down_w"] = trans_mul(activated, down_grad)
    grads["down_b"] = jnp.sum(down_grad.astype(jnp.float32), axis=0)
    act_grad = mul_trans(down_grad, table["down_w"])
    gelu_out, gelu_pull = jax.vjp(exact_gelu, hidden)
    hidden_grad = gelu_pull(act_grad)[0].astype(jnp.bfloat16)
    grads["up_w"] = trans_mul(normed_two, hidden_grad)
    grads["up_b"] = jnp.sum(hidden_grad.astype(jnp.float32), axis=0)
    mixed_part, gain_two, shift_two = norm_back(
        mixed, gains[1], shifts[1], mul_trans(hidden_grad, table["up_w"])
    )
    mixed_grad = grad_out + mixed_part
    branch_grad = mixed_grad.astype(jnp.bfloat16)
    grads["out_w"] = trans_mul(attended, branch_grad)
    grads["out_b"] = jnp.sum(branch_grad.astype(jnp.float32), axis=0)
    attended_grad = mul_trans(branch_grad, table["out_w"]).astype(jnp.bfloat16)
    query_grad, keys_grad_all, values_grad_all = attend_back(
        query, all_keys, all_values, allowed, heads, log_totals, attended_grad
    )
    keys_grad, values_grad = return_keys((keys_grad_all, values_grad_all))
    qkv_grad = jnp.concatenate([query_grad, keys_grad, values_grad], axis=1).astype(jnp.bfloat16)
    grads["qkv_w"] = trans_mul(normed_one, qkv_grad)
    input_part, gain_one, shift_one = norm_back(
        inputs, gains[0], shifts[0], mul_trans(qkv_grad, table["qkv_w"])
    )
    return (mixed_grad + input_part, grads, (gain_one, shift_one, gain_two, shift_two))


def adamw(weights, first, second, gradient, factor, steps_done):
    clipped = gradient * factor
    first_new = BETA_ONE * first + (1.0 - BETA_ONE) * clipped
    second_new = BETA_TWO * second + (1.0 - BETA_TWO) * clipped * clipped
    first_hat = first_new / (1.0 - BETA_ONE**steps_done)
    second_hat = second_new / (1.0 - BETA_TWO**steps_done)
    weights_new = weights * (1.0 - LEARN_RATE * WEIGHT_DECAY) - LEARN_RATE * first_hat / (
        jnp.sqrt(second_hat) + ADAM_EPS
    )
    return (weights_new, first_new, second_new)


def per_device(
    patches,
    segments,
    visible,
    enc_params,
    enc_first,
    enc_second,
    enc_average,
    dec_params,
    dec_first,
    dec_second,
    step_count,
):
    groups = lax.axis_size("grp")
    my_index = lax.axis_index("grp")
    slot_dev = segments.shape[0]
    vis_rows = visible.shape[0]
    capacity = vis_rows // 2
    enc_copy, dec_copy = (
        lax.all_gather(enc_params.astype(jnp.bfloat16), "dp", axis=0, tiled=True),
        lax.all_gather(dec_params.astype(jnp.bfloat16), "dp", axis=0, tiled=True),
    )
    enc_table = unpack(enc_copy.reshape(-1), enc_pieces())
    dec_table = unpack(dec_copy.reshape(-1), dec_pieces())
    group_seg, group_vis = (
        lax.all_gather(segments, "grp", axis=0, tiled=True),
        lax.all_gather(visible, "grp", axis=0, tiled=True),
    )
    vis_table = group_vis.reshape(groups, vis_rows)
    source = vis_table // slot_dev
    local_slot = vis_table % slot_dev
    row_ids = jnp.arange(vis_rows, dtype=jnp.int32)
    earlier = row_ids[None, :] < row_ids[:, None]
    same_source = source[:, :, None] == source[:, None, :]
    ranking = jnp.sum((same_source & earlier[None]).astype(jnp.int32), axis=2)
    recv_index = jnp.take(source, my_index, axis=0) * capacity + jnp.take(ranking, my_index, axis=0)
    matched = (source == my_index)[:, :, None] & (
        ranking[:, :, None] == jnp.arange(capacity, dtype=jnp.int32)[None, None, :]
    )
    picked = jnp.sum(jnp.where(matched, local_slot[:, :, None], 0), axis=1).reshape(-1)
    filled = jnp.any(matched, axis=1).reshape(-1)
    outgoing = jnp.where(filled[:, None], patches[picked], jnp.zeros((), jnp.bfloat16))
    enc_input = lax.all_to_all(outgoing, "grp", split_axis=0, concat_axis=0, tiled=True)[recv_index]
    own_slots = jnp.take(vis_table, my_index, axis=0)
    enc_allowed = group_seg[own_slots][:, None] == group_seg[group_vis][None, :]
    enc_start = (
        matmul(enc_input, enc_table["patch_w"])
        + enc_table["patch_b"].astype(jnp.float32)
        + sincos(own_slots % L, D)
    )
    enc_out, enc_saved = block_forward(
        enc_start,
        enc_table,
        H,
        enc_allowed,
        lambda pair: jax.tree.map(
            lambda part, own: part.astype(own.dtype),
            lax.all_gather(for_sending(pair), "grp", axis=0, tiled=True),
            pair,
        ),
    )
    enc_gain = enc_table["norm_g"].astype(jnp.float32)
    enc_shift = enc_table["norm_b"].astype(jnp.float32)
    enc_final = layer_norm(enc_out, enc_gain[2], enc_shift[2]).astype(jnp.bfloat16)
    latent = (
        matmul(enc_final, dec_table["embed_w"]) + dec_table["embed_b"].astype(jnp.float32)
    ).astype(jnp.bfloat16)
    parcel = jnp.zeros((groups * capacity, E), jnp.bfloat16).at[recv_index].set(latent)
    arrived = lax.all_to_all(parcel, "grp", split_axis=0, concat_axis=0, tiled=True)
    placed = (
        jnp.zeros((slot_dev, E), jnp.float32)
        .at[picked]
        .add(jnp.where(filled[:, None], arrived.astype(jnp.float32), 0.0))
    )
    seen = jnp.zeros((slot_dev,), jnp.float32).at[picked].add(filled.astype(jnp.float32)) > 0.5
    positions = (my_index * slot_dev + jnp.arange(slot_dev, dtype=jnp.int32)) % L
    dec_start = jnp.where(
        seen[:, None], placed, dec_table["mask_token"].astype(jnp.float32)[None, :]
    ) + sincos(positions, E)
    counted = jnp.where((segments >= 0) & jnp.logical_not(seen), 1.0, 0.0)
    total_count = lax.psum(jnp.sum(counted), ("dp", "grp"))
    rim = TILE_HI
    outside = jnp.full((rim,), -2, jnp.int32)
    key_ids = lax.dynamic_slice_in_dim(
        jnp.concatenate([outside, group_seg, outside]), my_index * slot_dev, slot_dev + 2 * rim
    )
    dec_allowed = segments[:, None] == key_ids[None, :]

    def dec_share(pair):
        joined = extended(for_sending(jnp.concatenate(pair, axis=1)), (("grp", 0),), rim)
        return (joined[:, :E], joined[:, E:])

    def dec_return(pair):
        joined = jnp.concatenate(pair, axis=1)
        from_upper = passed_along(joined[:rim], "grp", -1)
        from_lower = passed_along(joined[rim + slot_dev :], "grp", 1)
        middle = joined[rim : rim + slot_dev]
        middle = middle.at[:rim].add(from_lower).at[slot_dev - rim :].add(from_upper)
        return (middle[:, :E], middle[:, E:])

    dec_out, dec_saved = block_forward(dec_start, dec_table, EH, dec_allowed, dec_share)
    dec_gain = dec_table["norm_g"].astype(jnp.float32)
    dec_shift = dec_table["norm_b"].astype(jnp.float32)
    dec_final = layer_norm(dec_out, dec_gain[2], dec_shift[2]).astype(jnp.bfloat16)
    predicted = matmul(dec_final, dec_table["pix_w"]) + dec_table["pix_b"].astype(jnp.float32)
    pixels = patches.astype(jnp.float32)
    centered = pixels - jnp.mean(pixels, axis=1, keepdims=True)
    target = centered * lax.rsqrt(jnp.mean(centered * centered, axis=1, keepdims=True) + NORM_EPS)
    errors = predicted - target
    loss_part = jnp.sum(counted * jnp.mean(errors * errors, axis=1))
    pred_grad = (counted[:, None] * errors * (2.0 / PATCH) / total_count).astype(jnp.bfloat16)
    dec_grads = {}
    dec_grads["pix_w"] = trans_mul(dec_final, pred_grad)
    dec_grads["pix_b"] = jnp.sum(pred_grad.astype(jnp.float32), axis=0)
    dec_out_grad, dec_gain_last, dec_shift_last = norm_back(
        dec_out, dec_gain[2], dec_shift[2], mul_trans(pred_grad, dec_table["pix_w"])
    )
    start_grad, block_grads, dec_small = block_backward(
        dec_out_grad, dec_table, EH, dec_allowed, dec_saved, dec_return
    )
    dec_grads.update(block_grads)
    dec_grads["norm_g"] = jnp.stack([dec_small[0], dec_small[2], dec_gain_last])
    dec_grads["norm_b"] = jnp.stack([dec_small[1], dec_small[3], dec_shift_last])
    dec_grads["mask_token"] = jnp.sum(jnp.where(seen[:, None], 0.0, start_grad), axis=0)
    returned = jnp.where(filled[:, None], start_grad[picked], 0.0).astype(jnp.bfloat16)
    latent_grad = lax.all_to_all(returned, "grp", split_axis=0, concat_axis=0, tiled=True)[
        recv_index
    ]
    dec_grads["embed_w"] = trans_mul(enc_final, latent_grad)
    dec_grads["embed_b"] = jnp.sum(latent_grad.astype(jnp.float32), axis=0)
    enc_out_grad, enc_gain_last, enc_shift_last = norm_back(
        enc_out, enc_gain[2], enc_shift[2], mul_trans(latent_grad, dec_table["embed_w"])
    )
    enc_start_grad, enc_grads, enc_small = block_backward(
        enc_out_grad,
        enc_table,
        H,
        enc_allowed,
        enc_saved,
        lambda pair: lax.psum_scatter(pair, "grp", scatter_dimension=0, tiled=True),
    )
    enc_grads["norm_g"] = jnp.stack([enc_small[0], enc_small[2], enc_gain_last])
    enc_grads["norm_b"] = jnp.stack([enc_small[1], enc_small[3], enc_shift_last])
    patch_grad = enc_start_grad.astype(jnp.bfloat16)
    enc_grads["patch_w"] = trans_mul(enc_input, patch_grad)
    enc_grads["patch_b"] = jnp.sum(patch_grad.astype(jnp.float32), axis=0)
    enc_flat = pack(enc_grads, enc_pieces(), ER)
    dec_flat = pack(dec_grads, dec_pieces(), DR)
    enc_sum, dec_sum, loss_group = lax.psum((enc_flat, dec_flat, loss_part), "grp")
    enc_red, dec_red = lax.psum_scatter((enc_sum, dec_sum), "dp", scatter_dimension=0, tiled=True)
    total_sq, loss_total = lax.psum(
        (jnp.sum(enc_red * enc_red) + jnp.sum(dec_red * dec_red), loss_group), "dp"
    )
    grad_norm = jnp.sqrt(total_sq)
    factor = jnp.minimum(1.0, CLIP_LIMIT / (grad_norm + NORM_EPS))
    steps_done = step_count[0].astype(jnp.float32)
    enc_new, enc_first_new, enc_second_new = adamw(
        enc_params, enc_first, enc_second, enc_red, factor, steps_done
    )
    dec_new, dec_first_new, dec_second_new = adamw(
        dec_params, dec_first, dec_second, dec_red, factor, steps_done
    )
    average_new = EMA_RATE * enc_average + (1.0 - EMA_RATE) * enc_new
    return (
        enc_new,
        enc_first_new,
        enc_second_new,
        enc_new.astype(jnp.bfloat16),
        dec_new,
        dec_first_new,
        dec_second_new,
        dec_new.astype(jnp.bfloat16),
        average_new,
        grad_norm,
        loss_total,
        total_count,
    )


def solution(mesh):
    placed = (
        P(("dp", "grp"), None),
        P(("dp", "grp")),
        P(("dp", "grp")),
        P("dp", None),
        P("dp", None),
        P("dp", None),
        P("dp", None),
        P("dp", None),
        P("dp", None),
        P("dp", None),
        P(),
    )
    return jax.shard_map(
        per_device,
        mesh=mesh,
        in_specs=placed,
        out_specs=(
            P("dp", None),
            P("dp", None),
            P("dp", None),
            P("dp", None),
            P("dp", None),
            P("dp", None),
            P("dp", None),
            P("dp", None),
            P("dp", None),
            P(),
            P(),
            P(),
        ),
        check_vma=False,
    )
```

profile of v0, /device:TPU:0, one launch (start us, length us, event | category | flops | bytes accessed | tf_op | source)
XLA Modules:
  0.0 2687.2 jit_solution(68129003405545293)
XLA Ops:
  16.0 13.2 all-reduce.4
  57.8 87.4 %all-gather.5.cloned.1.call-done = bf16[34816,128]{1,0:T(8,128)(2,1)} async-done(((bf16[4352,128]{1,0:T(8,128)(2,1)}), bf16[34816,128]{1,0:T(8,128)(2,1)}) %all-gather.5.cloned.1.call-update) | async-done | bytes 8912912 | tf_op jit(solution)/shard_map/all_gather | solution.py:307
  183.2 287.8 %all-gather.3.cloned.1.call-done = bf16[66048,128]{1,0:T(8,128)(2,1)} async-done(((bf16[8256,128]{1,0:T(8,128)(2,1)}), bf16[66048,128]{1,0:T(8,128)(2,1)}) %all-gather.3.cloned.1.call-update) | async-done | bytes 16908304 | tf_op jit(solution)/shard_map/all_gather | solution.py:306
  474.0 5.8 reshape.753
  487.3 7.6 reshape.754
  499.1 8.0 all_gather.20
  507.1 8.6 all_gather.22
  516.9 77.3 %while.59 = (s32[]{:T(128)}, bf16[12,96,64]{1,2,0:T(8,128)(2,1)}, f32[12,96]{1,0:T(8,128)}, s32[12]{0:T(128)}, bf16[96,768]{1,0:T(8,128)(2,1)S(1)}, /*index=5*/b...) while((s32[]{:T(128)}, bf16[12,96,64]{1,2,0:T(8,128)(2,1)}, ...), condition=%wide.region_9.11_spmd.clone, body=%wide.region_6.10_spmd.clone.sunk | while | flops 9732006 | bytes 705627 | solution.py:174
  602.8 8.3 fusion.158
  611.1 8.2 reshape.756
  619.3 9.3 reshape.757
  629.4 7.2 multiply_convert_fusion.3
  643.9 5.2 all-to-all-done.1
  665.8 130.2 %while.60 = (s32[]{:T(128)}, bf16[16,864,32]{1,2,0:T(8,128)(2,1)}, f32[16,864]{1,0:T(8,128)}, s32[16]{0:T(128)S(1)}, bf16[864,512]{1,0:T(8,128)(2,1)}, /*index=5...) while((s32[]{:T(128)}, bf16[16,864,32]{1,2,0:T(8,128)(2,1)}, ...), condition=%wide.region_21.23_spmd.clone, body=%wide.region_18.22_spmd.clone.sunk | while | flops 146644128 | bytes 13962303 | solution.py:174
  799.3 19.6 multiply_convert_fusion.2
  821.8 4.7 multiply_reduce_fusion.2
  827.2 44.3 %psum.42 = f32[]{:T(128)} all-reduce(f32[]{:T(128)} %get-tuple-element.381), channel_id=1, replica_groups=mesh['dp'=8,'grp'=4] {'dp','grp'}, use_global_device_ids=true, to_apply=%region_29.31 | all-reduce | flops 1 | bytes 8 | tf_op jit(solution)/shard_map/psum | solution.py:367
  871.5 5.2 convert_reduce_fusion.2
  881.3 7.3 convert_reduce_fusion.1
  895.7 296.1 %while.61 = (s32[]{:T(128)}, bf16[16,864,32]{1,2,0:T(8,128)(2,1)}, f32[16,1248,32]{1,2,0:T(8,128)}, f32[16,1248,32]{1,2,0:T(8,128)}, s32[16]{0:T(128)S(1)}, /*in...) while((s32[]{:T(128)}, bf16[16,864,32]{1,2,0:T(8,128)(2,1)}, ...), condition=%wide.region_36.38_spmd.clone, body=%wide.region_34.37_spmd.clone.sunk | while | flops 355896480 | bytes 48104760 | solution.py:196
  1206.9 5.1 fusion.78
  1212.0 4.7 convolution_bitcast_fusion.5
  1216.7 6.0 scatter-add.26
  1226.7 6.1 scatter-add.27
  1242.3 15.2 all-to-all-start.2
  1257.6 6.6 fusion.143
  1267.1 4.7 convert_reduce_fusion.5
  1271.9 4.7 multiply_reduce_fusion.15
  1279.9 146.0 %while.62 = (s32[]{:T(128)}, bf16[12,96,64]{1,2,0:T(8,128)(2,1)}, f32[12,384,64]{1,2,0:T(8,128)}, f32[12,384,64]{1,2,0:T(8,128)}, s32[12]{0:T(128)}, /*index=5*/...) while((s32[]{:T(128)}, bf16[12,96,64]{1,2,0:T(8,128)(2,1)}, ...), condition=%wide.region_45.47_spmd.clone, body=%wide.region_43.46_spmd.clone.sunk | while | flops 23992232 | bytes 1736201 | solution.py:196
  1428.8 6.6 convolution_bitcast_fusion.4
  1435.5 5.7 reshape.790
  1441.2 5.3 copy.46
  1471.6 5.9 copy.43
  1477.5 5.1 fusion.171
  1482.6 11.1 reshape.775
  1500.3 137.2 %concatenate.46 = f32[4432576]{0:T(1024)} concatenate(f32[393216]{0:T(1024)} %bitcast.279, f32[786432]{0:T(1024)} %reshape.786, f32[262144]{0:T(1024)} %bitcast.281, f32[1048576]{0:T(1024)} %bitcast.273, f32[1048576]{0:T(1024)} %bitcast.274, f32[884736]{0:T(1024)S(1)} %copy-done.12, f32[512]{0:T(512)} %convert_reduce_fusion.9, f32[512]{0:T(512)} %get-tuple-element.486, ...), dimensions={0} | concatenate | bytes 35460608 | tf_op jit(solution)/shard_map/concatenate | solution.py:109
  1637.5 14.5 pad_bitcast_fusion.1
  1660.1 8.0 reshape.772
  1671.7 6.6 reshape.771
  1682.9 6.0 constant_dynamic-update-slice_fusion.9
  1693.1 5.0 constant_dynamic-update-slice_fusion.7
  1711.0 26.1 pad_bitcast_fusion
  1737.2 213.8 %reduce-scatter.11.cloned.1.call-done = f32[4352,128]{1,0:T(8,128)} async-done(((f32[34816,128]{1,0:T(8,128)}), f32[4352,128]{1,0:T(8,128)}) %reduce-scatter.11.cloned.1.call-update) | async-done | bytes 2228240 | tf_op jit(solution)/shard_map/reduce_scatter | solution.py:436
  1951.0 552.8 %reduce-scatter.9.cloned.1.call-done = f32[8256,128]{1,0:T(8,128)} async-done(((f32[66048,128]{1,0:T(8,128)}), f32[8256,128]{1,0:T(8,128)}) %reduce-scatter.9.cloned.1.call-update) | async-done | bytes 4227088 | tf_op jit(solution)/shard_map/reduce_scatter | solution.py:436
  2504.5 7.5 psum.46
  2512.0 115.7 %all-reduce.9.cloned.1.call-done = (f32[8256,128]{1,0:T(8,128)}, f32[4352,128]{1,0:T(8,128)}) async-done(((f32[8256,128]{1,0:T(8,128)}, f32[4352,128]{1,0:T(8,128)}), (f32[8256,128]{1,0:T(8,128)}, f32[4352,128]{1,0:T(8,128)})) %all-reduce.9.cloned.1.call-update) | async-done | bytes 6455312 | tf_op jit(solution)/shard_map/psum | solution.py:435
  2633.7 22.0 all-reduce.5
  2656.5 13.6 multiply_add_fusion.1
  (1049 shorter events, 813.8 us)
Async XLA Ops:
  7.2 138.0 %all-gather.5.cloned.1.call-start = ((), (), s32[]{:S(2)}) async-start(), calls=%async_computation.8 | async-start | bytes 10027008 | tf_op jit(solution)/shard_map/all_gather | solution.py:307
  10.0 461.1 %all-gather.3.cloned.1.call-start = ((), (), s32[]{:S(2)}) async-start(), calls=%async_computation.7 | async-start | bytes 19021824 | tf_op jit(solution)/shard_map/all_gather | solution.py:306
  10.1 19.8 copy-start
  29.8 14.0 copy-start.124
  32.0 11.8 copy-start.122
  34.1 20.6 all-to-all-start
  46.2 8.5 copy-start.121
  483.7 116.4 %copy-start.15 = (f32[96,768]{1,0:T(8,128)}, f32[96,768]{1,0:T(8,128)S(1)}, u32[]{:S(2)}) copy-start(f32[96,768]{1,0:T(8,128)S(1)} %get-tuple-element.568) | copy-start | bytes 884740
  483.7 12.6 copy-start.96
  483.9 12.4 copy-start.112
  499.1 17.9 copy-start.61
  601.9 27.4 %copy-start.98 = (f32[96]{0:T(128)}, f32[96]{0:T(128)S(1)}, u32[]{:S(2)}) copy-start(f32[96]{0:T(128)S(1)} %broadcast_multiply_fusion.5) | copy-start | bytes 1156
  602.8 8.3 copy-start.133
  602.8 26.5 copy-start.114
  619.3 10.0 copy-start.18
  619.3 10.0 copy-start.67
  619.3 10.0 copy-start.71
  636.6 12.5 copy-start.138
  637.7 14.8 copy-start.108
  637.7 14.7 copy-start.119
  640.4 8.7 all-to-all-start.1
  643.9 11.6 copy-start.110
  643.9 11.6 copy-start.126
  657.3 5.6 collective-permute-start
  658.8 4.1 collective-permute-start.1
  665.8 130.2 %copy-start.118 = (f32[512]{0:T(512)S(1)}, f32[512]{0:T(512)}, u32[]{:S(2)}) copy-start(f32[512]{0:T(512)} %get-tuple-element.533) | copy-start | bytes 6148
  798.9 20.1 copy-start.4
  799.3 19.7 copy-start.43
  799.3 19.6 copy-start.130
  871.5 9.1 slice-start.8
  1194.5 3.5 collective-permute-start.2
  1205.4 17.3 collective-permute-start.3
  1242.3 21.9 all-to-all-start.2
  1257.5 394.6 %reduce-scatter.13.cloned.1.call-start = ((), (), s32[]{:S(2)}) async-start(), calls=%async_computation.11 | async-start | bytes 1474560
  1265.1 196.0 %copy-start.51 = (bf16[96,512]{1,0:T(8,128)(2,1)}, bf16[96,512]{1,0:T(8,128)(2,1)S(1)}, u32[]{:S(2)}) copy-start(bf16[96,512]{1,0:T(8,128)(2,1)S(1)} %gather_fusion.5) | copy-start | bytes 294916
  1277.5 187.1 %copy-start.30 = (f32[96,768]{1,0:T(8,128)}, f32[96,768]{1,0:T(8,128)S(1)}, u32[]{:S(2)}) copy-start(f32[96,768]{1,0:T(8,128)S(1)} %get-tuple-element.493) | copy-start | bytes 884740
  1428.6 224.8 %reduce-scatter.15.cloned.1.call-start = ((), (), s32[]{:S(2)}) async-start(), calls=%async_computation.12 | async-start | bytes 1474560
  1482.6 17.7 copy-start.12
  1482.6 17.7 copy-start.85
  1500.3 450.7 %reduce-scatter.11.cloned.1.call-start = ((), (), s32[]{:S(2)}) async-start(), calls=%async_computation.10 | async-start | bytes 20054016 | tf_op jit(solution)/shard_map/reduce_scatter | solution.py:436
  1652.1 851.7 %reduce-scatter.9.cloned.1.call-start = ((), (), s32[]{:S(2)}) async-start(), calls=%async_computation.9 | async-start | bytes 38043648 | tf_op jit(solution)/shard_map/reduce_scatter | solution.py:436
  1660.1 8.3 copy-start.31
  1660.1 8.4 copy-start.29
  1682.9 8.7 slice-start.3
  1682.9 10.2 slice-start.4
  1688.9 9.2 slice-start.5
  1737.1 890.6 %all-reduce.9.cloned.1.call-start = ((), (), s32[]{:S(2)}) async-start(), calls=%async_computation.13 | async-start | bytes 12910592 | tf_op jit(solution)/shard_map/psum | solution.py:435
  2656.5 16.8 copy-start.40
  (161 other events, 627.0 us)
Sparse Core Ops, SparseCore 0:
  10.8 134.3 all-gather.4
  147.3 323.7 all-gather.2
  1428.7 26.3 reduce-scatter.12
  1500.4 26.3 reduce-scatter.14
  1652.2 298.7 reduce-scatter.10
  1955.2 548.5 reduce-scatter.8
  2506.3 121.3 all-reduce.8
where the time goes:
time: 2710 us; the launch traced here: 2690 us
  waiting for transfers between devices  1260 us (46%)
  matrix products  541 us (20%)
  local copies, waits for them, and re-layouts  522 us (19%)
  other arithmetic  113 us (4%)
  blocking collectives  104 us (4%)
  loops' own time  93.1 us (3%)
  starting transfers between devices  30 us (1%)
    reduce_scatter x2, waiting for transfers between devices, per_device(): lax.psum_scatter((enc_sum, dec_sum), 'dp', scatter_dimension=0, tiled=True)  767 us
    all_gather x1, waiting for transfers between devices, per_device(): lax.all_gather(enc_params.astype(jnp.bfloat16), 'dp', axis=0, tiled=True)  288 us
    dot_general x94, matrix products, mul_trans(): lax.dot_general(left, right, (((1,), (1,)), ((), ())), preferred_element_...  240 us
    dot_general x67, matrix products, matmul(): return jnp.dot(left, right, preferred_element_type=jnp.float32)  153 us
    dot_general x67, matrix products, trans_mul(): lax.dot_general(left, right, (((0,), (0,)), ((), ())), preferred_element_...  148 us
    concatenate x2, local copies, waits for them, and re-layouts, pack(): jnp.concatenate([table[piece_name].reshape(-1) for piece_name, piece_dims...  138 us
    psum x1, waiting for transfers between devices, per_device(): lax.psum((enc_flat, dec_flat, loss_part), 'grp')  116 us
    all_gather x1, waiting for transfers between devices, per_device(): lax.all_gather(dec_params.astype(jnp.bfloat16), 'dp', axis=0, tiled=True)  87.4 us
  transfers between devices with their start and end apart: 14, of which 7 were waited for; matrix products, arithmetic and copies ran while one was open for 15% of the time, Pallas kernels for 0%

commit v1 on v0

v1 whole, which is shorter than its diff:
```python
import functools
import math

import jax
import jax.numpy as jnp
from jax import lax
from jax.experimental import pallas as pl
from jax.experimental.pallas import tpu as pltpu
from jax.sharding import PartitionSpec as P

D = 768
H = 12
F = 3072
E = 512
EH = 16
FE = 2048
PATCH = 1728
L = 1728
TILE_HI = 192
ER = 66048
DR = 34816


NORM_EPS = 1e-06
MASK_FILL = -1e30
CLIP_LIMIT = 0.0002
LEARN_RATE = 0.02
BETA_ONE = 0.5
BETA_TWO = 0.5
ADAM_EPS = 1e-08
WEIGHT_DECAY = 0.05
EMA_RATE = 0.9


def swap(block, axis, bit):
    count = lax.axis_size(axis)
    return lax.ppermute(block, axis, [(i, i ^ bit) for i in range(count)])


def bit_of(axis, bit):
    return (lax.axis_index(axis) // bit) % 2


def double(block, dim, axis, bit):
    mine = bit_of(axis, bit)
    other = swap(block, axis, bit)
    first = jnp.where(mine == 0, block, other)
    second = jnp.where(mine == 0, other, block)
    return jnp.stack([first, second], axis=dim)


def total(values):
    for axis in ("grp", "dp"):
        bit = 1
        while bit < lax.axis_size(axis):
            values = values + swap(values, axis, bit)
            bit *= 2
    return values


def dp_bits():
    bits = [1]
    while bits[-1] * 2 < lax.axis_size("dp"):
        bits.append(bits[-1] * 2)
    return bits


def routes():
    bits = [("dp", bit) for bit in dp_bits()]
    side = [("grp", 2)]
    return [side + bits, bits + side, bits[1:] + side + bits[:1]]


def cut(rows, shares):
    unit = 16 if rows % 16 == 0 else 2
    units = rows // unit
    first = int(round(units * shares[0]))
    second = int(round(units * shares[1]))
    return [first * unit, second * unit, (units - first - second) * unit]


GATHER_SHARES = (0.36, 0.34)
REDUCE_SHARES = (0.333, 0.333)


def gather_chunk(block, route):
    blocks = [block]
    for order, stage in enumerate(reversed(route)):
        blocks = blocks + [swap(part, *stage) for part in blocks]
        if order < 2:
            blocks = [jnp.concatenate(blocks, axis=0)]
    return blocks


def place_kernel(route, rows, offset, part, *refs):
    sources, out_ref, sems = refs[:-2], refs[-2], refs[-1]
    stages = list(reversed(route))
    count = 2 ** len(stages)
    place = lax.axis_index("dp")
    lane = lax.axis_index("grp")
    arrays = count // 4
    for side in range(2):
        for index in range(count):
            shard, member = place, lane ^ side
            for order, (axis, bit) in enumerate(stages):
                differs = ((index >> order) & 1) * bit
                if axis == "dp":
                    shard = shard ^ differs
                else:
                    member = member ^ differs
            target = pl.multiple_of((shard * 4 + member) * part + offset, 16)
            pltpu.make_async_copy(
                sources[side * arrays + index // 4].at[pl.ds(index % 4 * rows, rows)],
                out_ref.at[pl.ds(target, rows)],
                sems.at[side * arrays + index // 4],
            ).start()
    for index in range(2 * arrays):
        pltpu.make_async_copy(
            sources[index], out_ref.at[pl.ds(0, 4 * rows)], sems.at[index]
        ).wait()


def gather_place(chunks, shard_rows):
    part = shard_rows // 4
    total_rows = shard_rows * lax.axis_size("dp")
    result = None
    offset = 0
    for route, rows, blocks in zip(routes(), cut(part, GATHER_SHARES), chunks):
        operands = blocks + [swap(block, "grp", 1) for block in blocks]
        count = len(operands)
        specs = [pl.BlockSpec(memory_space=pltpu.VMEM)] * count
        kernel = functools.partial(place_kernel, route, rows, offset, part)
        if result is not None:
            operands = operands + [result]
            specs = specs + [pl.BlockSpec(memory_space=pl.ANY)]
            kernel = functools.partial(skip_last_input, kernel, count)
        result = pl.pallas_call(
            kernel,
            in_specs=specs,
            out_specs=pl.BlockSpec(memory_space=pl.ANY),
            out_shape=jax.ShapeDtypeStruct((total_rows, 128), blocks[0].dtype),
            scratch_shapes=[pltpu.SemaphoreType.DMA((count,))],
            input_output_aliases={count: 0} if len(operands) > count else {},
        )(*operands)
        offset += rows
    return result


def skip_last_input(kernel, count, *refs):
    kernel(*refs[:count], *refs[count + 1 :])


def gather_both(enc_shard, dec_shard):
    if enc_shard.shape[0] % 64 or dec_shard.shape[0] % 64:
        return tuple(
            lax.all_gather(shard, "dp", axis=0, tiled=True) for shard in (enc_shard, dec_shard)
        )
    quarters = []
    for shard in (enc_shard, dec_shard):
        part = shard.shape[0] // 4
        quarters.append(
            lax.dynamic_slice_in_dim(shard, lax.axis_index("grp") * part, part, 0)
        )
    chunks = ([], [])
    start = [0, 0]
    for index, route in enumerate(routes()):
        blocks = None
        for which, quarter in enumerate(quarters):
            rows = cut(quarter.shape[0], GATHER_SHARES)[index]
            block = lax.slice_in_dim(quarter, start[which], start[which] + rows, axis=0)
            start[which] += rows
            if which:
                blocks, block = lax.optimization_barrier((blocks, block))
                chunks[0].append(blocks)
            blocks = gather_chunk(block, route)
        chunks[1].append(blocks)
    return gather_place(chunks[0], enc_shard.shape[0]), gather_place(chunks[1], dec_shard.shape[0])


def section(cells, dim, start, size):
    return lax.dynamic_slice_in_dim(cells, start, size, dim)


def reduce_bit(cells, dim, axis, bit, start=0, size=None):
    half = (cells.shape[dim] if size is None else size) // 2
    mine = bit_of(axis, bit)
    sent = section(cells, dim, start + (1 - mine) * half, half)
    return section(cells, dim, start + mine * half, half) + swap(sent, axis, bit)


def reduce_routes():
    low, rest = dp_bits()[:1], dp_bits()[1:]
    side, low = [("grp", 2)], [("dp", bit) for bit in low]
    rest = [("dp", bit) for bit in rest]
    return [side + low + rest, low + rest[:1] + side + rest[1:], rest[:1] + side + rest[1:] + low]


def reduce_stages(half):
    shards = lax.axis_size("dp")
    half_rows = half.shape[0] // shards
    bits = dp_bits()
    names = [("dp", bit) for bit in reversed(bits)]
    cells = half.reshape([2] * len(bits) + [half_rows, 128])
    blocks = []
    start = 0
    for route, rows in zip(reduce_routes(), cut(half_rows, REDUCE_SHARES)):
        axis, bit = route[0]
        if axis == "grp":
            block = reduce_bit(cells, len(bits), axis, bit, start, rows)
        else:
            dim = names.index(route[0])
            mine = bit_of(axis, bit)

            def pick(index, dim=dim, start=start, rows=rows):
                corner = [0] * dim + [index] + [0] * (len(bits) - dim - 1) + [start, 0]
                sizes = [2] * dim + [1] + [2] * (len(bits) - dim - 1) + [rows, 128]
                return lax.dynamic_slice(cells, corner, sizes)

            block = pick(mine) + swap(pick(1 - mine), axis, bit)
        blocks.append(block)
        start += rows
    for step in range(1, len(bits) + 1):
        for index, route in enumerate(reduce_routes()):
            axis, bit = route[step]
            dim = len(bits) if axis == "grp" else names.index(route[step])
            blocks[index] = reduce_bit(blocks[index], dim, axis, bit)
    return [block.reshape(-1, 128) for block in blocks]


def spread_pieces(pieces):
    wide = [double(piece, 0, "grp", 2).reshape(-1, 128) for piece in pieces]
    mine = jnp.concatenate(wide, axis=0)
    return mine, swap(mine, "grp", 1)


def group_rows(block):
    across = swap(block, "grp", 2)
    near, far = (
        swap(block, "grp", 1),
        swap(across, "grp", 1),
    )
    return jnp.concatenate([block, near, across, far], axis=0)


def own_rows(blocks):
    count = blocks.shape[0] // 4
    parts = [lax.slice_in_dim(blocks, i * count, (i + 1) * count, axis=0) for i in range(4)]
    sent = jnp.concatenate([parts[1], parts[3]], axis=0)
    arrived = swap(sent, "grp", 1)
    kept = parts[0] + arrived[:count]
    other = parts[2] + arrived[count:]
    return kept + swap(other, "grp", 2)


def extended(cells, width):
    count = lax.axis_size("grp")
    ends = count - 1
    head = cells[:width]
    tail = cells[cells.shape[0] - width :]
    return jnp.concatenate(
        [
            lax.ppermute(tail, "grp", [(i, i + 1) for i in range(ends)]),
            cells,
            lax.ppermute(head, "grp", [(i + 1, i) for i in range(ends)]),
        ],
        axis=0,
    )


def passed_along(block, axis, distance):
    devices = range(lax.axis_size(axis))
    route = [(i - distance, i) for i in devices if i - distance in devices]
    return lax.ppermute(block, axis, route)


def enc_pieces():
    return [
        ("patch_w", (PATCH, D)),
        ("qkv_w", (D, 3 * D)),
        ("out_w", (D, D)),
        ("up_w", (D, F)),
        ("down_w", (F, D)),
        ("patch_b", (D,)),
        ("out_b", (D,)),
        ("up_b", (F,)),
        ("down_b", (D,)),
        ("norm_g", (3, D)),
        ("norm_b", (3, D)),
    ]


def dec_pieces():
    return [
        ("embed_w", (D, E)),
        ("qkv_w", (E, 3 * E)),
        ("out_w", (E, E)),
        ("up_w", (E, FE)),
        ("down_w", (FE, E)),
        ("pix_w", (E, PATCH)),
        ("embed_b", (E,)),
        ("mask_token", (E,)),
        ("out_b", (E,)),
        ("up_b", (FE,)),
        ("down_b", (E,)),
        ("pix_b", (PATCH,)),
        ("norm_g", (3, E)),
        ("norm_b", (3, E)),
    ]


def unpack(rows, pieces):
    table = {}
    offset = 0
    vectors = sum(1 for _, dims in pieces if len(dims) == 2 and dims[0] > 3)
    for piece_name, piece_dims in pieces[:vectors]:
        amount = math.prod(piece_dims) // 128
        table[piece_name] = rows[offset : offset + amount].reshape(piece_dims)
        offset += amount
    small = rows[offset:].reshape(-1)
    offset = 0
    for piece_name, piece_dims in pieces[vectors:]:
        amount = math.prod(piece_dims)
        table[piece_name] = small[offset : offset + amount].reshape(piece_dims)
        offset += amount
    return table


def matmul(left, right):
    return jnp.dot(left, right, preferred_element_type=jnp.float32)


def mul_trans(left, right):
    return lax.dot_general(
        left, right, (((1,), (1,)), ((), ())), preferred_element_type=jnp.float32
    )


def trans_mul(left, right):
    return lax.dot_general(
        left, right, (((0,), (0,)), ((), ())), preferred_element_type=jnp.float32
    )


def sincos(positions, width):
    half_width = width // 2
    freq_row = jnp.exp(
        jnp.arange(half_width, dtype=jnp.float32) * (-2.0 * math.log(10000.0) / width)
    )
    angles = positions.astype(jnp.float32)[:, None] * freq_row[None, :]
    return jnp.concatenate([jnp.sin(angles), jnp.cos(angles)], axis=1)


def layer_norm(inputs, gain, shift):
    center = inputs - jnp.mean(inputs, axis=-1, keepdims=True)
    return (
        center * lax.rsqrt(jnp.mean(center * center, axis=-1, keepdims=True) + NORM_EPS) * gain
        + shift
    )


def norm_back(inputs, gain, shift, grad_out):
    outputs, pull = jax.vjp(layer_norm, inputs, gain, shift)
    return pull(grad_out)


def exact_gelu(values):
    return jax.nn.gelu(values, approximate=False)


BLOCK = 128


def head_masks(width):
    lanes = lax.broadcasted_iota(jnp.int32, (1, 128), 1) // width
    return [(lanes == index).astype(jnp.float32) for index in range(128 // width)]


def spread_heads(cells, masks):
    wide = cells.astype(jnp.float32)
    return jnp.concatenate([(wide * mask).astype(jnp.bfloat16) for mask in masks], axis=0)


def attend_kernel(window, width, q_ref, k_ref, v_ref, qid_ref, kid_ref, o_ref):
    start = pl.multiple_of(pl.program_id(0) * BLOCK, BLOCK)
    scale = width ** (-0.5)
    masks = head_masks(width)
    bias = jnp.where(qid_ref[...] == kid_ref[:, pl.ds(start, window)], 0.0, MASK_FILL)
    for group in range(q_ref.shape[1] // 128):
        lanes = slice(group * 128, (group + 1) * 128)
        keys = k_ref[pl.ds(start, window), lanes]
        values = v_ref[pl.ds(start, window), lanes]
        stacked = spread_heads(q_ref[:, lanes], masks)
        scores = mul_trans(stacked, keys) * scale
        outcome = jnp.zeros((BLOCK, 128), jnp.float32)
        for index, mask in enumerate(masks):
            part = scores[index * BLOCK : (index + 1) * BLOCK] + bias
            powers = jnp.exp(part - jnp.max(part, axis=1, keepdims=True))
            probs = powers * (1.0 / jnp.sum(powers, axis=1, keepdims=True))
            outcome += matmul(probs.astype(jnp.bfloat16), values) * mask
        o_ref[:, lanes] = outcome.astype(jnp.bfloat16)


def attend_back_kernel(
    window, width, q_ref, g_ref, k_ref, v_ref, qid_ref, kid_ref, dq_ref, dk_ref, dv_ref
):
    step = pl.program_id(0)
    start = pl.multiple_of(step * BLOCK, BLOCK)
    scale = width ** (-0.5)
    masks = head_masks(width)

    @pl.when(step == 0)
    def _():
        dk_ref[...] = jnp.zeros_like(dk_ref)
        dv_ref[...] = jnp.zeros_like(dv_ref)

    near = pl.ds(start, window)
    bias = jnp.where(kid_ref[near, :] == qid_ref[...], 0.0, MASK_FILL)
    bias = jnp.concatenate([bias, bias], axis=1)
    for group in range(q_ref.shape[1] // 128):
        lanes = slice(group * 128, (group + 1) * 128)
        keys = k_ref[near, lanes]
        values = v_ref[near, lanes]
        query = q_ref[:, lanes]
        grads = g_ref[:, lanes]
        dq = jnp.zeros((BLOCK, 128), jnp.float32)
        dk = jnp.zeros((window, 128), jnp.float32)
        dv = jnp.zeros((window, 128), jnp.float32)
        for pair in range(0, len(masks), 2):
            both = masks[pair : pair + 2]
            queries = spread_heads(query, both)
            outs = spread_heads(grads, both)
            scores = mul_trans(keys, queries) * scale + bias
            powers = jnp.exp(scores - jnp.max(scores, axis=0, keepdims=True))
            probs = powers * (1.0 / jnp.sum(powers, axis=0, keepdims=True))
            prob_grad = mul_trans(values, outs)
            shared = jnp.sum(probs * prob_grad, axis=0, keepdims=True)
            score_grad = (probs * (prob_grad - shared)).astype(jnp.bfloat16)
            dv += matmul(probs.astype(jnp.bfloat16), outs)
            dk += matmul(score_grad, queries)
            part = trans_mul(score_grad, keys)
            dq += part[:BLOCK] * both[0] + part[BLOCK:] * both[1]
        dq_ref[:, lanes] = dq * scale
        dk_ref[near, lanes] += dk * scale
        dv_ref[near, lanes] += dv


def padded(cells, rows, fill=0):
    return jnp.pad(
        cells, [(0, rows - cells.shape[0])] + [(0, 0)] * (cells.ndim - 1), constant_values=fill
    )


def attend_sizes(query, keys, rim):
    steps = -(-query.shape[0] // BLOCK)
    window = BLOCK + 2 * rim if rim else keys.shape[0]
    return steps, window, (steps - 1) * BLOCK + window


def whole_spec(dims):
    return pl.BlockSpec(dims, lambda i: (0, 0))


def step_spec(columns):
    return pl.BlockSpec((BLOCK, columns), lambda i: (i, 0))


def attend(query, keys, values, query_ids, key_ids, heads, rim):
    count, columns = query.shape
    steps, window, span = attend_sizes(query, keys, rim)
    outcome = pl.pallas_call(
        functools.partial(attend_kernel, window, columns // heads),
        grid=(steps,),
        in_specs=[
            step_spec(columns),
            whole_spec((span, columns)),
            whole_spec((span, columns)),
            step_spec(1),
            whole_spec((1, span)),
        ],
        out_specs=step_spec(columns),
        out_shape=jax.ShapeDtypeStruct((steps * BLOCK, columns), jnp.bfloat16),
        compiler_params=pltpu.CompilerParams(vmem_limit_bytes=48 << 20),
        cost_estimate=pl.CostEstimate(
            flops=4 * steps * BLOCK * window * columns,
            bytes_accessed=8 * span * columns,
            transcendentals=steps * BLOCK * window * heads,
        ),
    )(
        padded(query, steps * BLOCK),
        padded(keys, span),
        padded(values, span),
        padded(query_ids, steps * BLOCK, -4)[:, None],
        padded(key_ids, span, -5)[None, :],
    )
    return outcome[:count]


def attend_back(query, keys, values, query_ids, key_ids, heads, rim, out_grad):
    count, columns = query.shape
    steps, window, span = attend_sizes(query, keys, rim)
    dq, dk, dv = pl.pallas_call(
        functools.partial(attend_back_kernel, window, columns // heads),
        grid=(steps,),
        in_specs=[
            step_spec(columns),
            step_spec(columns),
            whole_spec((span, columns)),
            whole_spec((span, columns)),
            pl.BlockSpec((1, BLOCK), lambda i: (0, i)),
            whole_spec((span, 1)),
        ],
        out_specs=[step_spec(columns), whole_spec((span, columns)), whole_spec((span, columns))],
        out_shape=[
            jax.ShapeDtypeStruct((steps * BLOCK, columns), jnp.float32),
            jax.ShapeDtypeStruct((span, columns), jnp.float32),
            jax.ShapeDtypeStruct((span, columns), jnp.float32),
        ],
        compiler_params=pltpu.CompilerParams(vmem_limit_bytes=48 << 20),
        cost_estimate=pl.CostEstimate(
            flops=10 * steps * BLOCK * window * columns,
            bytes_accessed=20 * span * columns,
            transcendentals=steps * BLOCK * window * heads,
        ),
    )(
        padded(query, steps * BLOCK),
        padded(out_grad, steps * BLOCK),
        padded(keys, span),
        padded(values, span),
        padded(query_ids, steps * BLOCK, -4)[None, :],
        padded(key_ids, span, -5)[:, None],
    )
    return dq[:count], dk[: keys.shape[0]], dv[: keys.shape[0]]


def block_forward(inputs, table, heads, rim, query_ids, key_ids, share_keys):
    gains = table["norm_g"].astype(jnp.float32)
    shifts = table["norm_b"].astype(jnp.float32)
    width = inputs.shape[1]
    normed_one = layer_norm(inputs, gains[0], shifts[0]).astype(jnp.bfloat16)
    qkv = matmul(normed_one, table["qkv_w"]).astype(jnp.bfloat16)
    query = qkv[:, :width]
    all_keys, all_values = share_keys((qkv[:, width : 2 * width], qkv[:, 2 * width :]))
    attended = attend(query, all_keys, all_values, query_ids, key_ids, heads, rim)
    mixed = inputs + (matmul(attended, table["out_w"]) + table["out_b"].astype(jnp.float32))
    normed_two = layer_norm(mixed, gains[1], shifts[1]).astype(jnp.bfloat16)
    hidden = matmul(normed_two, table["up_w"]) + table["up_b"].astype(jnp.float32)
    activated = exact_gelu(hidden).astype(jnp.bfloat16)
    result = mixed + (matmul(activated, table["down_w"]) + table["down_b"].astype(jnp.float32))
    saved = (
        inputs,
        normed_one,
        query,
        all_keys,
        all_values,
        attended,
        mixed,
        normed_two,
        hidden,
        activated,
    )
    return (result, saved)


def block_backward(grad_out, table, heads, rim, query_ids, key_ids, saved, return_keys):
    (
        inputs,
        normed_one,
        query,
        all_keys,
        all_values,
        attended,
        mixed,
        normed_two,
        hidden,
        activated,
    ) = saved
    gains = table["norm_g"].astype(jnp.float32)
    shifts = table["norm_b"].astype(jnp.float32)
    grads = {}
    pairs = {}
    down_grad = grad_out.astype(jnp.bfloat16)
    pairs["down_w"] = (activated, down_grad)
    grads["down_b"] = jnp.sum(down_grad.astype(jnp.float32), axis=0)
    act_grad = mul_trans(down_grad, table["down_w"])
    gelu_out, gelu_pull = jax.vjp(exact_gelu, hidden)
    hidden_grad = gelu_pull(act_grad)[0].astype(jnp.bfloat16)
    pairs["up_w"] = (normed_two, hidden_grad)
    grads["up_b"] = jnp.sum(hidden_grad.astype(jnp.float32), axis=0)
    mixed_part, gain_two, shift_two = norm_back(
        mixed, gains[1], shifts[1], mul_trans(hidden_grad, table["up_w"])
    )
    mixed_grad = grad_out + mixed_part
    branch_grad = mixed_grad.astype(jnp.bfloat16)
    pairs["out_w"] = (attended, branch_grad)
    grads["out_b"] = jnp.sum(branch_grad.astype(jnp.float32), axis=0)
    attended_grad = mul_trans(branch_grad, table["out_w"]).astype(jnp.bfloat16)
    query_grad, keys_grad_all, values_grad_all = attend_back(
        query, all_keys, all_values, query_ids, key_ids, heads, rim, attended_grad
    )
    keys_grad, values_grad = return_keys((keys_grad_all, values_grad_all))
    qkv_grad = jnp.concatenate([query_grad, keys_grad, values_grad], axis=1).astype(jnp.bfloat16)
    pairs["qkv_w"] = (normed_one, qkv_grad)
    input_part, gain_one, shift_one = norm_back(
        inputs, gains[0], shifts[0], mul_trans(qkv_grad, table["qkv_w"])
    )
    return (mixed_grad + input_part, grads, (gain_one, shift_one, gain_two, shift_two), pairs)


def core_side():
    return (lax.axis_index("grp") % 2).astype(jnp.int32).reshape(1)


def small_rows(table, names, rows):
    joined = jnp.concatenate([table[name].reshape(-1) for name in names])
    return jnp.pad(joined, (0, rows * 128 - joined.size)).reshape(rows // 2, 256)


def pick_half(pairs, side):
    return jnp.where(side == 0, pairs[:, :128], pairs[:, 128:])


def store_flat(target, product):
    rows, blocks = product.shape[0], product.shape[1] // 128
    for index in range(blocks):
        target[pl.ds(index, rows, stride=blocks), :] = product[:, index * 128 : (index + 1) * 128]


def column_blocks(ref, blocks):
    parts = [ref[:, pl.ds(pl.multiple_of(index * 128, 128), 128)] for index in blocks]
    return parts[0] if len(parts) == 1 else jnp.concatenate(parts, axis=1)


def steps_of(rows, size):
    return [(start, min(size, rows - start)) for start in range(0, rows, size)]


def enc_grad_kernel(sizes, side_ref, *refs):
    small_ref, out_ref, stage_ref, sems = refs[-4:]
    side = side_ref[0]
    offset = 0
    flight = [None, None]
    turn = 0

    def send(source, rows):
        nonlocal turn, offset
        copy = pltpu.make_async_copy(source, out_ref.at[pl.ds(offset, rows)], sems.at[turn % 2])
        copy.start()
        flight[turn % 2] = copy
        turn += 1
        offset += rows

    def settle():
        if flight[turn % 2] is not None:
            flight[turn % 2].wait()

    for index, size in enumerate(sizes):
        x_ref, y_ref = refs[2 * index], refs[2 * index + 1]
        blocks = y_ref.shape[1] // 256
        right = column_blocks(y_ref, [2 * block + side for block in range(blocks)])
        for start, rows in steps_of(x_ref.shape[1], size):
            settle()
            target = stage_ref.at[turn % 2]
            store_flat(target, trans_mul(x_ref[:, start : start + rows], right))
            send(target.at[pl.ds(0, rows * blocks)], rows * blocks)
    settle()
    send(small_ref, small_ref.shape[0])
    settle()
    turn += 1
    settle()


def enc_grad_half(inputs, grads, small, total_rows):
    operands = [part for pair in zip(inputs, grads) for part in pair]
    sizes = [640, 256, 384, 256, 768]
    whole = pl.BlockSpec(memory_space=pltpu.VMEM)
    return pl.pallas_call(
        functools.partial(enc_grad_kernel, sizes),
        in_specs=[pl.BlockSpec(memory_space=pltpu.SMEM)] + [whole] * (len(operands) + 1),
        out_specs=pl.BlockSpec(memory_space=pl.ANY),
        out_shape=jax.ShapeDtypeStruct((total_rows // 2, 128), jnp.float32),
        scratch_shapes=[pltpu.VMEM((2, 3072, 128), jnp.float32), pltpu.SemaphoreType.DMA((2,))],
        compiler_params=pltpu.CompilerParams(vmem_limit_bytes=40 << 20),
        cost_estimate=pl.CostEstimate(
            flops=total_rows * 128 * inputs[0].shape[0],
            bytes_accessed=total_rows * 256,
            transcendentals=0,
        ),
    )(core_side(), *operands, small)


def store_pixels(product_ref, targets):
    groups = product_ref.shape[1] // 4

    def load(row, block):
        return product_ref.at[block][pl.ds(row, groups, stride=4), :]

    def piece(row, block):
        if block < 13:
            return load(row, block)
        if block == 13:
            left, right = load(row, 13)[:, :64], load(row + 1, 0)[:, :64]
        else:
            left, right = load(row + 1, block - 14)[:, 64:], load(row + 1, block - 13)[:, :64]
        return jnp.concatenate([left, right], axis=1)

    for index in range(54):
        block = piece(0, index) if index < 27 else piece(2, index - 27)
        targets[index % 2][pl.ds(index // 2, groups, stride=27), :] = block


def dec_grad_kernel(plan, side_ref, *refs):
    small_mine, small_theirs, mine_ref, theirs_ref, stage_ref, pixel_ref, sems = refs[-7:]
    side = side_ref[0]
    flight = [None, None]
    turn = 0
    for index, (size, offset) in enumerate(plan):
        x_ref, y_ref = refs[2 * index], refs[2 * index + 1]
        pixels = y_ref.shape[1] % 256 != 0
        for start, rows in steps_of(x_ref.shape[1], size):
            product = trans_mul(x_ref[:, start : start + rows], y_ref[...])
            slot = turn % 2
            for copy in flight[slot] or ():
                copy.wait()
            if pixels:
                for block in range(14):
                    part = product[:, block * 128 : (block + 1) * 128]
                    pixel_ref[block, :, : part.shape[1]] = part
                store_pixels(pixel_ref, [stage_ref.at[slot, 0], stage_ref.at[slot, 1]])
            else:
                blocks = y_ref.shape[1] // 128
                for block in range(blocks):
                    stage_ref.at[slot, block % 2][
                        pl.ds(block // 2, rows, stride=blocks // 2), :
                    ] = product[:, block * 128 : (block + 1) * 128]
            amount = rows * y_ref.shape[1] // 256
            flight[slot] = [
                pltpu.make_async_copy(
                    stage_ref.at[slot, parity, pl.ds(0, amount)],
                    target.at[pl.ds(offset, amount)],
                    sems.at[slot, order],
                )
                for order, (parity, target) in enumerate(
                    ((side, mine_ref), (1 - side, theirs_ref))
                )
            ]
            for copy in flight[slot]:
                copy.start()
            offset += amount
            turn += 1
    rows = small_mine.shape[0]
    last = [
        pltpu.make_async_copy(
            source, target.at[pl.ds(target.shape[0] - rows, rows)], sems.at[2, order]
        )
        for order, (source, target) in enumerate(
            ((small_mine, mine_ref), (small_theirs, theirs_ref))
        )
    ]
    for copy in last:
        copy.start()
    for copy in last + flight[0] + flight[1]:
        copy.wait()


def dec_grad_halves(pairs, small_mine, small_theirs, total_rows):
    plan = [(256, 0), (256, 1536), (256, 4608), (256, 5632), (512, 9728), (512, 13824)]
    operands = [part for pair in pairs for part in pair]
    whole = pl.BlockSpec(memory_space=pltpu.VMEM)
    anywhere = pl.BlockSpec(memory_space=pl.ANY)
    shape = jax.ShapeDtypeStruct((total_rows // 2, 128), jnp.float32)
    return pl.pallas_call(
        functools.partial(dec_grad_kernel, plan),
        in_specs=[pl.BlockSpec(memory_space=pltpu.SMEM)] + [whole] * (len(operands) + 2),
        out_specs=[anywhere, anywhere],
        out_shape=[shape, shape],
        scratch_shapes=[
            pltpu.VMEM((2, 2, 3456, 128), jnp.float32),
            pltpu.VMEM((14, 512, 128), jnp.float32),
            pltpu.SemaphoreType.DMA((3, 2)),
        ],
        compiler_params=pltpu.CompilerParams(vmem_limit_bytes=56 << 20),
        cost_estimate=pl.CostEstimate(
            flops=total_rows * 256 * pairs[1][0].shape[0],
            bytes_accessed=total_rows * 512,
            transcendentals=0,
        ),
    )(core_side(), *operands, small_mine, small_theirs)


def adamw_kernel(with_average, side_ref, scalar_ref, mine_ref, theirs_ref, *refs):
    count = 4 if with_average else 3
    ins, outs, grad_ref = refs[:count], refs[count:-1], refs[-1]
    side = side_ref[0]
    rows = mine_ref.shape[0]
    grad_ref[pl.ds(side, rows, stride=2), :] = mine_ref[...]
    grad_ref[pl.ds(1 - side, rows, stride=2), :] = theirs_ref[...]
    weights = ins[0][...]
    clipped = grad_ref[...] * scalar_ref[0]
    first_new = BETA_ONE * ins[1][...] + (1.0 - BETA_ONE) * clipped
    second_new = BETA_TWO * ins[2][...] + (1.0 - BETA_TWO) * clipped * clipped
    first_hat = first_new / scalar_ref[1]
    second_hat = second_new / scalar_ref[2]
    weights_new = weights * (1.0 - LEARN_RATE * WEIGHT_DECAY) - LEARN_RATE * first_hat / (
        jnp.sqrt(second_hat) + ADAM_EPS
    )
    outs[0][...] = weights_new
    outs[1][...] = first_new
    outs[2][...] = second_new
    outs[3][...] = weights_new.astype(jnp.bfloat16)
    if with_average:
        outs[4][...] = EMA_RATE * ins[3][...] + (1.0 - EMA_RATE) * weights_new


def adamw(halves, arrays, factor, steps_done):
    rows = arrays[0].shape[0]
    steps = 1
    for count in (2, 3, 4, 6, 8):
        if rows % (count * 32) == 0:
            steps = count
    block = pl.BlockSpec((rows // steps, 128), lambda i: (i, 0))
    half = pl.BlockSpec((rows // steps // 2, 128), lambda i: (i, 0))
    scalar = pl.BlockSpec(memory_space=pltpu.SMEM)
    scalars = jnp.stack([factor, 1.0 - BETA_ONE**steps_done, 1.0 - BETA_TWO**steps_done])
    full = jax.ShapeDtypeStruct((rows, 128), jnp.float32)
    shapes = [full, full, full, jax.ShapeDtypeStruct((rows, 128), jnp.bfloat16)]
    if len(arrays) == 4:
        shapes.append(full)
    return pl.pallas_call(
        functools.partial(adamw_kernel, len(arrays) == 4),
        grid=(steps,),
        in_specs=[scalar, scalar, half, half] + [block] * len(arrays),
        out_specs=[block] * len(shapes),
        out_shape=shapes,
        scratch_shapes=[pltpu.VMEM((rows // steps, 128), jnp.float32)],
        compiler_params=pltpu.CompilerParams(vmem_limit_bytes=40 << 20),
    )(core_side(), scalars, *halves, *arrays)


def paired(block):
    return jnp.concatenate([block, swap(block, "grp", 1)], axis=0)


def per_device(
    patches,
    segments,
    visible,
    enc_params,
    enc_first,
    enc_second,
    enc_average,
    dec_params,
    dec_first,
    dec_second,
    step_count,
):
    my_index = lax.axis_index("grp")
    slot_dev = segments.shape[0]
    rim = TILE_HI
    counts = jnp.sum((segments >= 0).astype(jnp.float32)) - visible.shape[0]
    total_count = total(jnp.full((8, 128), counts))[0, 0]
    enc_copy, dec_copy = gather_both(
        enc_params.astype(jnp.bfloat16), dec_params.astype(jnp.bfloat16)
    )
    enc_table = unpack(enc_copy, enc_pieces())
    dec_table = unpack(dec_copy, dec_pieces())
    group_vis = group_rows(visible)
    group_seg = double(double(segments, 0, "grp", 2), 1, "grp", 1).reshape(-1)
    group_ids = group_seg[group_vis]
    own_ids = group_ids[: visible.shape[0]]
    key_ids = extended(segments + 3, rim) - 3
    local_slot = group_vis - my_index * slot_dev
    chosen = (
        local_slot[:, None] == jnp.arange(slot_dev, dtype=jnp.int32)[None, :]
    ).astype(jnp.bfloat16)
    seen = jnp.sum(chosen.astype(jnp.float32), axis=0) > 0.5
    enc_input = own_rows(matmul(chosen, patches).astype(jnp.bfloat16))
    enc_start = (
        matmul(enc_input, enc_table["patch_w"])
        + enc_table["patch_b"].astype(jnp.float32)
        + sincos(visible % L, D)
    )

    def enc_share(pair):
        joined = group_rows(jnp.concatenate(pair, axis=1))
        return (joined[:, :D], joined[:, D:])

    def enc_return(pair):
        joined = own_rows(jnp.concatenate(pair, axis=1))
        return (joined[:, :D], joined[:, D:])

    enc_out, enc_saved = block_forward(enc_start, enc_table, H, 0, own_ids, group_ids, enc_share)
    enc_gain = enc_table["norm_g"].astype(jnp.float32)
    enc_shift = enc_table["norm_b"].astype(jnp.float32)
    enc_final = layer_norm(enc_out, enc_gain[2], enc_shift[2]).astype(jnp.bfloat16)
    latent = (
        matmul(enc_final, dec_table["embed_w"]) + dec_table["embed_b"].astype(jnp.float32)
    ).astype(jnp.bfloat16)
    placed = trans_mul(chosen, group_rows(latent))
    positions = (my_index * slot_dev + jnp.arange(slot_dev, dtype=jnp.int32)) % L
    dec_start = jnp.where(
        seen[:, None], placed, dec_table["mask_token"].astype(jnp.float32)[None, :]
    ) + sincos(positions, E)
    counted = jnp.where((segments >= 0) & jnp.logical_not(seen), 1.0, 0.0)

    def dec_share(pair):
        joined = extended(jnp.concatenate(pair, axis=1), rim)
        return (joined[:, :E], joined[:, E:])

    def dec_return(pair):
        joined = jnp.concatenate(pair, axis=1)
        from_upper = passed_along(joined[:rim], "grp", -1)
        from_lower = passed_along(joined[rim + slot_dev :], "grp", 1)
        middle = joined[rim : rim + slot_dev]
        middle = jnp.concatenate(
            [
                middle[:rim] + from_lower,
                middle[rim : slot_dev - rim],
                middle[slot_dev - rim :] + from_upper,
            ],
            axis=0,
        )
        return (middle[:, :E], middle[:, E:])

    dec_out, dec_saved = block_forward(
        dec_start, dec_table, EH, rim, segments, key_ids, dec_share
    )
    dec_gain = dec_table["norm_g"].astype(jnp.float32)
    dec_shift = dec_table["norm_b"].astype(jnp.float32)
    dec_final = layer_norm(dec_out, dec_gain[2], dec_shift[2]).astype(jnp.bfloat16)
    predicted = matmul(dec_final, dec_table["pix_w"]) + dec_table["pix_b"].astype(jnp.float32)
    pixels = patches.astype(jnp.float32)
    centered = pixels - jnp.mean(pixels, axis=1, keepdims=True)
    target = centered * lax.rsqrt(jnp.mean(centered * centered, axis=1, keepdims=True) + NORM_EPS)
    errors = predicted - target
    loss_part = jnp.sum(counted * jnp.mean(errors * errors, axis=1))
    pred_grad = (counted[:, None] * errors * (2.0 / PATCH) / total_count).astype(jnp.bfloat16)
    dec_grads = {}
    side = core_side()[0]
    dec_grads["pix_b"] = jnp.sum(pred_grad.astype(jnp.float32), axis=0)
    dec_out_grad, dec_gain_last, dec_shift_last = norm_back(
        dec_out, dec_gain[2], dec_shift[2], mul_trans(pred_grad, dec_table["pix_w"])
    )
    start_grad, block_grads, dec_small, dec_pairs = block_backward(
        dec_out_grad, dec_table, EH, rim, segments, key_ids, dec_saved, dec_return
    )
    dec_grads.update(block_grads)
    dec_grads["norm_g"] = jnp.stack([dec_small[0], dec_small[2], dec_gain_last])
    dec_grads["norm_b"] = jnp.stack([dec_small[1], dec_small[3], dec_shift_last])
    dec_grads["mask_token"] = jnp.sum(jnp.where(seen[:, None], 0.0, start_grad), axis=0)
    latent_grad = own_rows(matmul(chosen, start_grad.astype(jnp.bfloat16)).astype(jnp.bfloat16))
    dec_grads["embed_b"] = jnp.sum(latent_grad.astype(jnp.float32), axis=0)
    dec_pairs["embed_w"] = (enc_final, latent_grad)
    dec_pairs["pix_w"] = (dec_final, pred_grad)
    dec_vectors = small_rows(
        dec_grads,
        ("embed_b", "mask_token", "out_b", "up_b", "down_b", "pix_b", "norm_g", "norm_b"),
        256,
    )
    halves = dec_grad_halves(
        [dec_pairs[name] for name in ("embed_w", "qkv_w", "out_w", "up_w", "down_w", "pix_w")],
        pick_half(dec_vectors, side),
        pick_half(dec_vectors, 1 - side),
        DR,
    )
    dec_half = halves[0] + swap(halves[1], "grp", 1)
    latent_grad, dec_half = lax.optimization_barrier((latent_grad, dec_half))
    dec_sum = reduce_stages(dec_half)
    enc_out_grad, enc_gain_last, enc_shift_last = norm_back(
        enc_out, enc_gain[2], enc_shift[2], mul_trans(latent_grad, dec_table["embed_w"])
    )
    enc_start_grad, enc_grads, enc_small, enc_pairs = block_backward(
        enc_out_grad, enc_table, H, 0, own_ids, group_ids, enc_saved, enc_return
    )
    enc_grads["norm_g"] = jnp.stack([enc_small[0], enc_small[2], enc_gain_last])
    enc_grads["norm_b"] = jnp.stack([enc_small[1], enc_small[3], enc_shift_last])
    patch_grad = enc_start_grad.astype(jnp.bfloat16)
    enc_pairs["patch_w"] = (enc_input, patch_grad)
    enc_grads["patch_b"] = jnp.sum(patch_grad.astype(jnp.float32), axis=0)
    names = ("patch_w", "qkv_w", "out_w", "up_w", "down_w")
    enc_vectors = small_rows(
        enc_grads, ("patch_b", "out_b", "up_b", "down_b", "norm_g", "norm_b"), 384
    )
    enc_half = enc_grad_half(
        [paired(enc_pairs[name][0]) for name in names],
        [paired(enc_pairs[name][1]) for name in names],
        pick_half(enc_vectors, side) + swap(pick_half(enc_vectors, 1 - side), "grp", 1),
        ER,
    )
    enc_sum = reduce_stages(enc_half)
    squares = sum(jnp.sum(part * part) for part in enc_sum + dec_sum)
    lane = lax.broadcasted_iota(jnp.int32, (8, 128), 1)
    sums = total(jnp.where(lane == 0, squares, jnp.where(lane == 1, loss_part, 0.0)))
    loss_total = sums[0, 1]
    grad_norm = jnp.sqrt(sums[0, 0])
    factor = jnp.minimum(1.0, CLIP_LIMIT / (grad_norm + NORM_EPS))
    steps_done = step_count[0].astype(jnp.float32)
    enc_new, enc_first_new, enc_second_new, enc_copy_new, average_new = adamw(
        spread_pieces(enc_sum), (enc_params, enc_first, enc_second, enc_average), factor, steps_done
    )
    dec_new, dec_first_new, dec_second_new, dec_copy_new = adamw(
        spread_pieces(dec_sum), (dec_params, dec_first, dec_second), factor, steps_done
    )
    return (
        enc_new,
        enc_first_new,
        enc_second_new,
        enc_copy_new,
        dec_new,
        dec_first_new,
        dec_second_new,
        dec_copy_new,
        average_new,
        grad_norm,
        loss_total,
        total_count,
    )


def solution(mesh):
    placed = (
        P(("dp", "grp"), None),
        P(("dp", "grp")),
        P(("dp", "grp")),
        P("dp", None),
        P("dp", None),
        P("dp", None),
        P("dp", None),
        P("dp", None),
        P("dp", None),
        P("dp", None),
        P(),
    )
    return jax.shard_map(
        per_device,
        mesh=mesh,
        in_specs=placed,
        out_specs=(
            P("dp", None),
            P("dp", None),
            P("dp", None),
            P("dp", None),
            P("dp", None),
            P("dp", None),
            P("dp", None),
            P("dp", None),
            P("dp", None),
            P(),
            P(),
            P(),
        ),
        check_vma=False,
    )
```

time: 2710 us -> 965 us (0.36)
  waiting for transfers between devices: 1260 us -> 369 us
  matrix products: 541 us -> 71.4 us
  local copies, waits for them, and re-layouts: 522 us -> 144 us
  Pallas kernels: 0 us -> 146 us
  blocking collectives: 104 us -> 0 us
  starting transfers between devices: 30 us -> 126 us
  loops' own time: 93.1 us -> 0 us
    reduce_scatter x2 -> x0, waiting for transfers between devices: 767 us -> none  [per_device(): lax.psum_scatter((enc_sum, dec_sum), 'dp', scatter_dimension=0, tiled=True)]
    all_gather x2 -> x0, waiting for transfers between devices: 375 us -> none  [the longest x1 288 us: per_device(): lax.all_gather(enc_params.astype(jnp.bfloat16), 'dp', axis=0, tiled=True)]
    ppermute x2 -> x129, waiting for transfers between devices: 0.05 us -> 360 us  [the longest x125 358 us: swap(): return lax.ppermute(block, axis, [(i, i ^ bit) for i in range(count)])]
    dot_general x94 -> x10, matrix products: 240 us -> 29.4 us  [mul_trans(): lax.dot_general(left, right, (((1,), (1,)), ((), ())), preferred_element_...]
    dot_general x67 -> x1, matrix products: 148 us -> 0.73 us  [trans_mul(): lax.dot_general(left, right, (((0,), (0,)), ((), ())), preferred_element_...]
    pallas_call x0 -> x14, Pallas kernels: none -> 146 us  [the longest x2 43.6 us: attend_back(): pl.pallas_call(functools.partial(attend_back_kernel, window, columns // h...]
    concatenate x4 -> x10, local copies, waits for them, and re-layouts: 139 us -> 4.52 us  [the longest x3 4.18 us: gather_chunk(): blocks = [jnp.concatenate(blocks, axis=0)]]
    ppermute x2 -> x129, starting transfers between devices: 3.01 us -> 123 us  [the longest x125 117 us: swap(): return lax.ppermute(block, axis, [(i, i ^ bit) for i in range(count)])]
  transfers between devices with their start and end apart: 14 -> 131, of which waited for: 7 -> 55; matrix products, arithmetic and copies ran while one was open for 15% -> 21% of each run, Pallas kernels for 0% -> 5%
where the time goes in v1:
time: 965 us; the launch traced here: 955 us
  waiting for transfers between devices  369 us (38%)
  Pallas kernels  146 us (15%)
  local copies, waits for them, and re-layouts  144 us (15%)
  starting transfers between devices  126 us (13%)
  other arithmetic  88 us (9%)
  matrix products  71.4 us (7%)
  between operations  11.6 us (1%)
    ppermute x125, waiting for transfers between devices, swap(): return lax.ppermute(block, axis, [(i, i ^ bit) for i in range(count)])  358 us
    ppermute x125, starting transfers between devices, swap(): return lax.ppermute(block, axis, [(i, i ^ bit) for i in range(count)])  117 us
    reshape x11, local copies, waits for them, and re-layouts, unpack(): table[piece_name] = rows[offset:offset + amount].reshape(piece_dims)  46.8 us
    pallas_call x2, Pallas kernels, attend_back(): pl.pallas_call(functools.partial(attend_back_kernel, window, columns // h...  43.6 us
    dot_general x13, matrix products, matmul(): return jnp.dot(left, right, preferred_element_type=jnp.float32)  41.2 us
    unnamed x444, local copies, waits for them, and re-layouts  30.4 us
    dot_general x10, matrix products, mul_trans(): lax.dot_general(left, right, (((1,), (1,)), ((), ())), preferred_element_...  29.4 us
    slice x9, local copies, waits for them, and re-layouts, unpack(): table[piece_name] = rows[offset:offset + amount].reshape(piece_dims)  26.4 us
  transfers between devices with their start and end apart: 131, of which 55 were waited for; matrix products, arithmetic and copies ran while one was open for 21% of the time, Pallas kernels for 5%

profile of v1, /device:TPU:0, one launch (start us, length us, event | category | flops | bytes accessed | tf_op | source)
XLA Modules:
  0.0 955.5 jit_solution(5817423588207468115)
XLA Ops:
  18.9 4.5 multiply_sine_fusion
  41.9 12.8 %collective-permute-done.16 = bf16[1408,128]{1,0:T(8,128)(2,1)S(1)} collective-permute-done((bf16[1408,128]{1,0:T(8,128)(2,1)S(1)}, bf16[1408,128]{1,0:T(8,128)(2,1)S(1)}, u32[]{:S(2)}, u32[]{:S(2)}) %collective-permute-start.16) | collective-permute-done | bytes 360480 | tf_op jit(solution)/shard_map/ppermute | solution.py:37
  63.2 16.6 %collective-permute-done.8.refs_1_ = bf16[2496,128]{1,0:T(8,128)(2,1)} collective-permute-done((bf16[2496,128]{1,0:T(8,128)(2,1)S(1)}, bf16[2496,128]{1,0:T(8,128)(2,1)}, u32[]{:S(2)}, u32[]{:S(2)}) %collective-permute-start.8) | collective-permute-done | bytes 639008 | tf_op jit(solution)/shard_map/ppermute | solution.py:37
  82.4 4.8 collective-permute-done.17.refs_1_
  89.8 11.1 %collective-permute-done.9.refs_2_ = bf16[2496,128]{1,0:T(8,128)(2,1)S(1)} collective-permute-done((bf16[2496,128]{1,0:T(8,128)(2,1)S(1)}, bf16[2496,128]{1,0:T(8,128)(2,1)S(1)}, u32[]{:S(2)}, u32[]{:S(2)}) %collective-permute-start.9) | collective-permute-done | bytes 639008 | tf_op jit(solution)/shard_map/ppermute | solution.py:37
  103.6 6.6 collective-permute-done.10.refs_3_
  120.3 9.8 %collective-permute-done.27.refs_2_ = bf16[2944,128]{1,0:T(8,128)(2,1)} collective-permute-done((bf16[2944,128]{1,0:T(8,128)(2,1)S(1)}, bf16[2944,128]{1,0:T(8,128)(2,1)}, u32[]{:S(2)}, u32[]{:S(2)}) %collective-permute-start.27) | collective-permute-done | bytes 753696 | tf_op jit(solution)/shard_map/ppermute | solution.py:37
  131.4 14.9 %collective-permute-done.28.refs_3_ = bf16[2944,128]{1,0:T(8,128)(2,1)} collective-permute-done((bf16[2944,128]{1,0:T(8,128)(2,1)}, bf16[2944,128]{1,0:T(8,128)(2,1)}, u32[]{:S(2)}, u32[]{:S(2)}) %collective-permute-start.28) | collective-permute-done | bytes 753696 | tf_op jit(solution)/shard_map/ppermute | solution.py:37
  151.1 5.1 collective-permute-start.56
  172.3 5.3 shard_map.202.refs_8_
  178.5 5.1 shard_map.203.refs_8_
  188.5 4.8 shard_map.204
  206.7 7.6 reshape.676
  225.8 8.3 fusion.87
  236.5 8.6 reshape.679
  245.2 9.3 reshape.680
  268.6 6.8 collective-permute-done.58.refs_1_
  276.6 4.5 multiply_convert_fusion.1
  318.9 4.3 reshape.683
  347.4 18.7 %shard_map.209 = bf16[896,512]{1,0:T(8,128)(2,1)S(1)} custom-call(bf16[896,512]{1,0:T(8,128)(2,1)S(1)} %pad.50.q_ref, bf16[1280,512]{1,0:T(8,128)(2,1)S(1)} %pad.51.k_ref, bf16[1280,512]{1,0:T(8,128)(2,1)S(1)} %pad.52.v_ref, s32[896,1]{1,0:T(8,128)S(1)} %copy-done.19, s32[1,1280]{1,0:T(1,128)S(1)} %broadcast_in_dim.92.kid_ref), custom_call_target="tpu_custom_call" | custom-call | flops 939524096 | bytes 5242880 | tf_op jit(solution)/shard_map/pallas_call | solution.py:470
  369.1 18.2 %multiply_convert_fusion = (bf16[864,2048]{1,0:T(8,128)(2,1)S(1)}, f32[864,2048]{1,0:T(8,128)}, f32[864,2048]{1,0:T(8,128)}) fusion(f32[2048]{0:T(1024)S(1)} %fusion.50, bf16[864,512]{1,0:T(8,128)(2,1)S(1)} %add_convert_fusion.2.refs_6_, bf16[512,2048]{1,0:T(8,128)(2,1)S(1)} %copy-done.68), kind=kOutput, calls=%fused_computation.17 | convolution fusion | flops 1928724480 | bytes 20684800 | tf_op jit(solution)/shard_map/dot_general | solution.py:329
  392.1 4.8 multiply_reduce_fusion
  398.2 6.0 collective-permute-start.72
  420.9 5.5 convert_reduce_fusion.2
  431.5 8.2 convert_reduce_fusion.1
  447.8 40.2 %shard_map.210 = (f32[896,512]{1,0:T(8,128)}, f32[1280,512]{1,0:T(8,128)}, f32[1280,512]{1,0:T(8,128)}) custom-call(bf16[896,512]{1,0:T(8,128)(2,1)S(1)} %copy-done.18, bf16[896,512]{1,0:T(8,128)(2,1)S(1)} %pad.55.g_ref, bf16[1280,512]{1,0:T(8,128)(2,1)S(1)} %pad.51.k_ref, bf16[1280,512]{1,0:T(8,128)(2,1)S(1)} %pad.52.v_ref, ...), custom_call_target="tpu_custom_call" | custom-call | flops 2348810240 | bytes 13107200 | tf_op jit(solution)/shard_map/pallas_call | solution.py:501
  499.3 7.7 collective-permute-done.78
  520.0 10.4 %collective-permute-start.79 = (bf16[192,512]{1,0:T(8,128)(2,1)S(1)}, bf16[192,512]{1,0:T(8,128)(2,1)S(1)}, u32[]{:S(2)}, u32[]{:S(2)}) collective-permute-start(bf16[192,512]{1,0:T(8,128)(2,1)S(1)} %pad_maximum_fusion.31), channel_id=1, source_target_pairs={{0,1},{1,0},{2,3},{3,2},{4,5},{5,4},{6,7},{7,6},{8,9},{9,8},{10,11... | collective-permute-start | bytes 589832 | tf_op jit(solution)/shard_map/ppermute | solution.py:37
  531.7 4.9 collective-permute-done.80
  538.2 24.0 %shard_map.211 = (f32[17408,128]{1,0:T(8,128)}, f32[17408,128]{1,0:T(8,128)}) custom-call(s32[1]{0:T(128)} %bitcast.side_ref, bf16[96,768]{1,0:T(8,128)(2,1)} %copy-done.104, bf16[96,512]{1,0:T(8,128)(2,1)} %get-tuple-element.66.refs_1_, bf16[864,512]{1,0:T(8,128)(2,1)} %copy-done.88, bf16[864,1536]{1,0:T(8,128)(2,1)} %copy-done.62, ...), custom_call_target="tpu_custom_call" | custom-call | flops 7700742144 | bytes 17825792 | tf_op jit(solution)/shard_map/pallas_call | solution.py:771
  563.5 5.6 collective-permute-done.5
  570.8 6.6 collective-permute-done.87
  578.1 7.0 add.671
  588.6 4.6 convert_reduce_fusion.6
  615.8 18.4 %collective-permute-done.106 = f32[2,2,2,360,128]{4,3,2,1,0:T(8,128)} collective-permute-done((f32[2,2,2,360,128]{4,3,2,1,0:T(8,128)}, f32[2,2,2,360,128]{4,3,2,1,0:T(8,128)}, u32[]{:S(2)}, u32[]{:S(2)}) %collective-permute-start.106) | collective-permute-done | bytes 1474592 | tf_op jit(solution)/shard_map/ppermute | solution.py:37
  638.2 5.1 collective-permute-done.110
  666.8 11.2 %shard_map.213 = f32[33024,128]{1,0:T(8,128)} custom-call(s32[1]{0:T(128)} %bitcast.side_ref, bf16[192,1728]{1,0:T(8,128)(2,1)S(1)} %pad_maximum_fusion.15.refs_0_, bf16[192,768]{1,0:T(8,128)(2,1)S(1)} %pad_maximum_fusion.24.refs_1_, bf16[192,768]{1,0:T(8,128)(2,1)S(1)} %pad_maximum_fusion.25.refs_2_, bf16[192,2304]{1,0:T(8,128)(2,1)S(1)} %pad_maximum_fusion.7.refs_3_, ...), custom_call_target="tpu_custom_call" | custom-call | flops 1623195648 | bytes 16908288 | tf_op jit(solution)/shard_map/pallas_call | solution.py:676
  696.8 60.8 %collective-permute-done.116 = f32[1,1,2,368,128]{4,3,2,1,0:T(8,128)S(1)} collective-permute-done((f32[1,1,2,368,128]{4,3,2,1,0:T(8,128)S(1)}, f32[1,1,2,368,128]{4,3,2,1,0:T(8,128)S(1)}, u32[]{:S(2)}, u32[]{:S(2)}) %collective-permute-start.116) | collective-permute-done | bytes 376864 | tf_op jit(solution)/shard_map/ppermute | solution.py:37
  762.8 7.3 collective-permute-done.113
  781.6 24.6 %collective-permute-done.99 = f32[2,1,1,1376,128]{4,3,2,1,0:T(8,128)S(1)} collective-permute-done((f32[2,1,1,1376,128]{4,3,2,1,0:T(8,128)S(1)}, f32[2,1,1,1376,128]{4,3,2,1,0:T(8,128)S(1)}, u32[]{:S(2)}, u32[]{:S(2)}) %collective-permute-start.99) | collective-permute-done | bytes 1409056 | tf_op jit(solution)/shard_map/ppermute | solution.py:37
  808.8 7.0 collective-permute-done.103
  816.1 13.9 %collective-permute-done.100 = f32[2,1,1,688,128]{4,3,2,1,0:T(8,128)S(1)} collective-permute-done((f32[2,1,1,688,128]{4,3,2,1,0:T(8,128)S(1)}, f32[2,1,1,688,128]{4,3,2,1,0:T(8,128)S(1)}, u32[]{:S(2)}, u32[]{:S(2)}) %collective-permute-start.100) | collective-permute-done | bytes 704544 | tf_op jit(solution)/shard_map/ppermute | solution.py:37
  833.3 32.6 %collective-permute-done.104 = f32[1,1,2,688,128]{4,3,2,1,0:T(8,128)S(1)} collective-permute-done((f32[1,1,2,688,128]{4,3,2,1,0:T(8,128)S(1)}, f32[1,1,2,688,128]{4,3,2,1,0:T(8,128)S(1)}, u32[]{:S(2)}, u32[]{:S(2)}) %collective-permute-start.104) | collective-permute-done | bytes 704544 | tf_op jit(solution)/shard_map/ppermute | solution.py:37
  866.6 11.6 %collective-permute-done.97 = f32[1,1,1,688,128]{4,3,2,1,0:T(8,128)S(1)} collective-permute-done((f32[1,1,1,688,128]{4,3,2,1,0:T(8,128)S(1)}, f32[1,1,1,688,128]{4,3,2,1,0:T(8,128)S(1)}, u32[]{:S(2)}, u32[]{:S(2)}) %collective-permute-start.97) | collective-permute-done | bytes 352288 | tf_op jit(solution)/shard_map/ppermute | solution.py:37
  882.8 7.3 collective-permute-done.123
  890.2 7.4 collective-permute-done.124
  930.2 6.8 shard_map.215
  941.4 12.8 %shard_map.214 = (f32[8256,128]{1,0:T(8,128)}, f32[8256,128]{1,0:T(8,128)}, f32[8256,128]{1,0:T(8,128)}, bf16[8256,128]{1,0:T(8,128)(2,1)}, f32[8256,128]{1,0:T(8,128)}) custom-call(s32[1]{0:T(128)} %bitcast.side_ref, f32[3]{0:T(128)S(1)} %pad_maximum_fusion.38.scalar_ref, f32[4128,128]{1,0:T(8,128)S(1)} %pad_maximum_fusion.1.mine_ref, ...), custom_call_target="tpu_custom_call" | custom-call | tf_op jit(solution)/shard_map/pallas_call | solution.py:828
  (992 shorter events, 393.5 us)
Async XLA Ops:
  5.0 29.5 %collective-permute-start.24 = (bf16[736,128]{1,0:T(8,128)(2,1)S(1)}, bf16[736,128]{1,0:T(8,128)(2,1)}, u32[]{:S(2)}, u32[]{:S(2)}) collective-permute-start(bf16[736,128]{1,0:T(8,128)(2,1)S(1)} %slice.443), channel_id=1, source_target_pairs={{0,16},{4,20},{8,24},{12,28},{16,0},{20,4},{24,8},{28,12},{1,17},{... | collective-permute-start | bytes 565256 | tf_op jit(solution)/shard_map/ppermute | solution.py:37
  7.7 25.1 %collective-permute-start.15 = (bf16[704,128]{1,0:T(8,128)(2,1)S(1)}, bf16[704,128]{1,0:T(8,128)(2,1)}, u32[]{:S(2)}, u32[]{:S(2)}) collective-permute-start(bf16[704,128]{1,0:T(8,128)(2,1)S(1)} %slice.441), channel_id=1, source_target_pairs={{0,2},{1,3},{2,0},{3,1},{4,6},{5,7},{6,4},{7,5},{8,10},{9,11},{10,... | collective-permute-start | bytes 540680 | tf_op jit(solution)/shard_map/ppermute | solution.py:37
  35.5 26.1 %collective-permute-start.25 = (bf16[1472,128]{1,0:T(8,128)(2,1)S(1)}, bf16[1472,128]{1,0:T(8,128)(2,1)S(1)}, u32[]{:S(2)}, u32[]{:S(2)}) collective-permute-start(bf16[1472,128]{1,0:T(8,128)(2,1)S(1)} %pad_maximum_fusion.18), channel_id=1, source_target_pairs={{0,8},{4,12},{8,0},{12,4},{16,24},{20,28},{24,16},{28,20},{1,9},{5... | collective-permute-start | bytes 1130504 | tf_op jit(solution)/shard_map/ppermute | solution.py:37
  41.2 38.6 %collective-permute-start.8 = (bf16[2496,128]{1,0:T(8,128)(2,1)S(1)}, bf16[2496,128]{1,0:T(8,128)(2,1)}, u32[]{:S(2)}, u32[]{:S(2)}) collective-permute-start(bf16[2496,128]{1,0:T(8,128)(2,1)S(1)} %pad_maximum_fusion.16.refs_0_), channel_id=1, source_target_pairs={{0,16},{4,20},{8,24},{12,28},{16,0},{20,4},{24,8},{28,12},{1,17},{... | collective-permute-start | bytes 1916936 | tf_op jit(solution)/shard_map/ppermute | solution.py:37
  55.8 31.5 %collective-permute-start.17 = (bf16[2816,128]{1,0:T(8,128)(2,1)S(1)}, bf16[2816,128]{1,0:T(8,128)(2,1)}, u32[]{:S(2)}, u32[]{:S(2)}) collective-permute-start(bf16[2816,128]{1,0:T(8,128)(2,1)S(1)} %pad_maximum_fusion.10.refs_0_), channel_id=1, source_target_pairs={{0,8},{4,12},{8,0},{12,4},{16,24},{20,28},{24,16},{28,20},{1,9},{5... | collective-permute-start | bytes 2162696 | tf_op jit(solution)/shard_map/ppermute | solution.py:37
  57.2 43.6 %collective-permute-start.9 = (bf16[2496,128]{1,0:T(8,128)(2,1)S(1)}, bf16[2496,128]{1,0:T(8,128)(2,1)S(1)}, u32[]{:S(2)}, u32[]{:S(2)}) collective-permute-start(bf16[2496,128]{1,0:T(8,128)(2,1)S(1)} %pad_maximum_fusion.16.refs_0_), channel_id=1, source_target_pairs={{0,8},{4,12},{8,0},{12,4},{16,24},{20,28},{24,16},{28,20},{1,9},{5... | collective-permute-start | bytes 1916936 | tf_op jit(solution)/shard_map/ppermute | solution.py:37
  61.6 41.5 %collective-permute-start.18 = (bf16[2816,128]{1,0:T(8,128)(2,1)S(1)}, bf16[2816,128]{1,0:T(8,128)(2,1)}, u32[]{:S(2)}, u32[]{:S(2)}) collective-permute-start(bf16[2816,128]{1,0:T(8,128)(2,1)S(1)} %pad_maximum_fusion.10.refs_0_), channel_id=1, source_target_pairs={{0,4},{4,0},{8,12},{12,8},{16,20},{20,16},{24,28},{28,24},{1,5},{5... | collective-permute-start | bytes 2162696 | tf_op jit(solution)/shard_map/ppermute | solution.py:37
  79.8 30.4 %collective-permute-start.10 = (bf16[2496,128]{1,0:T(8,128)(2,1)}, bf16[2496,128]{1,0:T(8,128)(2,1)}, u32[]{:S(2)}, u32[]{:S(2)}) collective-permute-start(bf16[2496,128]{1,0:T(8,128)(2,1)} %collective-permute-done.8.refs_1_), channel_id=1, source_target_pairs={{0,8},{4,12},{8,0},{12,4},{16,24},{20,28},{24,16},{28,20},{1,9},{5... | collective-permute-start | bytes 1916936 | tf_op jit(solution)/shard_map/ppermute | solution.py:37
  80.8 30.7 %collective-permute-start.26 = (bf16[2944,128]{1,0:T(8,128)(2,1)S(1)}, bf16[2944,128]{1,0:T(8,128)(2,1)}, u32[]{:S(2)}, u32[]{:S(2)}) collective-permute-start(bf16[2944,128]{1,0:T(8,128)(2,1)S(1)} %pad_maximum_fusion.9.refs_0_), channel_id=1, source_target_pairs={{0,4},{4,0},{8,12},{12,8},{16,20},{20,16},{24,28},{28,24},{1,5},{5... | collective-permute-start | bytes 2261000 | tf_op jit(solution)/shard_map/ppermute | solution.py:37
  87.2 26.7 %collective-permute-start.19 = (bf16[2816,128]{1,0:T(8,128)(2,1)}, bf16[2816,128]{1,0:T(8,128)(2,1)S(1)}, u32[]{:S(2)}, u32[]{:S(2)}) collective-permute-start(bf16[2816,128]{1,0:T(8,128)(2,1)} %collective-permute-done.17.refs_1_), channel_id=1, source_target_pairs={{0,4},{4,0},{8,12},{12,8},{16,20},{20,16},{24,28},{28,24},{1,5},{5... | collective-permute-start | bytes 2162696 | tf_op jit(solution)/shard_map/ppermute | solution.py:37
  111.5 34.8 %collective-permute-start.28 = (bf16[2944,128]{1,0:T(8,128)(2,1)}, bf16[2944,128]{1,0:T(8,128)(2,1)}, u32[]{:S(2)}, u32[]{:S(2)}) collective-permute-start(bf16[2944,128]{1,0:T(8,128)(2,1)} %collective-permute-done.26.refs_1_), channel_id=1, source_target_pairs={{0,2},{1,3},{2,0},{3,1},{4,6},{5,7},{6,4},{7,5},{8,10},{9,11},{10,... | collective-permute-start | bytes 2261000 | tf_op jit(solution)/shard_map/ppermute | solution.py:37
  115.5 44.5 %collective-permute-start.20 = (bf16[2816,128]{1,0:T(8,128)(2,1)S(1)}, bf16[2816,128]{1,0:T(8,128)(2,1)}, u32[]{:S(2)}, u32[]{:S(2)}) collective-permute-start(bf16[2816,128]{1,0:T(8,128)(2,1)S(1)} %pad_maximum_fusion.10.refs_0_), channel_id=1, source_target_pairs={{0,1},{1,0},{2,3},{3,2},{4,5},{5,4},{6,7},{7,6},{8,9},{9,8},{10,11... | collective-permute-start | bytes 2162696 | tf_op jit(solution)/shard_map/ppermute | solution.py:37
  115.5 45.0 %collective-permute-start.21 = (bf16[2816,128]{1,0:T(8,128)(2,1)}, bf16[2816,128]{1,0:T(8,128)(2,1)}, u32[]{:S(2)}, u32[]{:S(2)}) collective-permute-start(bf16[2816,128]{1,0:T(8,128)(2,1)} %collective-permute-done.17.refs_1_), channel_id=1, source_target_pairs={{0,1},{1,0},{2,3},{3,2},{4,5},{5,4},{6,7},{7,6},{8,9},{9,8},{10,11... | collective-permute-start | bytes 2162696 | tf_op jit(solution)/shard_map/ppermute | solution.py:37
  118.4 32.7 %collective-permute-start.4 = (bf16[96,1728]{1,0:T(8,128)(2,1)S(1)}, bf16[96,1728]{1,0:T(8,128)(2,1)S(1)}, u32[]{:S(2)}, u32[]{:S(2)}) collective-permute-start(bf16[96,1728]{1,0:T(8,128)(2,1)S(1)} %slice_add_fusion.2), channel_id=1, source_target_pairs={{0,2},{1,3},{2,0},{3,1},{4,6},{5,7},{6,4},{7,5},{8,10},{9,11},{10,... | collective-permute-start | bytes 995336 | tf_op jit(solution)/shard_map/ppermute | solution.py:37
  130.1 29.2 %collective-permute-start.39 = (bf16[672,128]{1,0:T(8,128)(2,1)}, bf16[672,128]{1,0:T(8,128)(2,1)}, u32[]{:S(2)}, u32[]{:S(2)}) collective-permute-start(bf16[672,128]{1,0:T(8,128)(2,1)} %pad_maximum_fusion.33), channel_id=1, source_target_pairs={{0,2},{1,3},{2,0},{3,1},{4,6},{5,7},{6,4},{7,5},{8,10},{9,11},{10,... | collective-permute-start | bytes 516104 | tf_op jit(solution)/shard_map/ppermute | solution.py:37
  165.2 23.2 %collective-permute-start.13 = (bf16[2496,128]{1,0:T(8,128)(2,1)}, bf16[2496,128]{1,0:T(8,128)(2,1)}, u32[]{:S(2)}, u32[]{:S(2)}) collective-permute-start(bf16[2496,128]{1,0:T(8,128)(2,1)} %copy-done.95), channel_id=1, source_target_pairs={{0,1},{1,0},{2,3},{3,2},{4,5},{5,4},{6,7},{7,6},{8,9},{9,8},{10,11... | collective-permute-start | bytes 1916936 | tf_op jit(solution)/shard_map/ppermute | solution.py:37
  177.7 84.0 %collective-permute-start.40 = (bf16[1344,128]{1,0:T(8,128)(2,1)}, bf16[1344,128]{1,0:T(8,128)(2,1)}, u32[]{:S(2)}, u32[]{:S(2)}) collective-permute-start(bf16[1344,128]{1,0:T(8,128)(2,1)} %constant_dynamic-update-slice_fusion.refs_0_), channel_id=1, source_target_pairs={{0,16},{4,20},{8,24},{12,28},{16,0},{20,4},{24,8},{28,12},{1,17},{... | collective-permute-start | bytes 1032200 | tf_op jit(solution)/shard_map/ppermute | solution.py:37
  183.7 78.7 %collective-permute-start.41 = (bf16[1344,128]{1,0:T(8,128)(2,1)}, bf16[1344,128]{1,0:T(8,128)(2,1)}, u32[]{:S(2)}, u32[]{:S(2)}) collective-permute-start(bf16[1344,128]{1,0:T(8,128)(2,1)} %constant_dynamic-update-slice_fusion.refs_0_), channel_id=1, source_target_pairs={{0,8},{4,12},{8,0},{12,4},{16,24},{20,28},{24,16},{28,20},{1,9},{5... | collective-permute-start | bytes 1032200 | tf_op jit(solution)/shard_map/ppermute | solution.py:37
  186.3 32.3 %collective-permute-start.48 = (bf16[736,128]{1,0:T(8,128)(2,1)}, bf16[736,128]{1,0:T(8,128)(2,1)}, u32[]{:S(2)}, u32[]{:S(2)}) collective-permute-start(bf16[736,128]{1,0:T(8,128)(2,1)} %pad_maximum_fusion.32), channel_id=1, source_target_pairs={{0,16},{4,20},{8,24},{12,28},{16,0},{20,4},{24,8},{28,12},{1,17},{... | collective-permute-start | bytes 565256 | tf_op jit(solution)/shard_map/ppermute | solution.py:37
  188.4 33.7 %collective-permute-start.57 = (bf16[768,128]{1,0:T(8,128)(2,1)}, bf16[768,128]{1,0:T(8,128)(2,1)}, u32[]{:S(2)}, u32[]{:S(2)}) collective-permute-start(bf16[768,128]{1,0:T(8,128)(2,1)} %pad_maximum_fusion.30), channel_id=1, source_target_pairs={{0,8},{4,12},{8,0},{12,4},{16,24},{20,28},{24,16},{28,20},{1,9},{5... | collective-permute-start | bytes 589832 | tf_op jit(solution)/shard_map/ppermute | solution.py:37
  220.2 44.0 %collective-permute-start.49 = (bf16[1472,128]{1,0:T(8,128)(2,1)}, bf16[1472,128]{1,0:T(8,128)(2,1)}, u32[]{:S(2)}, u32[]{:S(2)}) collective-permute-start(bf16[1472,128]{1,0:T(8,128)(2,1)} %constant_dynamic-update-slice_fusion.3.refs_0_), channel_id=1, source_target_pairs={{0,8},{4,12},{8,0},{12,4},{16,24},{20,28},{24,16},{28,20},{1,9},{5... | collective-permute-start | bytes 1130504 | tf_op jit(solution)/shard_map/ppermute | solution.py:37
  223.1 32.1 %collective-permute-start.33 = (bf16[96,1536]{1,0:T(8,128)(2,1)S(1)}, bf16[96,1536]{1,0:T(8,128)(2,1)}, u32[]{:S(2)}, u32[]{:S(2)}) collective-permute-start(bf16[96,1536]{1,0:T(8,128)(2,1)S(1)} %concatenate.221), channel_id=1, source_target_pairs={{0,1},{1,0},{2,3},{3,2},{4,5},{5,4},{6,7},{7,6},{8,9},{9,8},{10,11... | collective-permute-start | bytes 884744 | tf_op jit(solution)/shard_map/ppermute | solution.py:37
  225.8 30.9 %collective-permute-start.35 = (bf16[96,1536]{1,0:T(8,128)(2,1)}, bf16[96,1536]{1,0:T(8,128)(2,1)}, u32[]{:S(2)}, u32[]{:S(2)}) collective-permute-start(bf16[96,1536]{1,0:T(8,128)(2,1)} %collective-permute-done.34), channel_id=1, source_target_pairs={{0,1},{1,0},{2,3},{3,2},{4,5},{5,4},{6,7},{7,6},{8,9},{9,8},{10,11... | collective-permute-start | bytes 884744 | tf_op jit(solution)/shard_map/ppermute | solution.py:37
  306.5 28.8 %collective-permute-start.65 = (bf16[96,512]{1,0:T(8,128)(2,1)S(1)}, bf16[96,512]{1,0:T(8,128)(2,1)S(1)}, u32[]{:S(2)}, u32[]{:S(2)}) collective-permute-start(bf16[96,512]{1,0:T(8,128)(2,1)S(1)} %fusion.25), channel_id=1, source_target_pairs={{0,1},{1,0},{2,3},{3,2},{4,5},{5,4},{6,7},{7,6},{8,9},{9,8},{10,11... | collective-permute-start | bytes 294920 | tf_op jit(solution)/shard_map/ppermute | solution.py:37
  311.4 23.9 %collective-permute-start.67 = (bf16[96,512]{1,0:T(8,128)(2,1)S(1)}, bf16[96,512]{1,0:T(8,128)(2,1)S(1)}, u32[]{:S(2)}, u32[]{:S(2)}) collective-permute-start(bf16[96,512]{1,0:T(8,128)(2,1)S(1)} %collective-permute-done.66), channel_id=1, source_target_pairs={{0,1},{1,0},{2,3},{3,2},{4,5},{5,4},{6,7},{7,6},{8,9},{9,8},{10,11... | collective-permute-start | bytes 294920 | tf_op jit(solution)/shard_map/ppermute | solution.py:37
  569.7 35.0 %collective-permute-start.91 = (bf16[96,3072]{1,0:T(8,128)(2,1)S(1)}, bf16[96,3072]{1,0:T(8,128)(2,1)S(1)}, u32[]{:S(2)}, u32[]{:S(2)}) collective-permute-start(bf16[96,3072]{1,0:T(8,128)(2,1)S(1)} %copy-done.66), channel_id=1, source_target_pairs={{0,1},{1,0},{2,3},{3,2},{4,5},{5,4},{6,7},{7,6},{8,9},{9,8},{10,11... | collective-permute-start | bytes 1769480 | tf_op jit(solution)/shard_map/ppermute | solution.py:37
  598.8 35.4 %collective-permute-start.106 = (f32[2,2,2,360,128]{4,3,2,1,0:T(8,128)}, f32[2,2,2,360,128]{4,3,2,1,0:T(8,128)}, u32[]{:S(2)}, u32[]{:S(2)}) collective-permute-start(f32[2,2,2,360,128]{4,3,2,1,0:T(8,128)} %constant_dynamic-slice_fusion.11), channel_id=1, source_target_pairs={{0,2},{1,3},{2,0},{3,1},{4,6},{5,7},{6,4},{7,5},{8,10},{9,11},{10,... | collective-permute-start | bytes 4423688 | tf_op jit(solution)/shard_map/ppermute | solution.py:37
  608.2 35.1 %collective-permute-start.110 = (f32[2,2,1,720,128]{4,3,2,1,0:T(8,128)S(1)}, f32[2,2,1,720,128]{4,3,2,1,0:T(8,128)S(1)}, u32[]{:S(2)}, u32[]{:S(2)}) collective-permute-start(f32[2,2,1,720,128]{4,3,2,1,0:T(8,128)S(1)} %constant_dynamic-slice_fusion.7), channel_id=1, source_target_pairs={{0,4},{4,0},{8,12},{12,8},{16,20},{20,16},{24,28},{28,24},{1,5},{5... | collective-permute-start | bytes 4423688 | tf_op jit(solution)/shard_map/ppermute | solution.py:37
  610.4 35.7 %collective-permute-start.114 = (f32[2,1,2,736,128]{4,3,2,1,0:T(8,128)S(1)}, f32[2,1,2,736,128]{4,3,2,1,0:T(8,128)S(1)}, u32[]{:S(2)}, u32[]{:S(2)}) collective-permute-start(f32[2,1,2,736,128]{4,3,2,1,0:T(8,128)S(1)} %constant_dynamic-slice_fusion.3), channel_id=1, source_target_pairs={{0,8},{4,12},{8,0},{12,4},{16,24},{20,28},{24,16},{28,20},{1,9},{5... | collective-permute-start | bytes 4521992 | tf_op jit(solution)/shard_map/ppermute | solution.py:37
  614.1 35.0 %collective-permute-start.83 = (f32[96,1536]{1,0:T(8,128)S(1)}, f32[96,1536]{1,0:T(8,128)S(1)}, u32[]{:S(2)}, u32[]{:S(2)}) collective-permute-start(f32[96,1536]{1,0:T(8,128)S(1)} %slice_add_fusion), channel_id=1, source_target_pairs={{0,2},{1,3},{2,0},{3,1},{4,6},{5,7},{6,4},{7,5},{8,10},{9,11},{10,... | collective-permute-start | bytes 1769480 | tf_op jit(solution)/shard_map/ppermute | solution.py:37
  636.8 27.6 %collective-permute-start.107 = (f32[2,2,1,360,128]{4,3,2,1,0:T(8,128)}, f32[2,2,1,360,128]{4,3,2,1,0:T(8,128)}, u32[]{:S(2)}, u32[]{:S(2)}) collective-permute-start(f32[2,2,1,360,128]{4,3,2,1,0:T(8,128)} %constant_dynamic-slice_fusion.10), channel_id=1, source_target_pairs={{0,4},{4,0},{8,12},{12,8},{16,20},{20,16},{24,28},{28,24},{1,5},{5... | collective-permute-start | bytes 2211848 | tf_op jit(solution)/shard_map/ppermute | solution.py:37
  644.4 37.3 %collective-permute-start.111 = (f32[2,1,1,720,128]{4,3,2,1,0:T(8,128)}, f32[2,1,1,720,128]{4,3,2,1,0:T(8,128)}, u32[]{:S(2)}, u32[]{:S(2)}) collective-permute-start(f32[2,1,1,720,128]{4,3,2,1,0:T(8,128)} %constant_dynamic-slice_fusion.6), channel_id=1, source_target_pairs={{0,8},{4,12},{8,0},{12,4},{16,24},{20,28},{24,16},{28,20},{1,9},{5... | collective-permute-start | bytes 2211848 | tf_op jit(solution)/shard_map/ppermute | solution.py:37
  647.3 43.4 %collective-permute-start.115 = (f32[2,1,2,368,128]{4,3,2,1,0:T(8,128)}, f32[2,1,2,368,128]{4,3,2,1,0:T(8,128)}, u32[]{:S(2)}, u32[]{:S(2)}) collective-permute-start(f32[2,1,2,368,128]{4,3,2,1,0:T(8,128)} %constant_dynamic-slice_fusion.2), channel_id=1, source_target_pairs={{0,2},{1,3},{2,0},{3,1},{4,6},{5,7},{6,4},{7,5},{8,10},{9,11},{10,... | collective-permute-start | bytes 2261000 | tf_op jit(solution)/shard_map/ppermute | solution.py:37
  665.7 26.9 %collective-permute-start.108 = (f32[2,1,1,360,128]{4,3,2,1,0:T(8,128)S(1)}, f32[2,1,1,360,128]{4,3,2,1,0:T(8,128)}, u32[]{:S(2)}, u32[]{:S(2)}) collective-permute-start(f32[2,1,1,360,128]{4,3,2,1,0:T(8,128)S(1)} %constant_dynamic-slice_fusion.9), channel_id=1, source_target_pairs={{0,8},{4,12},{8,0},{12,4},{16,24},{20,28},{24,16},{28,20},{1,9},{5... | collective-permute-start | bytes 1105928 | tf_op jit(solution)/shard_map/ppermute | solution.py:37
  680.2 93.3 %collective-permute-start.98 = (f32[2,2,1,1376,128]{4,3,2,1,0:T(8,128)S(1)}, f32[2,2,1,1376,128]{4,3,2,1,0:T(8,128)S(1)}, u32[]{:S(2)}, u32[]{:S(2)}) collective-permute-start(f32[2,2,1,1376,128]{4,3,2,1,0:T(8,128)S(1)} %constant_dynamic-slice_fusion.19), channel_id=1, source_target_pairs={{0,4},{4,0},{8,12},{12,8},{16,20},{20,16},{24,28},{28,24},{1,5},{5... | collective-permute-start | bytes 8454152 | tf_op jit(solution)/shard_map/ppermute | solution.py:37
  686.9 87.8 %collective-permute-start.102 = (f32[2,1,2,1376,128]{4,3,2,1,0:T(8,128)S(1)}, f32[2,1,2,1376,128]{4,3,2,1,0:T(8,128)S(1)}, u32[]{:S(2)}, u32[]{:S(2)}) collective-permute-start(f32[2,1,2,1376,128]{4,3,2,1,0:T(8,128)S(1)} %constant_dynamic-slice_fusion.15), channel_id=1, source_target_pairs={{0,8},{4,12},{8,0},{12,4},{16,24},{20,28},{24,16},{28,20},{1,9},{5... | collective-permute-start | bytes 8454152 | tf_op jit(solution)/shard_map/ppermute | solution.py:37
  690.7 83.4 %collective-permute-start.94 = (f32[2,2,2,688,128]{4,3,2,1,0:T(8,128)S(1)}, f32[2,2,2,688,128]{4,3,2,1,0:T(8,128)S(1)}, u32[]{:S(2)}, u32[]{:S(2)}) collective-permute-start(f32[2,2,2,688,128]{4,3,2,1,0:T(8,128)S(1)} %constant_dynamic-slice_fusion.23), channel_id=1, source_target_pairs={{0,2},{1,3},{2,0},{3,1},{4,6},{5,7},{6,4},{7,5},{8,10},{9,11},{10,... | collective-permute-start | bytes 8454152 | tf_op jit(solution)/shard_map/ppermute | solution.py:37
  692.5 65.1 %collective-permute-start.116 = (f32[1,1,2,368,128]{4,3,2,1,0:T(8,128)S(1)}, f32[1,1,2,368,128]{4,3,2,1,0:T(8,128)S(1)}, u32[]{:S(2)}, u32[]{:S(2)}) collective-permute-start(f32[1,1,2,368,128]{4,3,2,1,0:T(8,128)S(1)} %constant_dynamic-slice_fusion.1), channel_id=1, source_target_pairs={{0,16},{4,20},{8,24},{12,28},{16,0},{20,4},{24,8},{28,12},{1,17},{... | collective-permute-start | bytes 1130504 | tf_op jit(solution)/shard_map/ppermute | solution.py:37
  694.7 66.9 %collective-permute-start.109 = (f32[1,1,1,360,128]{4,3,2,1,0:T(8,128)S(1)}, f32[1,1,1,360,128]{4,3,2,1,0:T(8,128)S(1)}, u32[]{:S(2)}, u32[]{:S(2)}) collective-permute-start(f32[1,1,1,360,128]{4,3,2,1,0:T(8,128)S(1)} %constant_dynamic-slice_fusion.8), channel_id=1, source_target_pairs={{0,16},{4,20},{8,24},{12,28},{16,0},{20,4},{24,8},{28,12},{1,17},{... | collective-permute-start | bytes 552968 | tf_op jit(solution)/shard_map/ppermute | solution.py:37
  773.5 128.5 %collective-permute-start.129 = (f32[368,128]{1,0:T(8,128)S(1)}, f32[368,128]{1,0:T(8,128)S(1)}, u32[]{:S(2)}, u32[]{:S(2)}) collective-permute-start(f32[368,128]{1,0:T(8,128)S(1)} %get-tuple-element.101), channel_id=1, source_target_pairs={{0,2},{1,3},{2,0},{3,1},{4,6},{5,7},{6,4},{7,5},{8,10},{9,11},{10,... | collective-permute-start | bytes 565256 | tf_op jit(solution)/shard_map/ppermute | solution.py:37
  774.2 32.0 %collective-permute-start.99 = (f32[2,1,1,1376,128]{4,3,2,1,0:T(8,128)S(1)}, f32[2,1,1,1376,128]{4,3,2,1,0:T(8,128)S(1)}, u32[]{:S(2)}, u32[]{:S(2)}) collective-permute-start(f32[2,1,1,1376,128]{4,3,2,1,0:T(8,128)S(1)} %constant_dynamic-slice_fusion.18), channel_id=1, source_target_pairs={{0,8},{4,12},{8,0},{12,4},{16,24},{20,28},{24,16},{28,20},{1,9},{5... | collective-permute-start | bytes 4227080 | tf_op jit(solution)/shard_map/ppermute | solution.py:37
  774.7 33.5 %collective-permute-start.95 = (f32[2,2,1,688,128]{4,3,2,1,0:T(8,128)S(1)}, f32[2,2,1,688,128]{4,3,2,1,0:T(8,128)S(1)}, u32[]{:S(2)}, u32[]{:S(2)}) collective-permute-start(f32[2,2,1,688,128]{4,3,2,1,0:T(8,128)S(1)} %constant_dynamic-slice_fusion.22), channel_id=1, source_target_pairs={{0,4},{4,0},{8,12},{12,8},{16,20},{20,16},{24,28},{28,24},{1,5},{5... | collective-permute-start | bytes 4227080 | tf_op jit(solution)/shard_map/ppermute | solution.py:37
  777.6 38.2 %collective-permute-start.103 = (f32[2,1,2,688,128]{4,3,2,1,0:T(8,128)S(1)}, f32[2,1,2,688,128]{4,3,2,1,0:T(8,128)S(1)}, u32[]{:S(2)}, u32[]{:S(2)}) collective-permute-start(f32[2,1,2,688,128]{4,3,2,1,0:T(8,128)S(1)} %constant_dynamic-slice_fusion.14), channel_id=1, source_target_pairs={{0,2},{1,3},{2,0},{3,1},{4,6},{5,7},{6,4},{7,5},{8,10},{9,11},{10,... | collective-permute-start | bytes 4227080 | tf_op jit(solution)/shard_map/ppermute | solution.py:37
  806.4 23.5 %collective-permute-start.100 = (f32[2,1,1,688,128]{4,3,2,1,0:T(8,128)S(1)}, f32[2,1,1,688,128]{4,3,2,1,0:T(8,128)S(1)}, u32[]{:S(2)}, u32[]{:S(2)}) collective-permute-start(f32[2,1,1,688,128]{4,3,2,1,0:T(8,128)S(1)} %constant_dynamic-slice_fusion.17), channel_id=1, source_target_pairs={{0,2},{1,3},{2,0},{3,1},{4,6},{5,7},{6,4},{7,5},{8,10},{9,11},{10,... | collective-permute-start | bytes 2113544 | tf_op jit(solution)/shard_map/ppermute | solution.py:37
  816.0 49.9 %collective-permute-start.104 = (f32[1,1,2,688,128]{4,3,2,1,0:T(8,128)S(1)}, f32[1,1,2,688,128]{4,3,2,1,0:T(8,128)S(1)}, u32[]{:S(2)}, u32[]{:S(2)}) collective-permute-start(f32[1,1,2,688,128]{4,3,2,1,0:T(8,128)S(1)} %constant_dynamic-slice_fusion.13), channel_id=1, source_target_pairs={{0,16},{4,20},{8,24},{12,28},{16,0},{20,4},{24,8},{28,12},{1,17},{... | collective-permute-start | bytes 2113544 | tf_op jit(solution)/shard_map/ppermute | solution.py:37
  830.1 49.2 %collective-permute-start.101 = (f32[1,1,1,688,128]{4,3,2,1,0:T(8,128)S(1)}, f32[1,1,1,688,128]{4,3,2,1,0:T(8,128)S(1)}, u32[]{:S(2)}, u32[]{:S(2)}) collective-permute-start(f32[1,1,1,688,128]{4,3,2,1,0:T(8,128)S(1)} %constant_dynamic-slice_fusion.16), channel_id=1, source_target_pairs={{0,16},{4,20},{8,24},{12,28},{16,0},{20,4},{24,8},{28,12},{1,17},{... | collective-permute-start | bytes 1056776 | tf_op jit(solution)/shard_map/ppermute | solution.py:37
  831.3 46.9 %collective-permute-start.97 = (f32[1,1,1,688,128]{4,3,2,1,0:T(8,128)S(1)}, f32[1,1,1,688,128]{4,3,2,1,0:T(8,128)S(1)}, u32[]{:S(2)}, u32[]{:S(2)}) collective-permute-start(f32[1,1,1,688,128]{4,3,2,1,0:T(8,128)S(1)} %constant_dynamic-slice_fusion.20), channel_id=1, source_target_pairs={{0,16},{4,20},{8,24},{12,28},{16,0},{20,4},{24,8},{28,12},{1,17},{... | collective-permute-start | bytes 1056776 | tf_op jit(solution)/shard_map/ppermute | solution.py:37
  901.8 35.2 %collective-permute-start.126 = (f32[4128,128]{1,0:T(8,128)S(1)}, f32[4128,128]{1,0:T(8,128)}, u32[]{:S(2)}, u32[]{:S(2)}) collective-permute-start(f32[4128,128]{1,0:T(8,128)S(1)} %pad_maximum_fusion.1.mine_ref), channel_id=1, source_target_pairs={{0,1},{1,0},{2,3},{3,2},{4,5},{5,4},{6,7},{7,6},{8,9},{9,8},{10,11... | collective-permute-start | bytes 6340616 | tf_op jit(solution)/shard_map/ppermute | solution.py:37
  (301 other events, 3173.6 us)

commit v2 on v1

v2 whole, which is shorter than its diff:
```python
import functools
import math

import jax
import jax.numpy as jnp
from jax import lax
from jax.experimental import pallas as pl
from jax.experimental.pallas import tpu as pltpu
from jax.sharding import PartitionSpec as P

D = 768
H = 12
F = 3072
E = 512
EH = 16
FE = 2048
PATCH = 1728
L = 1728
TILE_HI = 192
ER = 66048
DR = 34816


NORM_EPS = 1e-06
MASK_FILL = -1e30
CLIP_LIMIT = 0.0002
LEARN_RATE = 0.02
BETA_ONE = 0.5
BETA_TWO = 0.5
ADAM_EPS = 1e-08
WEIGHT_DECAY = 0.05
EMA_RATE = 0.9


def swap(block, axis, bit):
    count = lax.axis_size(axis)
    return lax.ppermute(block, axis, [(i, i ^ bit) for i in range(count)])


def bit_of(axis, bit):
    return (lax.axis_index(axis) // bit) % 2


def double(block, dim, axis, bit):
    mine = bit_of(axis, bit)
    other = swap(block, axis, bit)
    first = jnp.where(mine == 0, block, other)
    second = jnp.where(mine == 0, other, block)
    return jnp.stack([first, second], axis=dim)


def total(values):
    for axis in ("grp", "dp"):
        bit = 1
        while bit < lax.axis_size(axis):
            values = values + swap(values, axis, bit)
            bit *= 2
    return values


def dp_bits():
    bits = [1]
    while bits[-1] * 2 < lax.axis_size("dp"):
        bits.append(bits[-1] * 2)
    return bits


def cut(rows, shares):
    unit = 16 if rows % 16 == 0 else 2
    sizes = [int(round(rows // unit * share)) * unit for share in shares]
    return sizes + [rows - sum(sizes)]


def gather_quarters(shard):
    part = shard.shape[0] // 4
    quarter = lax.dynamic_slice_in_dim(shard, lax.axis_index("grp") * part, part, 0)
    return lax.all_gather(quarter, ("dp", "grp"), axis=0, tiled=True)


def gather_both(enc_shard, dec_shard):
    enc_copy = gather_quarters(enc_shard)
    enc_copy, dec_shard = lax.optimization_barrier((enc_copy, dec_shard))
    return enc_copy, gather_quarters(dec_shard)


def section(cells, dim, start, size):
    return lax.dynamic_slice_in_dim(cells, start, size, dim)


def reduce_bit(cells, dim, axis, bit, start=0, size=None):
    half = (cells.shape[dim] if size is None else size) // 2
    mine = bit_of(axis, bit)
    sent = section(cells, dim, start + (1 - mine) * half, half)
    return section(cells, dim, start + mine * half, half) + swap(sent, axis, bit)


def dec_routes():
    bits = [("dp", bit) for bit in dp_bits()]
    return [bits[:1] + [("grp", 2)] + bits[1:], bits[1:2] + [("grp", 2)] + bits[2:] + bits[:1]]


def reduce_first(half, routes, shares):
    shards = lax.axis_size("dp")
    half_rows = half.shape[0] // shards
    bits = dp_bits()
    names = [("dp", bit) for bit in reversed(bits)]
    cells = half.reshape([2] * len(bits) + [half_rows, 128])
    blocks = []
    start = 0
    for route, rows in zip(routes, cut(half_rows, shares)):
        axis, bit = route[0]
        if axis == "grp":
            block = reduce_bit(cells, len(bits), axis, bit, start, rows)
        else:
            dim = names.index(route[0])
            mine = bit_of(axis, bit)

            def pick(index, dim=dim, start=start, rows=rows):
                corner = [0] * dim + [index] + [0] * (len(bits) - dim - 1) + [start, 0]
                sizes = [2] * dim + [1] + [2] * (len(bits) - dim - 1) + [rows, 128]
                return lax.dynamic_slice(cells, corner, sizes)

            block = pick(mine) + swap(pick(1 - mine), axis, bit)
        blocks.append(block)
        start += rows
    return blocks


def reduce_rest(blocks, routes):
    bits = dp_bits()
    names = [("dp", bit) for bit in reversed(bits)]
    blocks = list(blocks)
    for step in range(1, len(routes[0])):
        for index, route in enumerate(routes):
            axis, bit = route[step]
            dim = len(bits) if axis == "grp" else names.index(route[step])
            blocks[index] = reduce_bit(blocks[index], dim, axis, bit)
    return [block.reshape(-1, 128) for block in blocks]


def dp_routes():
    bits = [("dp", bit) for bit in dp_bits()]
    return [bits, bits[1:] + bits[:1]]


def spread_pieces(pieces):
    wide = [double(piece, 0, "grp", 2).reshape(-1, 128) for piece in pieces]
    mine = jnp.concatenate(wide, axis=0)
    return mine, swap(mine, "grp", 1)


def group_rows(block):
    across = swap(block, "grp", 2)
    near, far = (
        swap(block, "grp", 1),
        swap(across, "grp", 1),
    )
    return jnp.concatenate([block, near, across, far], axis=0)


def own_rows(blocks):
    count = blocks.shape[0] // 4
    parts = [lax.slice_in_dim(blocks, i * count, (i + 1) * count, axis=0) for i in range(4)]
    sent = jnp.concatenate([parts[1], parts[3]], axis=0)
    arrived = swap(sent, "grp", 1)
    kept = parts[0] + arrived[:count]
    other = parts[2] + arrived[count:]
    return kept + swap(other, "grp", 2)


def extended(cells, width):
    count = lax.axis_size("grp")
    ends = count - 1
    head = cells[:width]
    tail = cells[cells.shape[0] - width :]
    return jnp.concatenate(
        [
            lax.ppermute(tail, "grp", [(i, i + 1) for i in range(ends)]),
            cells,
            lax.ppermute(head, "grp", [(i + 1, i) for i in range(ends)]),
        ],
        axis=0,
    )


def passed_along(block, axis, distance):
    devices = range(lax.axis_size(axis))
    route = [(i - distance, i) for i in devices if i - distance in devices]
    return lax.ppermute(block, axis, route)


def enc_pieces():
    return [
        ("patch_w", (PATCH, D)),
        ("qkv_w", (D, 3 * D)),
        ("out_w", (D, D)),
        ("up_w", (D, F)),
        ("down_w", (F, D)),
        ("patch_b", (D,)),
        ("out_b", (D,)),
        ("up_b", (F,)),
        ("down_b", (D,)),
        ("norm_g", (3, D)),
        ("norm_b", (3, D)),
    ]


def dec_pieces():
    return [
        ("embed_w", (D, E)),
        ("qkv_w", (E, 3 * E)),
        ("out_w", (E, E)),
        ("up_w", (E, FE)),
        ("down_w", (FE, E)),
        ("pix_w", (E, PATCH)),
        ("embed_b", (E,)),
        ("mask_token", (E,)),
        ("out_b", (E,)),
        ("up_b", (FE,)),
        ("down_b", (E,)),
        ("pix_b", (PATCH,)),
        ("norm_g", (3, E)),
        ("norm_b", (3, E)),
    ]


def relayout_kernel(plan, *refs):
    source, outs = refs[0], refs[1 : 1 + len(plan)]
    raw_ref, wide_ref, stages, in_sems, out_sems = (
        refs[1 + len(plan)],
        refs[2 + len(plan)],
        refs[3 + len(plan) : -2],
        refs[-2],
        refs[-1],
    )
    steps = [
        (index, offset + start * blocks, start, rows, blocks)
        for index, (offset, depth, blocks, rows) in enumerate(plan)
        for start in range(0, depth, rows)
    ]

    def fetch(turn):
        _, offset, _, rows, blocks = steps[turn]
        return pltpu.make_async_copy(
            source.at[pl.ds(offset, rows * blocks)],
            raw_ref.at[turn % 2, pl.ds(0, rows * blocks)],
            in_sems.at[turn % 2],
        )

    flight = {}
    fetch(0).start()
    for turn, (index, _, start, rows, blocks) in enumerate(steps):
        if turn + 1 < len(steps):
            fetch(turn + 1).start()
        fetch(turn).wait()
        wide_ref[: rows * blocks, :] = raw_ref[turn % 2, : rows * blocks, :].astype(jnp.float32)
        slot = turn % 2
        if slot in flight:
            flight.pop(slot).wait()
        stage = stages[index].at[slot]
        for block in range(blocks):
            stage[:, block * 128 : (block + 1) * 128] = wide_ref[
                pl.ds(block, rows, stride=blocks), :
            ].astype(jnp.bfloat16)
        flight[slot] = pltpu.make_async_copy(
            stage, outs[index].at[pl.ds(start, rows)], out_sems.at[slot]
        )
        flight[slot].start()
    for copy in flight.values():
        copy.wait()


def relayout(rows, plan):
    anywhere = pl.BlockSpec(memory_space=pl.ANY)
    most = max(step * blocks for _, _, blocks, step in plan)
    return pl.pallas_call(
        functools.partial(relayout_kernel, plan),
        in_specs=[anywhere],
        out_specs=[anywhere] * len(plan),
        out_shape=[
            jax.ShapeDtypeStruct((depth, blocks * 128), jnp.bfloat16)
            for _, depth, blocks, _ in plan
        ],
        scratch_shapes=[
            pltpu.VMEM((2, most, 128), jnp.bfloat16),
            pltpu.VMEM((most, 128), jnp.float32),
        ]
        + [pltpu.VMEM((2, step, blocks * 128), jnp.bfloat16) for _, _, blocks, step in plan]
        + [pltpu.SemaphoreType.DMA((2,)), pltpu.SemaphoreType.DMA((2,))],
        compiler_params=pltpu.CompilerParams(vmem_limit_bytes=40 << 20),
        cost_estimate=pl.CostEstimate(
            flops=0, bytes_accessed=rows.size * 4, transcendentals=0
        ),
    )(rows)


ENC_STEPS = {"patch_w": 576, "qkv_w": 192, "out_w": 384, "up_w": 128, "down_w": 512}
DEC_STEPS = {"embed_w": 768, "qkv_w": 256, "out_w": 512, "up_w": 128, "down_w": 512}


def unpack(rows, pieces, steps):
    table = {}
    offset = 0
    plan = []
    vectors = sum(1 for _, dims in pieces if len(dims) == 2 and dims[0] > 3)
    for piece_name, piece_dims in pieces[:vectors]:
        amount = math.prod(piece_dims) // 128
        if piece_name in steps:
            plan.append((offset, piece_dims[0], piece_dims[1] // 128, steps[piece_name]))
        else:
            table[piece_name] = rows[offset : offset + amount].reshape(piece_dims)
        offset += amount
    small = rows[offset:].reshape(-1)
    table.update(zip(steps, relayout(rows, plan)))
    offset = 0
    for piece_name, piece_dims in pieces[vectors:]:
        amount = math.prod(piece_dims)
        table[piece_name] = small[offset : offset + amount].reshape(piece_dims)
        offset += amount
    return table


def matmul(left, right):
    return jnp.dot(left, right, preferred_element_type=jnp.float32)


def mul_trans(left, right):
    return lax.dot_general(
        left, right, (((1,), (1,)), ((), ())), preferred_element_type=jnp.float32
    )


def trans_mul(left, right):
    return lax.dot_general(
        left, right, (((0,), (0,)), ((), ())), preferred_element_type=jnp.float32
    )


def sincos(positions, width):
    half_width = width // 2
    freq_row = jnp.exp(
        jnp.arange(half_width, dtype=jnp.float32) * (-2.0 * math.log(10000.0) / width)
    )
    angles = positions.astype(jnp.float32)[:, None] * freq_row[None, :]
    return jnp.concatenate([jnp.sin(angles), jnp.cos(angles)], axis=1)


def layer_norm(inputs, gain, shift):
    center = inputs - jnp.mean(inputs, axis=-1, keepdims=True)
    return (
        center * lax.rsqrt(jnp.mean(center * center, axis=-1, keepdims=True) + NORM_EPS) * gain
        + shift
    )


def norm_back(inputs, gain, shift, grad_out):
    outputs, pull = jax.vjp(layer_norm, inputs, gain, shift)
    return pull(grad_out)


def exact_gelu(values):
    return jax.nn.gelu(values, approximate=False)


BLOCK = 128


def head_masks(width):
    lanes = lax.broadcasted_iota(jnp.int32, (1, 128), 1) // width
    return [(lanes == index).astype(jnp.float32) for index in range(128 // width)]


def spread_heads(cells, masks):
    wide = cells.astype(jnp.float32)
    return jnp.concatenate([(wide * mask).astype(jnp.bfloat16) for mask in masks], axis=0)


TILE = 32
TALL = 64


def attend_kernel(
    window, width, q_ref, k_ref, v_ref, qid_ref, kid_ref, o_ref, bias_ref, score_ref, prob_ref
):
    start = pl.multiple_of(pl.program_id(0) * BLOCK, BLOCK)
    scale = width ** (-0.5)
    masks = head_masks(width)
    near = pl.ds(start, window)
    bias_ref[...] = jnp.where(qid_ref[...] == kid_ref[:, near], 0.0, MASK_FILL)
    for group in range(q_ref.shape[1] // 128):
        lanes = slice(group * 128, (group + 1) * 128)
        slot = group % 2
        score_ref[slot] = mul_trans(spread_heads(q_ref[:, lanes], masks), k_ref[near, lanes])
        for first in range(0, len(masks) * BLOCK, TILE):
            rows = slice(first, first + TILE)
            row = first % BLOCK
            part = score_ref[slot, rows, :] * scale + bias_ref[row : row + TILE, :]
            powers = jnp.exp(part - jnp.max(part, axis=1, keepdims=True))
            probs = powers * (1.0 / jnp.sum(powers, axis=1, keepdims=True))
            prob_ref[slot, rows, :] = probs.astype(jnp.bfloat16)
        wide = matmul(prob_ref[slot], v_ref[near, lanes])
        o_ref[:, lanes] = pick_heads(wide, masks).astype(jnp.bfloat16)


def pick_heads(wide, masks):
    return sum(wide[i * BLOCK : (i + 1) * BLOCK] * mask for i, mask in enumerate(masks))


def row_sums(cells, merge):
    return merge(cells.reshape(-1, 8, cells.shape[1]), axis=0)


def attend_back_kernel(window, width, *refs):
    q_ref, g_ref, k_ref, v_ref, qid_ref, kid_ref, dq_ref, dk_ref, dv_ref = refs[:9]
    bias_ref, score_ref, grad_ref, prob_ref, back_ref = refs[9:]
    step = pl.program_id(0)
    start = pl.multiple_of(step * BLOCK, BLOCK)
    scale = width ** (-0.5)
    masks = head_masks(width)

    @pl.when(step == 0)
    def _():
        dk_ref[...] = jnp.zeros_like(dk_ref)
        dv_ref[...] = jnp.zeros_like(dv_ref)

    near = pl.ds(start, window)
    bias_ref[...] = jnp.where(kid_ref[near, :] == qid_ref[...], 0.0, MASK_FILL)
    tiles = [slice(first, first + TALL) for first in range(0, window, TALL)]
    for group in range(q_ref.shape[1] // 128):
        lanes = slice(group * 128, (group + 1) * 128)
        slot = group % 2
        keys = k_ref[near, lanes]
        queries = spread_heads(q_ref[:, lanes], masks)
        outs = spread_heads(g_ref[:, lanes], masks)
        score_ref[slot] = mul_trans(keys, queries)
        grad_ref[slot] = mul_trans(v_ref[near, lanes], outs)
        for index in range(len(masks)):
            head = slice(index * BLOCK, (index + 1) * BLOCK)
            top = None
            for tile in tiles:
                part = score_ref[slot, tile, head] * scale + bias_ref[tile, :]
                score_ref[slot, tile, head] = part
                most = row_sums(part, jnp.max)
                top = most if top is None else jnp.maximum(top, most)
            top = jnp.max(top, axis=0, keepdims=True)
            whole = jnp.zeros((8, BLOCK), jnp.float32)
            for tile in tiles:
                powers = jnp.exp(score_ref[slot, tile, head] - top)
                score_ref[slot, tile, head] = powers
                whole += row_sums(powers, jnp.sum)
            inverse = 1.0 / jnp.sum(whole, axis=0, keepdims=True)
            shared = jnp.zeros((8, BLOCK), jnp.float32)
            for tile in tiles:
                probs = score_ref[slot, tile, head] * inverse
                prob_ref[slot, tile, head] = probs.astype(jnp.bfloat16)
                shared += row_sums(probs * grad_ref[slot, tile, head], jnp.sum)
            shared = jnp.sum(shared, axis=0, keepdims=True)
            for tile in tiles:
                probs = score_ref[slot, tile, head] * inverse
                back_ref[slot, tile, head] = (
                    probs * (grad_ref[slot, tile, head] - shared)
                ).astype(jnp.bfloat16)
        back = back_ref[slot]
        dv_ref[near, lanes] += matmul(prob_ref[slot], outs)
        dk_ref[near, lanes] += matmul(back, queries) * scale
        dq_ref[:, lanes] = pick_heads(trans_mul(back, keys), masks) * scale


def padded(cells, rows, fill=0):
    return jnp.pad(
        cells, [(0, rows - cells.shape[0])] + [(0, 0)] * (cells.ndim - 1), constant_values=fill
    )


def attend_sizes(query, keys, rim):
    steps = -(-query.shape[0] // BLOCK)
    window = BLOCK + 2 * rim if rim else keys.shape[0]
    return steps, window, (steps - 1) * BLOCK + window


def whole_spec(dims):
    return pl.BlockSpec(dims, lambda i: (0, 0))


def step_spec(columns):
    return pl.BlockSpec((BLOCK, columns), lambda i: (i, 0))


def attend(query, keys, values, query_ids, key_ids, heads, rim):
    count, columns = query.shape
    steps, window, span = attend_sizes(query, keys, rim)
    stack = 128 * heads // columns * BLOCK
    outcome = pl.pallas_call(
        functools.partial(attend_kernel, window, columns // heads),
        grid=(steps,),
        in_specs=[
            step_spec(columns),
            whole_spec((span, columns)),
            whole_spec((span, columns)),
            step_spec(1),
            whole_spec((1, span)),
        ],
        out_specs=step_spec(columns),
        out_shape=jax.ShapeDtypeStruct((steps * BLOCK, columns), jnp.bfloat16),
        scratch_shapes=[
            pltpu.VMEM((BLOCK, window), jnp.float32),
            pltpu.VMEM((2, stack, window), jnp.float32),
            pltpu.VMEM((2, stack, window), jnp.bfloat16),
        ],
        compiler_params=pltpu.CompilerParams(vmem_limit_bytes=48 << 20),
        cost_estimate=pl.CostEstimate(
            flops=4 * steps * BLOCK * window * columns,
            bytes_accessed=8 * span * columns,
            transcendentals=steps * BLOCK * window * heads,
        ),
    )(
        padded(query, steps * BLOCK),
        padded(keys, span),
        padded(values, span),
        padded(query_ids, steps * BLOCK, -4)[:, None],
        padded(key_ids, span, -5)[None, :],
    )
    return outcome[:count]


def attend_back(query, keys, values, query_ids, key_ids, heads, rim, out_grad):
    count, columns = query.shape
    steps, window, span = attend_sizes(query, keys, rim)
    stack = 128 * heads // columns * BLOCK
    dq, dk, dv = pl.pallas_call(
        functools.partial(attend_back_kernel, window, columns // heads),
        grid=(steps,),
        in_specs=[
            step_spec(columns),
            step_spec(columns),
            whole_spec((span, columns)),
            whole_spec((span, columns)),
            pl.BlockSpec((1, BLOCK), lambda i: (0, i)),
            whole_spec((span, 1)),
        ],
        out_specs=[step_spec(columns), whole_spec((span, columns)), whole_spec((span, columns))],
        out_shape=[
            jax.ShapeDtypeStruct((steps * BLOCK, columns), jnp.float32),
            jax.ShapeDtypeStruct((span, columns), jnp.float32),
            jax.ShapeDtypeStruct((span, columns), jnp.float32),
        ],
        scratch_shapes=[
            pltpu.VMEM((window, BLOCK), jnp.float32),
            pltpu.VMEM((2, window, stack), jnp.float32),
            pltpu.VMEM((2, window, stack), jnp.float32),
            pltpu.VMEM((2, window, stack), jnp.bfloat16),
            pltpu.VMEM((2, window, stack), jnp.bfloat16),
        ],
        compiler_params=pltpu.CompilerParams(vmem_limit_bytes=48 << 20),
        cost_estimate=pl.CostEstimate(
            flops=10 * steps * BLOCK * window * columns,
            bytes_accessed=20 * span * columns,
            transcendentals=steps * BLOCK * window * heads,
        ),
    )(
        padded(query, steps * BLOCK),
        padded(out_grad, steps * BLOCK),
        padded(keys, span),
        padded(values, span),
        padded(query_ids, steps * BLOCK, -4)[None, :],
        padded(key_ids, span, -5)[:, None],
    )
    return dq[:count], dk[: keys.shape[0]], dv[: keys.shape[0]]


def gelu_pair(hidden):
    below = 0.5 * (1.0 + lax.erf(hidden * math.sqrt(0.5)))
    bell = jnp.exp(-0.5 * hidden * hidden) * (1.0 / math.sqrt(2.0 * math.pi))
    return lax.optimization_barrier(
        ((hidden * below).astype(jnp.bfloat16), below + hidden * bell)
    )


def block_forward(inputs, table, heads, rim, query_ids, key_ids, share_keys):
    gains = table["norm_g"].astype(jnp.float32)
    shifts = table["norm_b"].astype(jnp.float32)
    width = inputs.shape[1]
    normed_one = layer_norm(inputs, gains[0], shifts[0]).astype(jnp.bfloat16)
    qkv = matmul(normed_one, table["qkv_w"]).astype(jnp.bfloat16)
    query = qkv[:, :width]
    all_keys, all_values = share_keys((qkv[:, width : 2 * width], qkv[:, 2 * width :]))
    attended = attend(query, all_keys, all_values, query_ids, key_ids, heads, rim)
    mixed = inputs + (matmul(attended, table["out_w"]) + table["out_b"].astype(jnp.float32))
    normed_two = layer_norm(mixed, gains[1], shifts[1]).astype(jnp.bfloat16)
    hidden = matmul(normed_two, table["up_w"]) + table["up_b"].astype(jnp.float32)
    activated, slope = gelu_pair(hidden)
    result = mixed + (matmul(activated, table["down_w"]) + table["down_b"].astype(jnp.float32))
    saved = (
        inputs,
        normed_one,
        query,
        all_keys,
        all_values,
        attended,
        mixed,
        normed_two,
        slope,
        activated,
    )
    return (result, saved)


def block_backward(
    grad_out, table, heads, rim, query_ids, key_ids, saved, return_keys, pause
):
    (
        inputs,
        normed_one,
        query,
        all_keys,
        all_values,
        attended,
        mixed,
        normed_two,
        slope,
        activated,
    ) = saved
    gains = table["norm_g"].astype(jnp.float32)
    shifts = table["norm_b"].astype(jnp.float32)
    pairs = {}
    down_grad = grad_out.astype(jnp.bfloat16)
    pairs["down_w"] = (activated, down_grad)
    act_grad = mul_trans(down_grad, table["down_w"])
    hidden_grad = (act_grad * slope).astype(jnp.bfloat16)
    pairs["up_w"] = (normed_two, hidden_grad)
    hidden_grad = pause(hidden_grad)
    mixed_part, gain_two, shift_two = norm_back(
        mixed, gains[1], shifts[1], mul_trans(hidden_grad, table["up_w"])
    )
    mixed_grad = grad_out + mixed_part
    branch_grad = mixed_grad.astype(jnp.bfloat16)
    pairs["out_w"] = (attended, branch_grad)
    attended_grad = mul_trans(branch_grad, table["out_w"]).astype(jnp.bfloat16)
    query_grad, keys_grad_all, values_grad_all = attend_back(
        query, all_keys, all_values, query_ids, key_ids, heads, rim, attended_grad
    )
    keys_grad, values_grad = return_keys((keys_grad_all, values_grad_all))
    qkv_grad = jnp.concatenate([query_grad, keys_grad, values_grad], axis=1).astype(jnp.bfloat16)
    pairs["qkv_w"] = (normed_one, qkv_grad)
    input_part, gain_one, shift_one = norm_back(
        inputs, gains[0], shifts[0], mul_trans(qkv_grad, table["qkv_w"])
    )
    return (mixed_grad + input_part, (gain_one, shift_one, gain_two, shift_two), pairs)


def core_side():
    return (lax.axis_index("grp") % 2).astype(jnp.int32).reshape(1)


def store_vector(target, first, lane, vector):
    width = vector.shape[1]
    done = 0
    while done < width:
        size = min(128 - lane, width - done)
        target[first : first + 1, lane : lane + size] = vector[:, done : done + size]
        done += size
        lane += size
        first, lane = first + lane // 128, lane % 128
    return first, lane


def column_sums(ref):
    return jnp.sum(ref[...].astype(jnp.float32), axis=0, keepdims=True)


def store_flat(target, product):
    rows, blocks = product.shape[0], product.shape[1] // 128
    for index in range(blocks):
        target[pl.ds(index, rows, stride=blocks), :] = product[:, index * 128 : (index + 1) * 128]


def column_blocks(ref, blocks):
    parts = [ref[:, pl.ds(pl.multiple_of(index * 128, 128), 128)] for index in blocks]
    return parts[0] if len(parts) == 1 else jnp.concatenate(parts, axis=1)


def steps_of(rows, size):
    return [(start, min(size, rows - start)) for start in range(0, rows, size)]


def enc_grad_kernel(sizes, places, place_ref, x_ref, *refs):
    norm_ref, out_ref, stage_ref, product_ref, small_ref, quarter_ref, sems = refs[-7:]
    side, far = place_ref[0], place_ref[1]
    offset = 0
    flight = [None, None]
    turn = 0

    def settle():
        if flight[turn % 2] is not None:
            flight[turn % 2].wait()

    for index, size in enumerate(sizes):
        y_ref = refs[index]
        blocks = y_ref.shape[1] // 256
        first, depth = places[index]
        if blocks % 2:
            columns = [2 * block + side for block in range(blocks)]
        else:
            columns = [4 * block + 2 * far + side for block in range(blocks // 2)]
        right = column_blocks(y_ref, columns)
        for start, rows in steps_of(depth, size):
            settle()
            target = stage_ref.at[turn % 2]
            product = trans_mul(x_ref[:, first + start : first + start + rows], right)
            if blocks % 2 == 0:
                store_flat(target, product)
            else:
                for block in range(blocks):
                    product_ref[block, :rows] = product[:, block * 128 : (block + 1) * 128]
                    odd = (far + block) % 2
                    target[
                        pl.ds((odd * blocks + block - far) // 2, rows // 2, stride=blocks), :
                    ] = product_ref.at[block][pl.ds(odd, rows // 2, stride=2), :]
            amount = rows * blocks // 2
            copy = pltpu.make_async_copy(
                target.at[pl.ds(0, amount)], out_ref.at[pl.ds(offset, amount)], sems.at[turn % 2]
            )
            copy.start()
            flight[turn % 2] = copy
            turn += 1
            offset += amount
    small_ref[...] = jnp.zeros_like(small_ref)
    spot = 0, 0
    for index in (0, 2, 3, 4):
        spot = store_vector(small_ref, *spot, column_sums(refs[index]))
    rows = norm_ref.shape[0] // 4
    norms = sum(norm_ref[index * rows : (index + 1) * rows] for index in range(4))
    for index in range(rows):
        spot = store_vector(small_ref, *spot, norms[index : index + 1])
    rows = quarter_ref.shape[0]
    quarter_ref[...] = small_ref[pl.ds(side + 2 * far, rows, stride=4), :]
    last = pltpu.make_async_copy(quarter_ref, out_ref.at[pl.ds(offset, rows)], sems.at[2])
    last.start()
    for copy in [last] + flight:
        copy.wait()


def member_place():
    place = lax.axis_index("grp").astype(jnp.int32)
    return jnp.stack([place % 2, place // 2])


def enc_grad_quarter(inputs, places, grads, norms, total_rows):
    sizes = [640, 256, 384, 256, 768]
    whole = pl.BlockSpec(memory_space=pltpu.VMEM)
    return pl.pallas_call(
        functools.partial(enc_grad_kernel, sizes, places),
        in_specs=[pl.BlockSpec(memory_space=pltpu.SMEM)] + [whole] * (len(grads) + 2),
        out_specs=pl.BlockSpec(memory_space=pl.ANY),
        out_shape=jax.ShapeDtypeStruct((total_rows // 4, 128), jnp.float32),
        scratch_shapes=[
            pltpu.VMEM((2, 1536, 128), jnp.float32),
            pltpu.VMEM((9, 768, 128), jnp.float32),
            pltpu.VMEM((384, 128), jnp.float32),
            pltpu.VMEM((96, 128), jnp.float32),
            pltpu.SemaphoreType.DMA((3,)),
        ],
        compiler_params=pltpu.CompilerParams(vmem_limit_bytes=48 << 20),
        cost_estimate=pl.CostEstimate(
            flops=total_rows * 128 * inputs.shape[0],
            bytes_accessed=total_rows * 128,
            transcendentals=0,
        ),
    )(member_place(), inputs, *grads, norms)


def store_pixels(product_ref, targets):
    groups = product_ref.shape[1] // 4

    def load(row, block):
        return product_ref.at[block][pl.ds(row, groups, stride=4), :]

    def piece(row, block):
        if block < 13:
            return load(row, block)
        if block == 13:
            left, right = load(row, 13)[:, :64], load(row + 1, 0)[:, :64]
        else:
            left, right = load(row + 1, block - 14)[:, 64:], load(row + 1, block - 13)[:, :64]
        return jnp.concatenate([left, right], axis=1)

    for index in range(54):
        block = piece(0, index) if index < 27 else piece(2, index - 27)
        targets[index % 2][pl.ds(index // 2, groups, stride=27), :] = block


def dec_grad_kernel(plan, side_ref, *refs):
    norm_ref, mine_ref, theirs_ref, stage_ref, pixel_ref, small_ref, halves_ref, sems = refs[-8:]
    side = side_ref[0]
    flight = [None, None]
    turn = 0
    for index, (size, offset) in enumerate(plan):
        x_ref, y_ref = refs[2 * index], refs[2 * index + 1]
        pixels = y_ref.shape[1] % 256 != 0
        for start, rows in steps_of(x_ref.shape[1], size):
            product = trans_mul(x_ref[:, start : start + rows], y_ref[...])
            slot = turn % 2
            for copy in flight[slot] or ():
                copy.wait()
            if pixels:
                for block in range(14):
                    part = product[:, block * 128 : (block + 1) * 128]
                    pixel_ref[block, :, : part.shape[1]] = part
                store_pixels(pixel_ref, [stage_ref.at[slot, 0], stage_ref.at[slot, 1]])
            else:
                blocks = y_ref.shape[1] // 128
                for block in range(blocks):
                    stage_ref.at[slot, block % 2][
                        pl.ds(block // 2, rows, stride=blocks // 2), :
                    ] = product[:, block * 128 : (block + 1) * 128]
            amount = rows * y_ref.shape[1] // 256
            flight[slot] = [
                pltpu.make_async_copy(
                    stage_ref.at[slot, parity, pl.ds(0, amount)],
                    target.at[pl.ds(offset, amount)],
                    sems.at[slot, order],
                )
                for order, (parity, target) in enumerate(
                    ((side, mine_ref), (1 - side, theirs_ref))
                )
            ]
            for copy in flight[slot]:
                copy.start()
            offset += amount
            turn += 1
    small_ref[...] = jnp.zeros_like(small_ref)
    spot = store_vector(small_ref, 0, 0, column_sums(refs[1]))
    spot = store_vector(small_ref, *spot, norm_ref[0:1])
    for index in (2, 3, 4, 5):
        spot = store_vector(small_ref, *spot, column_sums(refs[2 * index + 1]))
    for index in range(1, norm_ref.shape[0]):
        spot = store_vector(small_ref, *spot, norm_ref[index : index + 1])
    rows = halves_ref.shape[1]
    for parity in range(2):
        halves_ref[parity] = small_ref[pl.ds(parity, rows, stride=2), :]
    last = [
        pltpu.make_async_copy(
            halves_ref.at[parity], target.at[pl.ds(target.shape[0] - rows, rows)], sems.at[2, order]
        )
        for order, (parity, target) in enumerate(((side, mine_ref), (1 - side, theirs_ref)))
    ]
    for copy in last:
        copy.start()
    for copy in last + flight[0] + flight[1]:
        copy.wait()


def dec_grad_halves(pairs, norms, total_rows):
    plan = [(256, 0), (256, 1536), (256, 4608), (256, 5632), (512, 9728), (512, 13824)]
    operands = [part for pair in pairs for part in pair]
    whole = pl.BlockSpec(memory_space=pltpu.VMEM)
    anywhere = pl.BlockSpec(memory_space=pl.ANY)
    shape = jax.ShapeDtypeStruct((total_rows // 2, 128), jnp.float32)
    return pl.pallas_call(
        functools.partial(dec_grad_kernel, plan),
        in_specs=[pl.BlockSpec(memory_space=pltpu.SMEM)] + [whole] * (len(operands) + 1),
        out_specs=[anywhere, anywhere],
        out_shape=[shape, shape],
        scratch_shapes=[
            pltpu.VMEM((2, 2, 3456, 128), jnp.float32),
            pltpu.VMEM((14, 512, 128), jnp.float32),
            pltpu.VMEM((256, 128), jnp.float32),
            pltpu.VMEM((2, 128, 128), jnp.float32),
            pltpu.SemaphoreType.DMA((3, 2)),
        ],
        compiler_params=pltpu.CompilerParams(vmem_limit_bytes=56 << 20),
        cost_estimate=pl.CostEstimate(
            flops=total_rows * 256 * pairs[1][0].shape[0],
            bytes_accessed=total_rows * 512,
            transcendentals=0,
        ),
    )(core_side(), *operands, norms)


def adamw_kernel(parts, with_average, place_ref, scalar_ref, *refs):
    count = 4 if with_average else 3
    ins, outs, grad_ref = refs[parts : parts + count], refs[parts + count : -1], refs[-1]
    for index in range(parts):
        rows = refs[index].shape[0]
        grad_ref[pl.ds(place_ref[index], rows, stride=parts), :] = refs[index][...]
    weights = ins[0][...]
    clipped = grad_ref[...] * scalar_ref[0]
    first_new = BETA_ONE * ins[1][...] + (1.0 - BETA_ONE) * clipped
    second_new = BETA_TWO * ins[2][...] + (1.0 - BETA_TWO) * clipped * clipped
    first_hat = first_new / scalar_ref[1]
    second_hat = second_new / scalar_ref[2]
    weights_new = weights * (1.0 - LEARN_RATE * WEIGHT_DECAY) - LEARN_RATE * first_hat / (
        jnp.sqrt(second_hat) + ADAM_EPS
    )
    outs[0][...] = weights_new
    outs[1][...] = first_new
    outs[2][...] = second_new
    outs[3][...] = weights_new.astype(jnp.bfloat16)
    if with_average:
        outs[4][...] = EMA_RATE * ins[3][...] + (1.0 - EMA_RATE) * weights_new


def adamw(parts, arrays, factor, steps_done):
    count = len(parts)
    place = lax.axis_index("grp")
    places = jnp.stack([(place ^ index) % count for index in range(count)])
    rows = arrays[0].shape[0]
    steps = 1
    for split in (2, 3, 4, 6, 8):
        if rows % (split * 8 * count) == 0:
            steps = split
    block = pl.BlockSpec((rows // steps, 128), lambda i: (i, 0))
    share = pl.BlockSpec((rows // steps // count, 128), lambda i: (i, 0))
    scalar = pl.BlockSpec(memory_space=pltpu.SMEM)
    scalars = jnp.stack([factor, 1.0 - BETA_ONE**steps_done, 1.0 - BETA_TWO**steps_done])
    full = jax.ShapeDtypeStruct((rows, 128), jnp.float32)
    shapes = [full, full, full, jax.ShapeDtypeStruct((rows, 128), jnp.bfloat16)]
    if len(arrays) == 4:
        shapes.append(full)
    return pl.pallas_call(
        functools.partial(adamw_kernel, count, len(arrays) == 4),
        grid=(steps,),
        in_specs=[scalar, scalar] + [share] * count + [block] * len(arrays),
        out_specs=[block] * len(shapes),
        out_shape=shapes,
        scratch_shapes=[pltpu.VMEM((rows // steps, 128), jnp.float32)],
        compiler_params=pltpu.CompilerParams(vmem_limit_bytes=40 << 20),
    )(places.astype(jnp.int32), scalars, *parts, *arrays)


def per_device(
    patches,
    segments,
    visible,
    enc_params,
    enc_first,
    enc_second,
    enc_average,
    dec_params,
    dec_first,
    dec_second,
    step_count,
):
    my_index = lax.axis_index("grp")
    slot_dev = segments.shape[0]
    rim = TILE_HI
    counts = jnp.sum((segments >= 0).astype(jnp.float32)) - visible.shape[0]
    total_count = total(jnp.full((8, 128), counts))[0, 0]
    enc_copy = gather_quarters(enc_params.astype(jnp.bfloat16))
    group_vis = group_rows(visible)
    group_seg = double(double(segments, 0, "grp", 2), 1, "grp", 1).reshape(-1)
    group_ids = group_seg[group_vis]
    key_ids = extended(segments + 3, rim) - 3
    local_slot = group_vis - my_index * slot_dev
    chosen = (
        local_slot[:, None] == jnp.arange(slot_dev, dtype=jnp.int32)[None, :]
    ).astype(jnp.bfloat16)
    seen = jnp.sum(chosen.astype(jnp.float32), axis=0) > 0.5
    enc_input = own_rows(matmul(chosen, patches).astype(jnp.bfloat16))
    enc_waves = sincos(visible % L, D)
    positions = (my_index * slot_dev + jnp.arange(slot_dev, dtype=jnp.int32)) % L
    dec_waves = sincos(positions, E)
    pixels = patches.astype(jnp.float32)
    pixel_mean = jnp.mean(pixels, axis=1, keepdims=True)
    centered = pixels - pixel_mean
    pixel_rate = lax.rsqrt(jnp.mean(centered * centered, axis=1, keepdims=True) + NORM_EPS)
    (
        enc_copy,
        enc_input,
        enc_waves,
        dec_waves,
        pixel_mean,
        pixel_rate,
        seen,
        group_ids,
        key_ids,
        chosen,
        total_count,
    ) = lax.optimization_barrier(
        (
            enc_copy,
            enc_input,
            enc_waves,
            dec_waves,
            pixel_mean,
            pixel_rate,
            seen,
            group_ids,
            key_ids,
            chosen,
            total_count,
        )
    )
    own_ids = group_ids[: visible.shape[0]]
    enc_copy, dec_shard = lax.optimization_barrier((enc_copy, dec_params))
    dec_copy = gather_quarters(dec_shard.astype(jnp.bfloat16))
    enc_table = unpack(enc_copy, enc_pieces(), ENC_STEPS)
    dec_table = unpack(dec_copy, dec_pieces(), DEC_STEPS)
    enc_start = (
        matmul(enc_input, enc_table["patch_w"])
        + enc_table["patch_b"].astype(jnp.float32)
        + enc_waves
    )

    def enc_share(pair):
        joined = group_rows(jnp.concatenate(pair, axis=1))
        return (joined[:, :D], joined[:, D:])

    enc_out, enc_saved = block_forward(enc_start, enc_table, H, 0, own_ids, group_ids, enc_share)
    enc_gain = enc_table["norm_g"].astype(jnp.float32)
    enc_shift = enc_table["norm_b"].astype(jnp.float32)
    enc_final = layer_norm(enc_out, enc_gain[2], enc_shift[2]).astype(jnp.bfloat16)
    latent = (
        matmul(enc_final, dec_table["embed_w"]) + dec_table["embed_b"].astype(jnp.float32)
    ).astype(jnp.bfloat16)
    group_latent = group_rows(latent)
    enc_inputs = jnp.concatenate(
        [enc_saved[1], enc_saved[5], enc_saved[7], enc_saved[9], enc_input], axis=1
    )
    group_latent, enc_inputs = lax.optimization_barrier((group_latent, enc_inputs))
    group_inputs = group_rows(enc_inputs)
    placed = trans_mul(chosen, group_latent)
    dec_start = jnp.where(
        seen[:, None], placed, dec_table["mask_token"].astype(jnp.float32)[None, :]
    ) + dec_waves
    counted = jnp.where((segments >= 0) & jnp.logical_not(seen), 1.0, 0.0)

    def dec_share(pair):
        joined = extended(jnp.concatenate(pair, axis=1), rim)
        return (joined[:, :E], joined[:, E:])

    def dec_return(pair):
        joined = jnp.concatenate(pair, axis=1)
        from_upper = passed_along(joined[:rim], "grp", -1)
        from_lower = passed_along(joined[rim + slot_dev :], "grp", 1)
        middle = joined[rim : rim + slot_dev]
        middle = jnp.concatenate(
            [
                middle[:rim] + from_lower,
                middle[rim : slot_dev - rim],
                middle[slot_dev - rim :] + from_upper,
            ],
            axis=0,
        )
        return (middle[:, :E], middle[:, E:])

    dec_out, dec_saved = block_forward(
        dec_start, dec_table, EH, rim, segments, key_ids, dec_share
    )
    dec_gain = dec_table["norm_g"].astype(jnp.float32)
    dec_shift = dec_table["norm_b"].astype(jnp.float32)
    dec_final = layer_norm(dec_out, dec_gain[2], dec_shift[2]).astype(jnp.bfloat16)
    predicted = matmul(dec_final, dec_table["pix_w"]) + dec_table["pix_b"].astype(jnp.float32)
    target = (patches.astype(jnp.float32) - pixel_mean) * pixel_rate
    errors = predicted - target
    loss_part = jnp.sum(counted * jnp.mean(errors * errors, axis=1))
    errors, group_inputs = lax.optimization_barrier((errors, group_inputs))
    pred_grad = (counted[:, None] * errors * (2.0 / PATCH) / total_count).astype(jnp.bfloat16)
    dec_out_grad, dec_gain_last, dec_shift_last = norm_back(
        dec_out, dec_gain[2], dec_shift[2], mul_trans(pred_grad, dec_table["pix_w"])
    )
    start_grad, dec_small, dec_pairs = block_backward(
        dec_out_grad, dec_table, EH, rim, segments, key_ids, dec_saved, dec_return, lambda grad: grad
    )
    mask_grad = jnp.sum(jnp.where(seen[:, None], 0.0, start_grad), axis=0)
    latent_grad = own_rows(matmul(chosen, start_grad.astype(jnp.bfloat16)).astype(jnp.bfloat16))
    dec_pairs["embed_w"] = (enc_final, latent_grad)
    dec_pairs["pix_w"] = (dec_final, pred_grad)
    mine, theirs = dec_grad_halves(
        [dec_pairs[name] for name in ("embed_w", "qkv_w", "out_w", "up_w", "down_w", "pix_w")],
        jnp.stack(
            [
                mask_grad,
                dec_small[0],
                dec_small[2],
                dec_gain_last,
                dec_small[1],
                dec_small[3],
                dec_shift_last,
            ]
        ),
        DR,
    )
    arrived = swap(theirs, "grp", 1)
    latent_grad, mine = lax.optimization_barrier((latent_grad, mine))
    dec_blocks = None

    def enc_pause(grad):
        nonlocal dec_blocks
        grad, dec_half = lax.optimization_barrier((grad, mine + arrived))
        dec_blocks = reduce_first(dec_half, dec_routes(), (0.5,))
        return grad

    enc_out_grad, enc_gain_last, enc_shift_last = norm_back(
        enc_out, enc_gain[2], enc_shift[2], mul_trans(latent_grad, dec_table["embed_w"])
    )
    def enc_return(pair):
        nonlocal dec_blocks
        joined = own_rows(jnp.concatenate(pair, axis=1))
        joined, dec_blocks = lax.optimization_barrier((joined, dec_blocks))
        return (joined[:, :D], joined[:, D:])

    enc_start_grad, enc_small, enc_pairs = block_backward(
        enc_out_grad, enc_table, H, 0, own_ids, group_ids, enc_saved, enc_return, enc_pause
    )
    enc_norms = jnp.stack(
        [
            enc_small[0],
            enc_small[2],
            enc_gain_last,
            enc_small[1],
            enc_small[3],
            enc_shift_last,
            jnp.zeros_like(enc_shift_last),
            jnp.zeros_like(enc_shift_last),
        ]
    )
    enc_pairs["patch_w"] = (enc_input, enc_start_grad.astype(jnp.bfloat16))
    names = ("patch_w", "qkv_w", "out_w", "up_w", "down_w")
    places = [(3 * D + F, PATCH), (0, D), (D, D), (2 * D, D), (3 * D, F)]
    enc_quarter = enc_grad_quarter(
        group_inputs,
        places,
        [group_rows(enc_pairs[name][1]) for name in names],
        group_rows(enc_norms),
        ER,
    )
    enc_blocks = reduce_first(enc_quarter, dp_routes(), (0.5,))
    enc_sum = reduce_rest(enc_blocks, dp_routes())
    dec_sum = reduce_rest(dec_blocks, dec_routes())
    squares = sum(jnp.sum(part * part) for part in enc_sum + dec_sum)
    lane = lax.broadcasted_iota(jnp.int32, (8, 128), 1)
    enc_own = jnp.concatenate(enc_sum, axis=0)
    enc_across = swap(enc_own, "grp", 2)
    sums = total(jnp.where(lane == 0, squares, jnp.where(lane == 1, loss_part, 0.0)))
    enc_across, sums = lax.optimization_barrier((enc_across, sums))
    enc_quarters = (
        enc_own,
        swap(enc_own, "grp", 1),
        enc_across,
        swap(enc_across, "grp", 1),
    )
    loss_total = sums[0, 1]
    grad_norm = jnp.sqrt(sums[0, 0])
    factor = jnp.minimum(1.0, CLIP_LIMIT / (grad_norm + NORM_EPS))
    steps_done = step_count[0].astype(jnp.float32)
    enc_new, enc_first_new, enc_second_new, enc_copy_new, average_new = adamw(
        enc_quarters, (enc_params, enc_first, enc_second, enc_average), factor, steps_done
    )
    dec_new, dec_first_new, dec_second_new, dec_copy_new = adamw(
        spread_pieces(dec_sum), (dec_params, dec_first, dec_second), factor, steps_done
    )
    return (
        enc_new,
        enc_first_new,
        enc_second_new,
        enc_copy_new,
        dec_new,
        dec_first_new,
        dec_second_new,
        dec_copy_new,
        average_new,
        grad_norm,
        loss_total,
        total_count,
    )


def solution(mesh):
    placed = (
        P(("dp", "grp"), None),
        P(("dp", "grp")),
        P(("dp", "grp")),
        P("dp", None),
        P("dp", None),
        P("dp", None),
        P("dp", None),
        P("dp", None),
        P("dp", None),
        P("dp", None),
        P(),
    )
    return jax.shard_map(
        per_device,
        mesh=mesh,
        in_specs=placed,
        out_specs=(
            P("dp", None),
            P("dp", None),
            P("dp", None),
            P("dp", None),
            P("dp", None),
            P("dp", None),
            P("dp", None),
            P("dp", None),
            P("dp", None),
            P(),
            P(),
            P(),
        ),
        check_vma=False,
    )
```

time: 965 us -> 823 us (0.85)
  local copies, waits for them, and re-layouts: 144 us -> 83.3 us
  starting transfers between devices: 126 us -> 74.3 us
  waiting for transfers between devices: 369 us -> 342 us
  matrix products: 71.4 us -> 54.3 us
  between operations: 11.6 us -> 22.5 us
    ppermute x125 -> x69, waiting for transfers between devices: 358 us -> 246 us  [swap(): return lax.ppermute(block, axis, [(i, i ^ bit) for i in range(count)])]
    all_gather x0 -> x2, waiting for transfers between devices: none -> 86.6 us  [gather_quarters(): return lax.all_gather(quarter, ('dp', 'grp'), axis=0, tiled=True)]
    ppermute x125 -> x69, starting transfers between devices: 117 us -> 61.4 us  [swap(): return lax.ppermute(block, axis, [(i, i ^ bit) for i in range(count)])]
    reshape x11 -> x1, local copies, waits for them, and re-layouts: 46.8 us -> 4.16 us  [unpack(): table[piece_name] = rows[offset:offset + amount].reshape(piece_dims)]
    slice x9 -> x1, local copies, waits for them, and re-layouts: 26.4 us -> 2.8 us  [unpack(): table[piece_name] = rows[offset:offset + amount].reshape(piece_dims)]
    dot_general x13, matrix products: 41.2 us -> 24.8 us  [matmul(): return jnp.dot(left, right, preferred_element_type=jnp.float32)]
    concatenate x1 -> x8, other arithmetic: 1.22 us -> 17.1 us  [group_rows(): return jnp.concatenate([block, near, across, far], axis=0)]
    pallas_call x9 -> x5, Pallas kernels: 56.6 us -> 60.7 us  [the longest x2 27.7 us: relayout(): pl.pallas_call(functools.partial(relayout_kernel, plan), in_specs=[anywhe...]
  transfers between devices with their start and end apart: 131 -> 77, of which waited for: 55 -> 36; matrix products, arithmetic and copies ran while one was open for 21% -> 18% of each run, Pallas kernels for 5% -> 7%
where the time goes in v2:
time: 823 us; the launch traced here: 814 us
  waiting for transfers between devices  342 us (42%)
  Pallas kernels  141 us (17%)
  other arithmetic  97.2 us (12%)
  local copies, waits for them, and re-layouts  83.3 us (10%)
  starting transfers between devices  74.3 us (9%)
  matrix products  54.3 us (7%)
  between operations  22.5 us (3%)
    ppermute x69, waiting for transfers between devices, swap(): return lax.ppermute(block, axis, [(i, i ^ bit) for i in range(count)])  246 us
    all_gather x2, waiting for transfers between devices, gather_quarters(): return lax.all_gather(quarter, ('dp', 'grp'), axis=0, tiled=True)  86.6 us
    ppermute x69, starting transfers between devices, swap(): return lax.ppermute(block, axis, [(i, i ^ bit) for i in range(count)])  61.4 us
    pallas_call x2, Pallas kernels, attend_back(): pl.pallas_call(functools.partial(attend_back_kernel, window, columns // h...  38 us
    unnamed x281, local copies, waits for them, and re-layouts  29.6 us
    pallas_call x2, Pallas kernels, relayout(): pl.pallas_call(functools.partial(relayout_kernel, plan), in_specs=[anywhe...  27.7 us
    dot_general x10, matrix products, mul_trans(): lax.dot_general(left, right, (((1,), (1,)), ((), ())), preferred_element_...  27.2 us
    pallas_call x1, Pallas kernels, dec_grad_halves(): pl.pallas_call(functools.partial(dec_grad_kernel, plan), in_specs=[pl.Blo...  24.8 us
  transfers between devices with their start and end apart: 77, of which 36 were waited for; matrix products, arithmetic and copies ran while one was open for 18% of the time, Pallas kernels for 7%

profile of v2, /device:TPU:0, one launch (start us, length us, event | category | flops | bytes accessed | tf_op | source)
XLA Modules:
  0.0 814.1 jit_solution(7961168822344971198)
XLA Ops:
  34.6 3.6 collective-permute-start.7
  55.8 10.2 %collective-permute-done.4 = bf16[96,1728]{1,0:T(8,128)(2,1)S(1)} collective-permute-done((bf16[96,1728]{1,0:T(8,128)(2,1)S(1)}, bf16[96,1728]{1,0:T(8,128)(2,1)S(1)}, u32[]{:S(2)}, u32[]{:S(2)}) %collective-permute-start.4) | collective-permute-done | bytes 331808 | tf_op jit(solution)/shard_map/ppermute | solution.py:37
  67.7 69.3 %all-gather.3.cloned.1.call-done.refs_0_ = bf16[66048,128]{1,0:T(8,128)(2,1)} async-done(((bf16[2064,128]{1,0:T(8,128)(2,1)}), bf16[66048,128]{1,0:T(8,128)(2,1)}) %all-gather.3.cloned.1.call-update) | async-done | bytes 16908304 | tf_op jit(solution)/shard_map/all_gather | solution.py:77
  138.9 18.7 %shard_map.202 = (bf16[1728,768]{1,0:T(8,128)(2,1)S(1)}, bf16[768,2304]{1,0:T(8,128)(2,1)S(1)}, bf16[768,768]{1,0:T(8,128)(2,1)S(1)}, bf16[768,3072]{1,0:T(8,128)(2,1)S(1)}, bf16[3072,768]{1,0:T(8,128)(2,1)}) custom-call(bf16[66048,128]{1,0:T(8,128)(2,1)} %all-gather.3.cloned.1.call-done.refs_0_), custom_call_target="tpu_custom_call" | custom-call | bytes 33816576 | tf_op jit(solution)/shard_map/pallas_call | solution.py:276
  169.8 11.8 %collective-permute-done.15 = bf16[96,1536]{1,0:T(8,128)(2,1)} collective-permute-done((bf16[96,1536]{1,0:T(8,128)(2,1)}, bf16[96,1536]{1,0:T(8,128)(2,1)}, u32[]{:S(2)}, u32[]{:S(2)}) %collective-permute-start.15) | collective-permute-done | bytes 294944 | tf_op jit(solution)/shard_map/ppermute | solution.py:37
  197.5 4.8 fusion.15
  207.5 17.2 %all-gather.5.cloned.1.call-done.refs_0_ = bf16[34816,128]{1,0:T(8,128)(2,1)} async-done(((bf16[1088,128]{1,0:T(8,128)(2,1)}), bf16[34816,128]{1,0:T(8,128)(2,1)}) %all-gather.5.cloned.1.call-update) | async-done | bytes 8912912 | tf_op jit(solution)/shard_map/all_gather | solution.py:77
  226.1 9.1 %shard_map.204 = (bf16[768,512]{1,0:T(8,128)(2,1)S(1)}, bf16[512,1536]{1,0:T(8,128)(2,1)S(1)}, bf16[512,512]{1,0:T(8,128)(2,1)S(1)}, bf16[512,2048]{1,0:T(8,128)(2,1)S(1)}, bf16[2048,512]{1,0:T(8,128)(2,1)S(1)}) custom-call(bf16[34816,128]{1,0:T(8,128)(2,1)} %all-gather.5.cloned.1.call-done.refs_0_), custom_call_target="tpu_custom_call" | custom-call | bytes 17825792 | tf_op jit(solution)/shard_map/pallas_call | solution.py:276
  249.5 4.2 reshape.622
  270.8 14.7 %shard_map.205 = bf16[896,512]{1,0:T(8,128)(2,1)S(1)} custom-call(bf16[896,512]{1,0:T(8,128)(2,1)S(1)} %pad.42.q_ref.refs_0_, bf16[1280,512]{1,0:T(8,128)(2,1)S(1)} %pad.43.k_ref.refs_2_, bf16[1280,512]{1,0:T(8,128)(2,1)S(1)} %pad.44.v_ref.refs_3_, s32[896,1]{1,0:T(8,128)S(1)} %copy-done.22, s32[1,1280]{1,0:T(1,128)S(1)} %broadcast_in_dim.91.kid_ref), custom_call_target="tpu_custom_call" | custom-call | flops 939524096 | bytes 5242880 | tf_op jit(solution)/shard_map/pallas_call | solution.py:493
  288.2 4.9 fusion.3
  295.7 7.0 collective-permute-done.23
  303.2 4.7 multiply_reduce_fusion
  308.5 6.0 pad_maximum_fusion.x_ref
  314.5 5.8 divide_convert_fusion.refs_11_
  320.3 4.7 multiply_reduce_fusion.1
  326.1 3.8 multiply_convert_fusion.refs_7_
  329.9 5.0 multiply_reduce_fusion.2
  338.1 34.6 %shard_map.206 = (f32[896,512]{1,0:T(8,128)}, f32[1280,512]{1,0:T(8,128)}, f32[1280,512]{1,0:T(8,128)}) custom-call(bf16[896,512]{1,0:T(8,128)(2,1)S(1)} %pad.42.q_ref.refs_0_, bf16[896,512]{1,0:T(8,128)(2,1)S(1)} %pad.47.refs_1_, bf16[1280,512]{1,0:T(8,128)(2,1)S(1)} %pad.43.k_ref.refs_2_, bf16[1280,512]{1,0:T(8,128)(2,1)S(1)} %pad.44.v_ref.refs_3_, ...), custom_call_target="tpu_custom_call" | custom-call | flops 2348810240 | bytes 13107200 | tf_op jit(solution)/shard_map/pallas_call | solution.py:530
  383.5 7.7 collective-permute-done.26
  391.3 3.8 maximum_maximum_fusion.refs_3_
  399.4 10.4 %collective-permute-start.27 = (bf16[192,512]{1,0:T(8,128)(2,1)S(1)}, bf16[192,512]{1,0:T(8,128)(2,1)S(1)}, u32[]{:S(2)}, u32[]{:S(2)}) collective-permute-start(bf16[192,512]{1,0:T(8,128)(2,1)S(1)} %pad_maximum_fusion.19), channel_id=1, source_target_pairs={{0,1},{1,0},{2,3},{3,2},{4,5},{5,4},{6,7},{7,6},{8,9},{9,8},{10,11... | collective-permute-start | bytes 589832 | tf_op jit(solution)/shard_map/ppermute | solution.py:37
  413.5 3.5 collective-permute-done.28
  418.7 24.8 %shard_map.207 = (f32[17408,128]{1,0:T(8,128)}, f32[17408,128]{1,0:T(8,128)}) custom-call(s32[1]{0:T(128)} %bitcast.4.side_ref, bf16[96,768]{1,0:T(8,128)(2,1)} %add_convert_fusion.5.refs_0_, bf16[96,512]{1,0:T(8,128)(2,1)} %fusion.32.refs_1_, bf16[864,512]{1,0:T(8,128)(2,1)} %copy-done.68, bf16[864,1536]{1,0:T(8,128)(2,1)} %copy-done.56, ...), custom_call_target="tpu_custom_call" | custom-call | flops 7700742144 | bytes 17825792 | tf_op jit(solution)/shard_map/pallas_call | solution.py:859
  445.8 4.5 fusion.8
  450.4 7.3 collective-permute-done.29
  457.7 3.9 add.623
  466.5 3.4 shard_map.208
  485.1 22.4 %collective-permute-done.47 = bf16[96,768]{1,0:T(8,128)(2,1)} collective-permute-done((bf16[96,768]{1,0:T(8,128)(2,1)S(1)}, bf16[96,768]{1,0:T(8,128)(2,1)}, u32[]{:S(2)}, u32[]{:S(2)}) %collective-permute-start.47) | collective-permute-done | bytes 147488 | tf_op jit(solution)/shard_map/ppermute | solution.py:37
  516.6 4.4 collective-permute-done.41
  521.0 5.8 collective-permute-done.32
  526.8 3.9 dynamic-slice_add_fusion.1
  530.7 3.9 dynamic-slice_add_fusion
  544.3 6.0 collective-permute-done.38
  564.4 14.3 %shard_map.209 = f32[16512,128]{1,0:T(8,128)} custom-call(s32[2]{0:T(128)S(1)} %pad_add_fusion.3.place_ref, bf16[384,7104]{1,0:T(8,128)(2,1)} %pad_maximum_fusion.x_ref, bf16[384,768]{1,0:T(8,128)(2,1)S(1)} %pad_maximum_fusion.11.refs_0_, bf16[384,2304]{1,0:T(8,128)(2,1)S(1)} %pad_maximum_fusion.4.refs_1_, bf16[384,768]{1,0:T(8,128)(2,1)S(1)} %pad_maximum_fusion.12.refs_2_, ...), custom_call_target="tpu_custom_call" | custom-call | flops 3246391296 | bytes 8454144 | tf_op jit(solution)/shard_map/pallas_call | solution.py:751
  582.0 3.2 constant_dynamic-slice_fusion.8
  590.2 19.0 %collective-permute-done.59 = f32[2,2,1,544,128]{4,3,2,1,0:T(8,128)} collective-permute-done((f32[2,2,1,544,128]{4,3,2,1,0:T(8,128)}, f32[2,2,1,544,128]{4,3,2,1,0:T(8,128)}, u32[]{:S(2)}, u32[]{:S(2)}) %collective-permute-start.59) | collective-permute-done | bytes 1114144 | tf_op jit(solution)/shard_map/ppermute | solution.py:37
  613.0 32.8 %collective-permute-done.63 = f32[1,1,2,544,128]{4,3,2,1,0:T(8,128)S(1)} collective-permute-done((f32[1,1,2,544,128]{4,3,2,1,0:T(8,128)}, f32[1,1,2,544,128]{4,3,2,1,0:T(8,128)S(1)}, u32[]{:S(2)}, u32[]{:S(2)}) %collective-permute-start.63) | collective-permute-done | bytes 557088 | tf_op jit(solution)/shard_map/ppermute | solution.py:37
  647.8 9.3 %collective-permute-done.60 = f32[2,1,1,544,128]{4,3,2,1,0:T(8,128)S(1)} collective-permute-done((f32[2,1,1,544,128]{4,3,2,1,0:T(8,128)}, f32[2,1,1,544,128]{4,3,2,1,0:T(8,128)S(1)}, u32[]{:S(2)}, u32[]{:S(2)}) %collective-permute-start.60) | collective-permute-done | bytes 557088 | tf_op jit(solution)/shard_map/ppermute | solution.py:37
  669.1 3.5 collective-permute-done.61
  674.8 32.9 %collective-permute-done.53 = f32[2,1,1,1024,128]{4,3,2,1,0:T(8,128)S(1)} collective-permute-done((f32[2,1,1,1024,128]{4,3,2,1,0:T(8,128)S(1)}, f32[2,1,1,1024,128]{4,3,2,1,0:T(8,128)S(1)}, u32[]{:S(2)}, u32[]{:S(2)}) %collective-permute-start.53) | collective-permute-done | bytes 1048608 | tf_op jit(solution)/shard_map/ppermute | solution.py:37
  708.0 21.4 %collective-permute-done.56 = f32[1,1,2,1040,128]{4,3,2,1,0:T(8,128)S(1)} collective-permute-done((f32[1,1,2,1040,128]{4,3,2,1,0:T(8,128)S(1)}, f32[1,1,2,1040,128]{4,3,2,1,0:T(8,128)S(1)}, u32[]{:S(2)}, u32[]{:S(2)}) %collective-permute-start.56) | collective-permute-done | bytes 1064992 | tf_op jit(solution)/shard_map/ppermute | solution.py:37
  731.5 8.0 collective-permute-done.54
  748.6 17.1 %collective-permute-done.66 = f32[8,128]{1,0:T(8,128)S(1)} collective-permute-done((f32[8,128]{1,0:T(8,128)S(1)}, f32[8,128]{1,0:T(8,128)S(1)}, u32[]{:S(2)}, u32[]{:S(2)}) %collective-permute-start.66) | collective-permute-done | bytes 4128 | tf_op jit(solution)/shard_map/ppermute | solution.py:37
  769.3 3.6 collective-permute-done.68
  773.7 3.7 collective-permute-done.69
  784.9 5.2 shard_map.211
  792.4 13.5 %shard_map.210 = (f32[8256,128]{1,0:T(8,128)}, f32[8256,128]{1,0:T(8,128)}, f32[8256,128]{1,0:T(8,128)}, bf16[8256,128]{1,0:T(8,128)(2,1)}, f32[8256,128]{1,0:T(8,128)}) custom-call(s32[4]{0:T(128)S(1)} %pad_add_fusion.2.place_ref, f32[3]{0:T(128)S(1)} %pad_maximum_fusion.20.scalar_ref, f32[2064,128]{1,0:T(8,128)S(1)} %pad_maximum_fusion.8.refs_0_, ...), custom_call_target="tpu_custom_call" | custom-call | tf_op jit(solution)/shard_map/pallas_call | solution.py:920
  (649 shorter events, 248.2 us)
Async XLA Ops:
  7.2 129.9 %all-gather.3.cloned.1.call-start = ((), (), s32[]{:S(2)}) async-start(), calls=%async_computation | async-start | bytes 17436672 | tf_op jit(solution)/shard_map/all_gather | solution.py:77
  9.3 215.4 %all-gather.5.cloned.1.call-start = ((), (), s32[]{:S(2)}) async-start(), calls=%async_computation.1 | async-start | bytes 9191424 | tf_op jit(solution)/shard_map/all_gather | solution.py:77
  9.4 17.2 %collective-permute-start.1 = (s32[96]{0:T(128)}, s32[96]{0:T(128)S(1)}, u32[]{:S(2)}, u32[]{:S(2)}) collective-permute-start(s32[96]{0:T(128)} %param.13), channel_id=1, source_target_pairs={{0,2},{1,3},{2,0},{3,1},{4,6},{5,7},{6,4},{7,5},{8,10},{9,11},{10,... | collective-permute-start | bytes 1160 | tf_op jit(solution)/shard_map/ppermute | solution.py:37
  12.4 15.0 %collective-permute-start = (s32[96]{0:T(128)}, s32[96]{0:T(128)S(1)}, u32[]{:S(2)}, u32[]{:S(2)}) collective-permute-start(s32[96]{0:T(128)} %param.13), channel_id=1, source_target_pairs={{0,1},{1,0},{2,3},{3,2},{4,5},{5,4},{6,7},{7,6},{8,9},{9,8},{10,11... | collective-permute-start | bytes 1160 | tf_op jit(solution)/shard_map/ppermute | solution.py:37
  12.4 20.5 %collective-permute-start.5 = (s32[864]{0:T(1024)}, s32[864]{0:T(1024)S(1)}, u32[]{:S(2)}, u32[]{:S(2)}) collective-permute-start(s32[864]{0:T(1024)} %param.12), channel_id=1, source_target_pairs={{0,2},{1,3},{2,0},{3,1},{4,6},{5,7},{6,4},{7,5},{8,10},{9,11},{10,... | collective-permute-start | bytes 10376 | tf_op jit(solution)/shard_map/ppermute | solution.py:37
  15.1 23.0 %collective-permute-start.9 = (f32[8,128]{1,0:T(8,128)S(1)}, f32[8,128]{1,0:T(8,128)S(1)}, u32[]{:S(2)}, u32[]{:S(2)}) collective-permute-start(f32[8,128]{1,0:T(8,128)S(1)} %broadcast_in_dim.85), channel_id=1, source_target_pairs={{0,1},{1,0},{2,3},{3,2},{4,5},{5,4},{6,7},{7,6},{8,9},{9,8},{10,11... | collective-permute-start | bytes 12296 | tf_op jit(solution)/shard_map/ppermute | solution.py:37
  32.6 14.7 %collective-permute-start.3 = (bf16[192,1728]{1,0:T(8,128)(2,1)S(1)}, bf16[192,1728]{1,0:T(8,128)(2,1)S(1)}, u32[]{:S(2)}, u32[]{:S(2)}) collective-permute-start(bf16[192,1728]{1,0:T(8,128)(2,1)S(1)} %pad_maximum_fusion.10), channel_id=1, source_target_pairs={{0,1},{1,0},{2,3},{3,2},{4,5},{5,4},{6,7},{7,6},{8,9},{9,8},{10,11... | collective-permute-start | bytes 1990664 | tf_op jit(solution)/shard_map/ppermute | solution.py:37
  48.3 17.7 %collective-permute-start.4 = (bf16[96,1728]{1,0:T(8,128)(2,1)S(1)}, bf16[96,1728]{1,0:T(8,128)(2,1)S(1)}, u32[]{:S(2)}, u32[]{:S(2)}) collective-permute-start(bf16[96,1728]{1,0:T(8,128)(2,1)S(1)} %slice_add_fusion.2), channel_id=1, source_target_pairs={{0,2},{1,3},{2,0},{3,1},{4,6},{5,7},{6,4},{7,5},{8,10},{9,11},{10,... | collective-permute-start | bytes 995336 | tf_op jit(solution)/shard_map/ppermute | solution.py:37
  166.1 15.5 %collective-permute-start.15 = (bf16[96,1536]{1,0:T(8,128)(2,1)}, bf16[96,1536]{1,0:T(8,128)(2,1)}, u32[]{:S(2)}, u32[]{:S(2)}) collective-permute-start(bf16[96,1536]{1,0:T(8,128)(2,1)} %concatenate.152), channel_id=1, source_target_pairs={{0,2},{1,3},{2,0},{3,1},{4,6},{5,7},{6,4},{7,5},{8,10},{9,11},{10,... | collective-permute-start | bytes 884744 | tf_op jit(solution)/shard_map/ppermute | solution.py:37
  168.5 22.8 %collective-permute-start.14 = (bf16[96,1536]{1,0:T(8,128)(2,1)}, bf16[96,1536]{1,0:T(8,128)(2,1)}, u32[]{:S(2)}, u32[]{:S(2)}) collective-permute-start(bf16[96,1536]{1,0:T(8,128)(2,1)} %concatenate.152), channel_id=1, source_target_pairs={{0,1},{1,0},{2,3},{3,2},{4,5},{5,4},{6,7},{7,6},{8,9},{9,8},{10,11... | collective-permute-start | bytes 884744 | tf_op jit(solution)/shard_map/ppermute | solution.py:37
  242.1 11.6 %collective-permute-start.17 = (bf16[96,512]{1,0:T(8,128)(2,1)}, bf16[96,512]{1,0:T(8,128)(2,1)}, u32[]{:S(2)}, u32[]{:S(2)}) collective-permute-start(bf16[96,512]{1,0:T(8,128)(2,1)} %fusion.19), channel_id=1, source_target_pairs={{0,1},{1,0},{2,3},{3,2},{4,5},{5,4},{6,7},{7,6},{8,9},{9,8},{10,11... | collective-permute-start | bytes 294920 | tf_op jit(solution)/shard_map/ppermute | solution.py:37
  265.7 37.1 %collective-permute-start.23 = (bf16[96,7104]{1,0:T(8,128)(2,1)}, bf16[96,7104]{1,0:T(8,128)(2,1)}, u32[]{:S(2)}, u32[]{:S(2)}) collective-permute-start(bf16[96,7104]{1,0:T(8,128)(2,1)} %constant_dynamic-update-slice_fusion), channel_id=1, source_target_pairs={{0,2},{1,3},{2,0},{3,1},{4,6},{5,7},{6,4},{7,5},{8,10},{9,11},{10,... | collective-permute-start | bytes 4091912 | tf_op jit(solution)/shard_map/ppermute | solution.py:37
  268.8 39.7 %collective-permute-start.22 = (bf16[96,7104]{1,0:T(8,128)(2,1)}, bf16[96,7104]{1,0:T(8,128)(2,1)}, u32[]{:S(2)}, u32[]{:S(2)}) collective-permute-start(bf16[96,7104]{1,0:T(8,128)(2,1)} %constant_dynamic-update-slice_fusion), channel_id=1, source_target_pairs={{0,1},{1,0},{2,3},{3,2},{4,5},{5,4},{6,7},{7,6},{8,9},{9,8},{10,11... | collective-permute-start | bytes 4091912 | tf_op jit(solution)/shard_map/ppermute | solution.py:37
  380.5 10.7 %collective-permute-start.26 = (f32[192,1024]{1,0:T(8,128)S(1)}, f32[192,1024]{1,0:T(8,128)S(1)}, u32[]{:S(2)}, u32[]{:S(2)}) collective-permute-start(f32[192,1024]{1,0:T(8,128)S(1)} %get-tuple-element.182), channel_id=1, source_target_pairs={{1,0},{2,1},{3,2},{5,4},{6,5},{7,6},{9,8},{10,9},{11,10},{13,12},{... | collective-permute-start | bytes 2359304 | tf_op jit(solution)/shard_map/ppermute | solution.py:189
  399.4 11.5 %collective-permute-start.27 = (bf16[192,512]{1,0:T(8,128)(2,1)S(1)}, bf16[192,512]{1,0:T(8,128)(2,1)S(1)}, u32[]{:S(2)}, u32[]{:S(2)}) collective-permute-start(bf16[192,512]{1,0:T(8,128)(2,1)S(1)} %pad_maximum_fusion.19), channel_id=1, source_target_pairs={{0,1},{1,0},{2,3},{3,2},{4,5},{5,4},{6,7},{7,6},{8,9},{9,8},{10,11... | collective-permute-start | bytes 589832 | tf_op jit(solution)/shard_map/ppermute | solution.py:37
  443.5 14.2 %collective-permute-start.29 = (f32[17408,128]{1,0:T(8,128)}, f32[17408,128]{1,0:T(8,128)S(1)}, u32[]{:S(2)}, u32[]{:S(2)}) collective-permute-start(f32[17408,128]{1,0:T(8,128)} %get-tuple-element.106), channel_id=1, source_target_pairs={{0,1},{1,0},{2,3},{3,2},{4,5},{5,4},{6,7},{7,6},{8,9},{9,8},{10,11... | collective-permute-start | bytes 26738696 | tf_op jit(solution)/shard_map/ppermute | solution.py:37
  475.8 51.0 %collective-permute-start.32 = (f32[2,2,1,1088,128]{4,3,2,1,0:T(8,128)}, f32[2,2,1,1088,128]{4,3,2,1,0:T(8,128)}, u32[]{:S(2)}, u32[]{:S(2)}) collective-permute-start(f32[2,2,1,1088,128]{4,3,2,1,0:T(8,128)} %constant_dynamic-slice_fusion.13), channel_id=1, source_target_pairs={{0,4},{4,0},{8,12},{12,8},{16,20},{20,16},{24,28},{28,24},{1,5},{5... | collective-permute-start | bytes 6684680 | tf_op jit(solution)/shard_map/ppermute | solution.py:37
  476.1 37.3 %collective-permute-start.44 = (bf16[96,3072]{1,0:T(8,128)(2,1)}, bf16[96,3072]{1,0:T(8,128)(2,1)}, u32[]{:S(2)}, u32[]{:S(2)}) collective-permute-start(bf16[96,3072]{1,0:T(8,128)(2,1)} %copy-done.44), channel_id=1, source_target_pairs={{0,2},{1,3},{2,0},{3,1},{4,6},{5,7},{6,4},{7,5},{8,10},{9,11},{10,... | collective-permute-start | bytes 1769480 | tf_op jit(solution)/shard_map/ppermute | solution.py:37
  479.5 51.2 %collective-permute-start.33 = (f32[2,1,2,1088,128]{4,3,2,1,0:T(8,128)}, f32[2,1,2,1088,128]{4,3,2,1,0:T(8,128)}, u32[]{:S(2)}, u32[]{:S(2)}) collective-permute-start(f32[2,1,2,1088,128]{4,3,2,1,0:T(8,128)} %constant_dynamic-slice_fusion.12), channel_id=1, source_target_pairs={{0,8},{4,12},{8,0},{12,4},{16,24},{20,28},{24,16},{28,20},{1,9},{5... | collective-permute-start | bytes 6684680 | tf_op jit(solution)/shard_map/ppermute | solution.py:37
  483.1 31.7 %collective-permute-start.31 = (f32[96,1536]{1,0:T(8,128)}, f32[96,1536]{1,0:T(8,128)}, u32[]{:S(2)}, u32[]{:S(2)}) collective-permute-start(f32[96,1536]{1,0:T(8,128)} %slice_add_fusion), channel_id=1, source_target_pairs={{0,2},{1,3},{2,0},{3,1},{4,6},{5,7},{6,4},{7,5},{8,10},{9,11},{10,... | collective-permute-start | bytes 1769480 | tf_op jit(solution)/shard_map/ppermute | solution.py:37
  484.8 22.7 %collective-permute-start.47 = (bf16[96,768]{1,0:T(8,128)(2,1)S(1)}, bf16[96,768]{1,0:T(8,128)(2,1)}, u32[]{:S(2)}, u32[]{:S(2)}) collective-permute-start(bf16[96,768]{1,0:T(8,128)(2,1)S(1)} %copy-done.64), channel_id=1, source_target_pairs={{0,2},{1,3},{2,0},{3,1},{4,6},{5,7},{6,4},{7,5},{8,10},{9,11},{10,... | collective-permute-start | bytes 442376 | tf_op jit(solution)/shard_map/ppermute | solution.py:37
  511.3 27.7 %collective-permute-start.43 = (bf16[96,3072]{1,0:T(8,128)(2,1)}, bf16[96,3072]{1,0:T(8,128)(2,1)S(1)}, u32[]{:S(2)}, u32[]{:S(2)}) collective-permute-start(bf16[96,3072]{1,0:T(8,128)(2,1)} %copy-done.44), channel_id=1, source_target_pairs={{0,1},{1,0},{2,3},{3,2},{4,5},{5,4},{6,7},{7,6},{8,9},{9,8},{10,11... | collective-permute-start | bytes 1769480 | tf_op jit(solution)/shard_map/ppermute | solution.py:37
  513.4 26.6 %collective-permute-start.45 = (bf16[96,3072]{1,0:T(8,128)(2,1)}, bf16[96,3072]{1,0:T(8,128)(2,1)S(1)}, u32[]{:S(2)}, u32[]{:S(2)}) collective-permute-start(bf16[96,3072]{1,0:T(8,128)(2,1)} %collective-permute-done.44), channel_id=1, source_target_pairs={{0,1},{1,0},{2,3},{3,2},{4,5},{5,4},{6,7},{7,6},{8,9},{9,8},{10,11... | collective-permute-start | bytes 1769480 | tf_op jit(solution)/shard_map/ppermute | solution.py:37
  521.0 22.2 %collective-permute-start.40 = (bf16[96,768]{1,0:T(8,128)(2,1)}, bf16[96,768]{1,0:T(8,128)(2,1)}, u32[]{:S(2)}, u32[]{:S(2)}) collective-permute-start(bf16[96,768]{1,0:T(8,128)(2,1)} %fusion.53), channel_id=1, source_target_pairs={{0,1},{1,0},{2,3},{3,2},{4,5},{5,4},{6,7},{7,6},{8,9},{9,8},{10,11... | collective-permute-start | bytes 442376 | tf_op jit(solution)/shard_map/ppermute | solution.py:37
  526.8 23.4 %collective-permute-start.42 = (bf16[96,768]{1,0:T(8,128)(2,1)}, bf16[96,768]{1,0:T(8,128)(2,1)}, u32[]{:S(2)}, u32[]{:S(2)}) collective-permute-start(bf16[96,768]{1,0:T(8,128)(2,1)} %collective-permute-done.41), channel_id=1, source_target_pairs={{0,1},{1,0},{2,3},{3,2},{4,5},{5,4},{6,7},{7,6},{8,9},{9,8},{10,11... | collective-permute-start | bytes 442376 | tf_op jit(solution)/shard_map/ppermute | solution.py:37
  536.9 13.3 %collective-permute-start.38 = (bf16[96,2304]{1,0:T(8,128)(2,1)}, bf16[96,2304]{1,0:T(8,128)(2,1)}, u32[]{:S(2)}, u32[]{:S(2)}) collective-permute-start(bf16[96,2304]{1,0:T(8,128)(2,1)} %pad_maximum_fusion.16), channel_id=1, source_target_pairs={{0,2},{1,3},{2,0},{3,1},{4,6},{5,7},{6,4},{7,5},{8,10},{9,11},{10,... | collective-permute-start | bytes 1327112 | tf_op jit(solution)/shard_map/ppermute | solution.py:37
  539.0 14.5 %collective-permute-start.35 = (bf16[96,768]{1,0:T(8,128)(2,1)}, bf16[96,768]{1,0:T(8,128)(2,1)}, u32[]{:S(2)}, u32[]{:S(2)}) collective-permute-start(bf16[96,768]{1,0:T(8,128)(2,1)} %add_convert_fusion.4), channel_id=1, source_target_pairs={{0,2},{1,3},{2,0},{3,1},{4,6},{5,7},{6,4},{7,5},{8,10},{9,11},{10,... | collective-permute-start | bytes 442376 | tf_op jit(solution)/shard_map/ppermute | solution.py:37
  543.0 19.8 %collective-permute-start.37 = (bf16[96,2304]{1,0:T(8,128)(2,1)}, bf16[96,2304]{1,0:T(8,128)(2,1)}, u32[]{:S(2)}, u32[]{:S(2)}) collective-permute-start(bf16[96,2304]{1,0:T(8,128)(2,1)} %pad_maximum_fusion.16), channel_id=1, source_target_pairs={{0,1},{1,0},{2,3},{3,2},{4,5},{5,4},{6,7},{7,6},{8,9},{9,8},{10,11... | collective-permute-start | bytes 1327112 | tf_op jit(solution)/shard_map/ppermute | solution.py:37
  543.2 10.2 %collective-permute-start.50 = (f32[8,768]{1,0:T(8,128)S(1)}, f32[8,768]{1,0:T(8,128)S(1)}, u32[]{:S(2)}, u32[]{:S(2)}) collective-permute-start(f32[8,768]{1,0:T(8,128)S(1)} %stack.120), channel_id=1, source_target_pairs={{0,2},{1,3},{2,0},{3,1},{4,6},{5,7},{6,4},{7,5},{8,10},{9,11},{10,... | collective-permute-start | bytes 73736 | tf_op jit(solution)/shard_map/ppermute | solution.py:37
  550.2 12.7 %collective-permute-start.39 = (bf16[96,2304]{1,0:T(8,128)(2,1)}, bf16[96,2304]{1,0:T(8,128)(2,1)}, u32[]{:S(2)}, u32[]{:S(2)}) collective-permute-start(bf16[96,2304]{1,0:T(8,128)(2,1)} %collective-permute-done.38), channel_id=1, source_target_pairs={{0,1},{1,0},{2,3},{3,2},{4,5},{5,4},{6,7},{7,6},{8,9},{9,8},{10,11... | collective-permute-start | bytes 1327112 | tf_op jit(solution)/shard_map/ppermute | solution.py:37
  558.1 28.7 %collective-permute-start.62 = (f32[2,1,2,544,128]{4,3,2,1,0:T(8,128)}, f32[2,1,2,544,128]{4,3,2,1,0:T(8,128)}, u32[]{:S(2)}, u32[]{:S(2)}) collective-permute-start(f32[2,1,2,544,128]{4,3,2,1,0:T(8,128)} %constant_dynamic-slice_fusion.2), channel_id=1, source_target_pairs={{0,2},{1,3},{2,0},{3,1},{4,6},{5,7},{6,4},{7,5},{8,10},{9,11},{10,... | collective-permute-start | bytes 3342344 | tf_op jit(solution)/shard_map/ppermute | solution.py:37
  560.0 49.2 %collective-permute-start.59 = (f32[2,2,1,544,128]{4,3,2,1,0:T(8,128)}, f32[2,2,1,544,128]{4,3,2,1,0:T(8,128)}, u32[]{:S(2)}, u32[]{:S(2)}) collective-permute-start(f32[2,2,1,544,128]{4,3,2,1,0:T(8,128)} %constant_dynamic-slice_fusion.5), channel_id=1, source_target_pairs={{0,2},{1,3},{2,0},{3,1},{4,6},{5,7},{6,4},{7,5},{8,10},{9,11},{10,... | collective-permute-start | bytes 3342344 | tf_op jit(solution)/shard_map/ppermute | solution.py:37
  581.7 77.6 %collective-permute-start.52 = (f32[2,2,1,1024,128]{4,3,2,1,0:T(8,128)}, f32[2,2,1,1024,128]{4,3,2,1,0:T(8,128)}, u32[]{:S(2)}, u32[]{:S(2)}) collective-permute-start(f32[2,2,1,1024,128]{4,3,2,1,0:T(8,128)} %constant_dynamic-slice_fusion.11), channel_id=1, source_target_pairs={{0,4},{4,0},{8,12},{12,8},{16,20},{20,16},{24,28},{28,24},{1,5},{5... | collective-permute-start | bytes 6291464 | tf_op jit(solution)/shard_map/ppermute | solution.py:37
  585.2 77.3 %collective-permute-start.55 = (f32[2,1,2,1040,128]{4,3,2,1,0:T(8,128)}, f32[2,1,2,1040,128]{4,3,2,1,0:T(8,128)}, u32[]{:S(2)}, u32[]{:S(2)}) collective-permute-start(f32[2,1,2,1040,128]{4,3,2,1,0:T(8,128)} %constant_dynamic-slice_fusion.8), channel_id=1, source_target_pairs={{0,8},{4,12},{8,0},{12,4},{16,24},{20,28},{24,16},{28,20},{1,9},{5... | collective-permute-start | bytes 6389768 | tf_op jit(solution)/shard_map/ppermute | solution.py:37
  589.1 56.8 %collective-permute-start.63 = (f32[1,1,2,544,128]{4,3,2,1,0:T(8,128)}, f32[1,1,2,544,128]{4,3,2,1,0:T(8,128)S(1)}, u32[]{:S(2)}, u32[]{:S(2)}) collective-permute-start(f32[1,1,2,544,128]{4,3,2,1,0:T(8,128)} %constant_dynamic-slice_fusion.1), channel_id=1, source_target_pairs={{0,16},{4,20},{8,24},{12,28},{16,0},{20,4},{24,8},{28,12},{1,17},{... | collective-permute-start | bytes 1671176 | tf_op jit(solution)/shard_map/ppermute | solution.py:37
  611.4 45.7 %collective-permute-start.60 = (f32[2,1,1,544,128]{4,3,2,1,0:T(8,128)}, f32[2,1,1,544,128]{4,3,2,1,0:T(8,128)S(1)}, u32[]{:S(2)}, u32[]{:S(2)}) collective-permute-start(f32[2,1,1,544,128]{4,3,2,1,0:T(8,128)} %constant_dynamic-slice_fusion.4), channel_id=1, source_target_pairs={{0,8},{4,12},{8,0},{12,4},{16,24},{20,28},{24,16},{28,20},{1,9},{5... | collective-permute-start | bytes 1671176 | tf_op jit(solution)/shard_map/ppermute | solution.py:37
  646.0 21.0 %collective-permute-start.64 = (f32[1,1,1,544,128]{4,3,2,1,0:T(8,128)S(1)}, f32[1,1,1,544,128]{4,3,2,1,0:T(8,128)S(1)}, u32[]{:S(2)}, u32[]{:S(2)}) collective-permute-start(f32[1,1,1,544,128]{4,3,2,1,0:T(8,128)S(1)} %constant_dynamic-slice_fusion), channel_id=1, source_target_pairs={{0,4},{4,0},{8,12},{12,8},{16,20},{20,16},{24,28},{28,24},{1,5},{5... | collective-permute-start | bytes 835592 | tf_op jit(solution)/shard_map/ppermute | solution.py:37
  657.2 15.4 %collective-permute-start.61 = (f32[1,1,1,544,128]{4,3,2,1,0:T(8,128)S(1)}, f32[1,1,1,544,128]{4,3,2,1,0:T(8,128)S(1)}, u32[]{:S(2)}, u32[]{:S(2)}) collective-permute-start(f32[1,1,1,544,128]{4,3,2,1,0:T(8,128)S(1)} %constant_dynamic-slice_fusion.3), channel_id=1, source_target_pairs={{0,16},{4,20},{8,24},{12,28},{16,0},{20,4},{24,8},{28,12},{1,17},{... | collective-permute-start | bytes 835592 | tf_op jit(solution)/shard_map/ppermute | solution.py:37
  661.8 45.9 %collective-permute-start.53 = (f32[2,1,1,1024,128]{4,3,2,1,0:T(8,128)S(1)}, f32[2,1,1,1024,128]{4,3,2,1,0:T(8,128)S(1)}, u32[]{:S(2)}, u32[]{:S(2)}) collective-permute-start(f32[2,1,1,1024,128]{4,3,2,1,0:T(8,128)S(1)} %constant_dynamic-slice_fusion.10), channel_id=1, source_target_pairs={{0,8},{4,12},{8,0},{12,4},{16,24},{20,28},{24,16},{28,20},{1,9},{5... | collective-permute-start | bytes 3145736 | tf_op jit(solution)/shard_map/ppermute | solution.py:37
  665.0 64.4 %collective-permute-start.56 = (f32[1,1,2,1040,128]{4,3,2,1,0:T(8,128)S(1)}, f32[1,1,2,1040,128]{4,3,2,1,0:T(8,128)S(1)}, u32[]{:S(2)}, u32[]{:S(2)}) collective-permute-start(f32[1,1,2,1040,128]{4,3,2,1,0:T(8,128)S(1)} %constant_dynamic-slice_fusion.7), channel_id=1, source_target_pairs={{0,16},{4,20},{8,24},{12,28},{16,0},{20,4},{24,8},{28,12},{1,17},{... | collective-permute-start | bytes 3194888 | tf_op jit(solution)/shard_map/ppermute | solution.py:37
  673.3 58.2 %collective-permute-start.72 = (f32[544,128]{1,0:T(8,128)S(1)}, f32[544,128]{1,0:T(8,128)S(1)}, u32[]{:S(2)}, u32[]{:S(2)}) collective-permute-start(f32[544,128]{1,0:T(8,128)S(1)} %get-tuple-element.147), channel_id=1, source_target_pairs={{0,2},{1,3},{2,0},{3,1},{4,6},{5,7},{6,4},{7,5},{8,10},{9,11},{10,... | collective-permute-start | bytes 835592 | tf_op jit(solution)/shard_map/ppermute | solution.py:37
  707.9 31.6 %collective-permute-start.54 = (f32[1,1,1,1024,128]{4,3,2,1,0:T(8,128)S(1)}, f32[1,1,1,1024,128]{4,3,2,1,0:T(8,128)S(1)}, u32[]{:S(2)}, u32[]{:S(2)}) collective-permute-start(f32[1,1,1,1024,128]{4,3,2,1,0:T(8,128)S(1)} %constant_dynamic-slice_fusion.9), channel_id=1, source_target_pairs={{0,16},{4,20},{8,24},{12,28},{16,0},{20,4},{24,8},{28,12},{1,17},{... | collective-permute-start | bytes 1572872 | tf_op jit(solution)/shard_map/ppermute | solution.py:37
  729.6 11.8 %collective-permute-start.57 = (f32[1,1,1,1040,128]{4,3,2,1,0:T(8,128)S(1)}, f32[1,1,1,1040,128]{4,3,2,1,0:T(8,128)S(1)}, u32[]{:S(2)}, u32[]{:S(2)}) collective-permute-start(f32[1,1,1,1040,128]{4,3,2,1,0:T(8,128)S(1)} %constant_dynamic-slice_fusion.6), channel_id=1, source_target_pairs={{0,4},{4,0},{8,12},{12,8},{16,20},{20,16},{24,28},{28,24},{1,5},{5... | collective-permute-start | bytes 1597448 | tf_op jit(solution)/shard_map/ppermute | solution.py:37
  742.3 35.1 %collective-permute-start.58 = (f32[2064,128]{1,0:T(8,128)S(1)}, f32[2064,128]{1,0:T(8,128)}, u32[]{:S(2)}, u32[]{:S(2)}) collective-permute-start(f32[2064,128]{1,0:T(8,128)S(1)} %pad_maximum_fusion.8.refs_0_), channel_id=1, source_target_pairs={{0,2},{1,3},{2,0},{3,1},{4,6},{5,7},{6,4},{7,5},{8,10},{9,11},{10,... | collective-permute-start | bytes 3170312 | tf_op jit(solution)/shard_map/ppermute | solution.py:37
  747.2 18.5 %collective-permute-start.66 = (f32[8,128]{1,0:T(8,128)S(1)}, f32[8,128]{1,0:T(8,128)S(1)}, u32[]{:S(2)}, u32[]{:S(2)}) collective-permute-start(f32[8,128]{1,0:T(8,128)S(1)} %fusion.46), channel_id=1, source_target_pairs={{0,2},{1,3},{2,0},{3,1},{4,6},{5,7},{6,4},{7,5},{8,10},{9,11},{10,... | collective-permute-start | bytes 12296 | tf_op jit(solution)/shard_map/ppermute | solution.py:37
  748.5 31.2 %collective-permute-start.74 = (f32[2176,128]{1,0:T(8,128)S(1)}, f32[2176,128]{1,0:T(8,128)S(1)}, u32[]{:S(2)}, u32[]{:S(2)}) collective-permute-start(f32[2176,128]{1,0:T(8,128)S(1)} %pad_maximum_fusion.7.refs_0_), channel_id=1, source_target_pairs={{0,1},{1,0},{2,3},{3,2},{4,5},{5,4},{6,7},{7,6},{8,9},{9,8},{10,11... | collective-permute-start | bytes 3342344 | tf_op jit(solution)/shard_map/ppermute | solution.py:37
  773.7 16.4 %collective-permute-start.70 = (f32[2064,128]{1,0:T(8,128)S(1)}, f32[2064,128]{1,0:T(8,128)}, u32[]{:S(2)}, u32[]{:S(2)}) collective-permute-start(f32[2064,128]{1,0:T(8,128)S(1)} %pad_maximum_fusion.8.refs_0_), channel_id=1, source_target_pairs={{0,1},{1,0},{2,3},{3,2},{4,5},{5,4},{6,7},{7,6},{8,9},{9,8},{10,11... | collective-permute-start | bytes 3170312 | tf_op jit(solution)/shard_map/ppermute | solution.py:37
  777.4 12.7 %collective-permute-start.71 = (f32[2064,128]{1,0:T(8,128)}, f32[2064,128]{1,0:T(8,128)}, u32[]{:S(2)}, u32[]{:S(2)}) collective-permute-start(f32[2064,128]{1,0:T(8,128)} %collective-permute-done.58.refs_2_), channel_id=1, source_target_pairs={{0,1},{1,0},{2,3},{3,2},{4,5},{5,4},{6,7},{7,6},{8,9},{9,8},{10,11... | collective-permute-start | bytes 3170312 | tf_op jit(solution)/shard_map/ppermute | solution.py:37
  (168 other events, 1244.5 us)
Sparse Core Ops, SparseCore 0:
  11.5 125.5 all-gather.2
  140.5 84.2 all-gather.4

commit v3 on v2

--- a/solution.py
+++ b/solution.py
@@ -75,12 +75,6 @@
     part = shard.shape[0] // 4
     quarter = lax.dynamic_slice_in_dim(shard, lax.axis_index("grp") * part, part, 0)
     return lax.all_gather(quarter, ("dp", "grp"), axis=0, tiled=True)
-
-
-def gather_both(enc_shard, dec_shard):
-    enc_copy = gather_quarters(enc_shard)
-    enc_copy, dec_shard = lax.optimization_barrier((enc_copy, dec_shard))
-    return enc_copy, gather_quarters(dec_shard)
 
 
 def section(cells, dim, start, size):
@@ -126,15 +120,17 @@
     return blocks
 
 
-def reduce_rest(blocks, routes):
+def reduce_rest(blocks, routes, first=1, last=None):
     bits = dp_bits()
     names = [("dp", bit) for bit in reversed(bits)]
     blocks = list(blocks)
-    for step in range(1, len(routes[0])):
+    for step in range(first, len(routes[0]) if last is None else last):
         for index, route in enumerate(routes):
             axis, bit = route[step]
             dim = len(bits) if axis == "grp" else names.index(route[step])
             blocks[index] = reduce_bit(blocks[index], dim, axis, bit)
+    if last is not None:
+        return blocks
     return [block.reshape(-1, 128) for block in blocks]
 
 
@@ -380,9 +376,20 @@
 
 
 def attend_kernel(
-    window, width, q_ref, k_ref, v_ref, qid_ref, kid_ref, o_ref, bias_ref, score_ref, prob_ref
+    window,
+    stride,
+    width,
+    q_ref,
+    k_ref,
+    v_ref,
+    qid_ref,
+    kid_ref,
+    o_ref,
+    bias_ref,
+    score_ref,
+    prob_ref,
 ):
-    start = pl.multiple_of(pl.program_id(0) * BLOCK, BLOCK)
+    start = pl.multiple_of(pl.program_id(0) * stride, BLOCK)
     scale = width ** (-0.5)
     masks = head_masks(width)
     near = pl.ds(start, window)
@@ -410,18 +417,19 @@
     return merge(cells.reshape(-1, 8, cells.shape[1]), axis=0)
 
 
-def attend_back_kernel(window, width, *refs):
-    q_ref, g_ref, k_ref, v_ref, qid_ref, kid_ref, dq_ref, dk_ref, dv_ref = refs[:9]
-    bias_ref, score_ref, grad_ref, prob_ref, back_ref = refs[9:]
+def attend_back_kernel(window, stride, width, pick, *refs):
+    q_ref, g_ref, k_ref, v_ref, qid_ref, kid_ref = refs[:6]
+    dq_ref, dk_ref, dv_ref, bias_ref, score_ref, grad_ref, prob_ref, back_ref = refs[-8:]
+    before = refs[6:-8]
     step = pl.program_id(0)
-    start = pl.multiple_of(step * BLOCK, BLOCK)
+    start = pl.multiple_of(pick(step) * stride, BLOCK)
     scale = width ** (-0.5)
     masks = head_masks(width)
 
     @pl.when(step == 0)
     def _():
-        dk_ref[...] = jnp.zeros_like(dk_ref)
-        dv_ref[...] = jnp.zeros_like(dv_ref)
+        dk_ref[...] = before[0][...] if before else jnp.zeros_like(dk_ref)
+        dv_ref[...] = before[1][...] if before else jnp.zeros_like(dv_ref)
 
     near = pl.ds(start, window)
     bias_ref[...] = jnp.where(kid_ref[near, :] == qid_ref[...], 0.0, MASK_FILL)
@@ -474,8 +482,9 @@
 
 def attend_sizes(query, keys, rim):
     steps = -(-query.shape[0] // BLOCK)
-    window = BLOCK + 2 * rim if rim else keys.shape[0]
-    return steps, window, (steps - 1) * BLOCK + window
+    if rim:
+        return steps, BLOCK + 2 * rim, steps * BLOCK + 2 * rim, BLOCK
+    return steps, keys.shape[0], keys.shape[0], 0
 
 
 def whole_spec(dims):
@@ -488,10 +497,10 @@
 
 def attend(query, keys, values, query_ids, key_ids, heads, rim):
     count, columns = query.shape
-    steps, window, span = attend_sizes(query, keys, rim)
+    steps, window, span, stride = attend_sizes(query, keys, rim)
     stack = 128 * heads // columns * BLOCK
     outcome = pl.pallas_call(
-        functools.partial(attend_kernel, window, columns // heads),
+        functools.partial(attend_kernel, window, stride, columns // heads),
         grid=(steps,),
         in_specs=[
             step_spec(columns),
@@ -523,24 +532,33 @@
     return outcome[:count]
 
 
-def attend_back(query, keys, values, query_ids, key_ids, heads, rim, out_grad):
+def same_step(step):
+    return step
+
+
+def attend_back(
+    query, keys, values, query_ids, key_ids, heads, rim, out_grad, steps=None, pick=same_step, before=()
+):
     count, columns = query.shape
-    steps, window, span = attend_sizes(query, keys, rim)
+    all_steps, window, span, stride = attend_sizes(query, keys, rim)
+    steps = all_steps if steps is None else steps
     stack = 128 * heads // columns * BLOCK
-    dq, dk, dv = pl.pallas_call(
-        functools.partial(attend_back_kernel, window, columns // heads),
+    block = pl.BlockSpec((BLOCK, columns), lambda i: (pick(i), 0))
+    return pl.pallas_call(
+        functools.partial(attend_back_kernel, window, stride, columns // heads, pick),
         grid=(steps,),
         in_specs=[
-            step_spec(columns),
-            step_spec(columns),
+            block,
+            block,
             whole_spec((span, columns)),
             whole_spec((span, columns)),
-            pl.BlockSpec((1, BLOCK), lambda i: (0, i)),
+            pl.BlockSpec((1, BLOCK), lambda i: (0, pick(i))),
             whole_spec((span, 1)),
-        ],
-        out_specs=[step_spec(columns), whole_spec((span, columns)), whole_spec((span, columns))],
+        ]
+        + [whole_spec((span, columns))] * len(before),
+        out_specs=[block, whole_spec((span, columns)), whole_spec((span, columns))],
         out_shape=[
-            jax.ShapeDtypeStruct((steps * BLOCK, columns), jnp.float32),
+            jax.ShapeDtypeStruct((all_steps * BLOCK, columns), jnp.float32),
             jax.ShapeDtypeStruct((span, columns), jnp.float32),
             jax.ShapeDtypeStruct((span, columns), jnp.float32),
         ],
@@ -553,19 +571,58 @@
         ],
         compiler_params=pltpu.CompilerParams(vmem_limit_bytes=48 << 20),
         cost_estimate=pl.CostEstimate(
-            flops=10 * steps * BLOCK * window * columns,
+            flops=80 * steps * BLOCK * window * columns,
             bytes_accessed=20 * span * columns,
             transcendentals=steps * BLOCK * window * heads,
         ),
     )(
-        padded(query, steps * BLOCK),
-        padded(out_grad, steps * BLOCK),
+        padded(query, all_steps * BLOCK),
+        padded(out_grad, all_steps * BLOCK),
         padded(keys, span),
         padded(values, span),
-        padded(query_ids, steps * BLOCK, -4)[None, :],
+        padded(query_ids, all_steps * BLOCK, -4)[None, :],
         padded(key_ids, span, -5)[:, None],
-    )
-    return dq[:count], dk[: keys.shape[0]], dv[: keys.shape[0]]
+        *before,
+    )
+
+
+def attend_back_slots(query, keys, values, query_ids, key_ids, heads, rim, out_grad):
+    count = query.shape[0]
+    steps, window, _, _ = attend_sizes(query, keys, rim)
+    low = -(-rim // BLOCK)
+    high = next(i for i in range(low, steps) if i * BLOCK + window > rim + count)
+    args = (query, keys, values, query_ids, key_ids, heads, rim, out_grad)
+    edges = attend_back(
+        *args, steps=low + steps - high, pick=lambda i: i + (i // low) * (high - low)
+    )
+    ends = slice(rim + count, 2 * rim + count)
+    from_upper = passed_along(
+        jnp.concatenate([edges[1][:rim], edges[2][:rim]], axis=1), "grp", -1
+    )
+    from_lower = passed_along(
+        jnp.concatenate([edges[1][ends], edges[2][ends]], axis=1), "grp", 1
+    )
+    inner = attend_back(
+        *args, steps=high - low, pick=lambda i: i + low, before=(edges[1], edges[2])
+    )
+    query_grad = jnp.concatenate(
+        [
+            edges[0][: low * BLOCK],
+            inner[0][low * BLOCK : high * BLOCK],
+            edges[0][high * BLOCK : count],
+        ],
+        axis=0,
+    )
+    middle = jnp.concatenate([inner[1], inner[2]], axis=1)[rim : rim + count]
+    middle = jnp.concatenate(
+        [
+            middle[:rim] + from_lower,
+            middle[rim : count - rim],
+            middle[count - rim :] + from_upper,
+        ],
+        axis=0,
+    )
+    return jnp.concatenate([query_grad, middle], axis=1)
 
 
 def gelu_pair(hidden):
@@ -606,7 +663,7 @@
 
 
 def block_backward(
-    grad_out, table, heads, rim, query_ids, key_ids, saved, return_keys, pause
+    grad_out, table, heads, rim, query_ids, key_ids, saved
 ):
     (
         inputs,
@@ -628,7 +685,6 @@
     act_grad = mul_trans(down_grad, table["down_w"])
     hidden_grad = (act_grad * slope).astype(jnp.bfloat16)
     pairs["up_w"] = (normed_two, hidden_grad)
-    hidden_grad = pause(hidden_grad)
     mixed_part, gain_two, shift_two = norm_back(
         mixed, gains[1], shifts[1], mul_trans(hidden_grad, table["up_w"])
     )
@@ -636,16 +692,57 @@
     branch_grad = mixed_grad.astype(jnp.bfloat16)
     pairs["out_w"] = (attended, branch_grad)
     attended_grad = mul_trans(branch_grad, table["out_w"]).astype(jnp.bfloat16)
-    query_grad, keys_grad_all, values_grad_all = attend_back(
+    qkv_grad = attend_back_slots(
         query, all_keys, all_values, query_ids, key_ids, heads, rim, attended_grad
-    )
-    keys_grad, values_grad = return_keys((keys_grad_all, values_grad_all))
-    qkv_grad = jnp.concatenate([query_grad, keys_grad, values_grad], axis=1).astype(jnp.bfloat16)
+    ).astype(jnp.bfloat16)
     pairs["qkv_w"] = (normed_one, qkv_grad)
     input_part, gain_one, shift_one = norm_back(
         inputs, gains[0], shifts[0], mul_trans(qkv_grad, table["qkv_w"])
     )
     return (mixed_grad + input_part, (gain_one, shift_one, gain_two, shift_two), pairs)
+
+
+def enc_forward(inputs, table, own, ids):
+    gains = table["norm_g"].astype(jnp.float32)
+    shifts = table["norm_b"].astype(jnp.float32)
+    normed_one = layer_norm(inputs, gains[0], shifts[0]).astype(jnp.bfloat16)
+    qkv = matmul(normed_one, table["qkv_w"]).astype(jnp.bfloat16)
+    attended = attend(
+        qkv[:own, :D], qkv[:, D : 2 * D], qkv[:, 2 * D :], ids[:own], ids, H, 0
+    )
+    mixed = inputs[:own] + (matmul(attended, table["out_w"]) + table["out_b"].astype(jnp.float32))
+    normed_two = layer_norm(mixed, gains[1], shifts[1]).astype(jnp.bfloat16)
+    hidden = matmul(normed_two, table["up_w"]) + table["up_b"].astype(jnp.float32)
+    activated, slope = gelu_pair(hidden)
+    result = mixed + (matmul(activated, table["down_w"]) + table["down_b"].astype(jnp.float32))
+    return result, (normed_one, qkv, attended, mixed, normed_two, slope, activated)
+
+
+def enc_backward(grad_out, table, inputs, ids, saved, pause, settle):
+    normed_one, qkv, attended, mixed, normed_two, slope, activated = saved
+    gains = table["norm_g"].astype(jnp.float32)
+    shifts = table["norm_b"].astype(jnp.float32)
+    down_grad = grad_out.astype(jnp.bfloat16)
+    hidden_grad = (mul_trans(down_grad, table["down_w"]) * slope).astype(jnp.bfloat16)
+    hidden_grad = pause(hidden_grad)
+    mixed_part, gain_two, shift_two = norm_back(
+        mixed, gains[1], shifts[1], mul_trans(hidden_grad, table["up_w"])
+    )
+    mixed_grad = group_rows(grad_out + mixed_part)
+    branch_grad = mixed_grad.astype(jnp.bfloat16)
+    attended_grad = mul_trans(branch_grad, table["out_w"]).astype(jnp.bfloat16)
+    parts = attend_back(
+        qkv[:, :D], qkv[:, D : 2 * D], qkv[:, 2 * D :], ids, ids, H, 0, attended_grad
+    )
+    qkv_grad = jnp.concatenate(parts, axis=1).astype(jnp.bfloat16)
+    input_part, gain_one, shift_one = norm_back(
+        inputs, gains[0], shifts[0], mul_trans(qkv_grad, table["qkv_w"])
+    )
+    patch_grad = settle((mixed_grad + input_part).astype(jnp.bfloat16))
+    return (
+        (patch_grad, qkv_grad, branch_grad, jnp.concatenate([hidden_grad, down_grad], axis=1)),
+        (gain_one, shift_one, gain_two, shift_two),
+    )
 
 
 def core_side():
@@ -664,8 +761,10 @@
     return first, lane
 
 
-def column_sums(ref):
-    return jnp.sum(ref[...].astype(jnp.float32), axis=0, keepdims=True)
+def column_sums(ref, first=0, width=None):
+    width = ref.shape[1] if width is None else width
+    cells = ref[:, first : first + width].astype(jnp.float32)
+    return jnp.sum(cells, axis=0, keepdims=True)
 
 
 def store_flat(target, product):
@@ -683,30 +782,26 @@
     return [(start, min(size, rows - start)) for start in range(0, rows, size)]
 
 
-def enc_grad_kernel(sizes, places, place_ref, x_ref, *refs):
-    norm_ref, out_ref, stage_ref, product_ref, small_ref, quarter_ref, sems = refs[-7:]
+def enc_grad_kernel(plan, place_ref, *refs):
+    norm_ref, own_norm_ref, out_ref, stage_ref, product_ref, small_ref, quarter_ref, sems = refs[
+        -8:
+    ]
     side, far = place_ref[0], place_ref[1]
     offset = 0
     flight = [None, None]
     turn = 0
-
-    def settle():
-        if flight[turn % 2] is not None:
-            flight[turn % 2].wait()
-
-    for index, size in enumerate(sizes):
-        y_ref = refs[index]
-        blocks = y_ref.shape[1] // 256
-        first, depth = places[index]
+    for size, left, first, depth, right, column, blocks in plan:
+        x_ref, y_ref = refs[left], refs[right]
         if blocks % 2:
             columns = [2 * block + side for block in range(blocks)]
         else:
             columns = [4 * block + 2 * far + side for block in range(blocks // 2)]
-        right = column_blocks(y_ref, columns)
+        factor = column_blocks(y_ref, [column // 128 + block for block in columns])
         for start, rows in steps_of(depth, size):
-            settle()
+            if flight[turn % 2] is not None:
+                flight[turn % 2].wait()
             target = stage_ref.at[turn % 2]
-            product = trans_mul(x_ref[:, first + start : first + start + rows], right)
+            product = trans_mul(x_ref[:, first + start : first + start + rows], factor)
             if blocks % 2 == 0:
                 store_flat(target, product)
             else:
@@ -726,12 +821,21 @@
             offset += amount
     small_ref[...] = jnp.zeros_like(small_ref)
     spot = 0, 0
-    for index in (0, 2, 3, 4):
-        spot = store_vector(small_ref, *spot, column_sums(refs[index]))
+    for _, _, _, _, right, column, blocks in plan[:1] + plan[2:]:
+        spot = store_vector(
+            small_ref, *spot, column_sums(refs[right], column, blocks * 256)
+        )
     rows = norm_ref.shape[0] // 4
     norms = sum(norm_ref[index * rows : (index + 1) * rows] for index in range(4))
-    for index in range(rows):
-        spot = store_vector(small_ref, *spot, norms[index : index + 1])
+    for vector in (
+        own_norm_ref[0:1],
+        norms[0:1],
+        norms[1:2],
+        own_norm_ref[1:2],
+        norms[2:3],
+        norms[3:4],
+    ):
+        spot = store_vector(small_ref, *spot, vector)
     rows = quarter_ref.shape[0]
     quarter_ref[...] = small_ref[pl.ds(side + 2 * far, rows, stride=4), :]
     last = pltpu.make_async_copy(quarter_ref, out_ref.at[pl.ds(offset, rows)], sems.at[2])
@@ -745,12 +849,19 @@
     return jnp.stack([place % 2, place // 2])
 
 
-def enc_grad_quarter(inputs, places, grads, norms, total_rows):
-    sizes = [640, 256, 384, 256, 768]
+def enc_grad_quarter(inputs, grads, norms, own_norms, total_rows):
+    count = len(inputs)
+    plan = [
+        (640, 0, 0, PATCH, count, 0, D // 256),
+        (256, 1, 0, D, count + 1, 0, 3 * D // 256),
+        (384, 2, 0, D, count + 2, 0, D // 256),
+        (256, 2, D, D, count + 3, 0, F // 256),
+        (768, 2, 2 * D, F, count + 3, F, D // 256),
+    ]
     whole = pl.BlockSpec(memory_space=pltpu.VMEM)
     return pl.pallas_call(
-        functools.partial(enc_grad_kernel, sizes, places),
-        in_specs=[pl.BlockSpec(memory_space=pltpu.SMEM)] + [whole] * (len(grads) + 2),
+        functools.partial(enc_grad_kernel, plan),
+        in_specs=[pl.BlockSpec(memory_space=pltpu.SMEM)] + [whole] * (count + len(grads) + 2),
         out_specs=pl.BlockSpec(memory_space=pl.ANY),
         out_shape=jax.ShapeDtypeStruct((total_rows // 4, 128), jnp.float32),
         scratch_shapes=[
@@ -762,11 +873,11 @@
         ],
         compiler_params=pltpu.CompilerParams(vmem_limit_bytes=48 << 20),
         cost_estimate=pl.CostEstimate(
-            flops=total_rows * 128 * inputs.shape[0],
+            flops=total_rows * 128 * inputs[0].shape[0],
             bytes_accessed=total_rows * 128,
             transcendentals=0,
         ),
-    )(member_place(), inputs, *grads, norms)
+    )(member_place(), *inputs, *grads, norms, own_norms)
 
 
 def store_pixels(product_ref, targets):
@@ -956,8 +1067,8 @@
         local_slot[:, None] == jnp.arange(slot_dev, dtype=jnp.int32)[None, :]
     ).astype(jnp.bfloat16)
     seen = jnp.sum(chosen.astype(jnp.float32), axis=0) > 0.5
-    enc_input = own_rows(matmul(chosen, patches).astype(jnp.bfloat16))
-    enc_waves = sincos(visible % L, D)
+    enc_input = group_rows(own_rows(matmul(chosen, patches).astype(jnp.bfloat16)))
+    enc_waves = sincos(group_vis % L, D)
     positions = (my_index * slot_dev + jnp.arange(slot_dev, dtype=jnp.int32)) % L
     dec_waves = sincos(positions, E)
     pixels = patches.astype(jnp.float32)
@@ -991,7 +1102,6 @@
             total_count,
         )
     )
-    own_ids = group_ids[: visible.shape[0]]
     enc_copy, dec_shard = lax.optimization_barrier((enc_copy, dec_params))
     dec_copy = gather_quarters(dec_shard.astype(jnp.bfloat16))
     enc_table = unpack(enc_copy, enc_pieces(), ENC_STEPS)
@@ -1002,11 +1112,8 @@
         + enc_waves
     )
 
-    def enc_share(pair):
-        joined = group_rows(jnp.concatenate(pair, axis=1))
-        return (joined[:, :D], joined[:, D:])
-
-    enc_out, enc_saved = block_forward(enc_start, enc_table, H, 0, own_ids, group_ids, enc_share)
+    own = visible.shape[0]
+    enc_out, enc_saved = enc_forward(enc_start, enc_table, own, group_ids)
     enc_gain = enc_table["norm_g"].astype(jnp.float32)
     enc_shift = enc_table["norm_b"].astype(jnp.float32)
     enc_final = layer_norm(enc_out, enc_gain[2], enc_shift[2]).astype(jnp.bfloat16)
@@ -1014,9 +1121,7 @@
         matmul(enc_final, dec_table["embed_w"]) + dec_table["embed_b"].astype(jnp.float32)
     ).astype(jnp.bfloat16)
     group_latent = group_rows(latent)
-    enc_inputs = jnp.concatenate(
-        [enc_saved[1], enc_saved[5], enc_saved[7], enc_saved[9], enc_input], axis=1
-    )
+    enc_inputs = jnp.concatenate([enc_saved[2], enc_saved[4], enc_saved[6]], axis=1)
     group_latent, enc_inputs = lax.optimization_barrier((group_latent, enc_inputs))
     group_inputs = group_rows(enc_inputs)
     placed = trans_mul(chosen, group_latent)
@@ -1028,21 +1133,6 @@
     def dec_share(pair):
         joined = extended(jnp.concatenate(pair, axis=1), rim)
         return (joined[:, :E], joined[:, E:])
-
-    def dec_return(pair):
-        joined = jnp.concatenate(pair, axis=1)
-        from_upper = passed_along(joined[:rim], "grp", -1)
-        from_lower = passed_along(joined[rim + slot_dev :], "grp", 1)
-        middle = joined[rim : rim + slot_dev]
-        middle = jnp.concatenate(
-            [
-                middle[:rim] + from_lower,
-                middle[rim : slot_dev - rim],
-                middle[slot_dev - rim :] + from_upper,
-            ],
-            axis=0,
-        )
-        return (middle[:, :E], middle[:, E:])
 
     dec_out, dec_saved = block_forward(
         dec_start, dec_table, EH, rim, segments, key_ids, dec_share
@@ -1060,7 +1150,7 @@
         dec_out, dec_gain[2], dec_shift[2], mul_trans(pred_grad, dec_table["pix_w"])
     )
     start_grad, dec_small, dec_pairs = block_backward(
-        dec_out_grad, dec_table, EH, rim, segments, key_ids, dec_saved, dec_return, lambda grad: grad
+        dec_out_grad, dec_table, EH, rim, segments, key_ids, dec_saved
     )
     mask_grad = jnp.sum(jnp.where(seen[:, None], 0.0, start_grad), axis=0)
     latent_grad = own_rows(matmul(chosen, start_grad.astype(jnp.bfloat16)).astype(jnp.bfloat16))
@@ -1091,55 +1181,47 @@
         dec_blocks = reduce_first(dec_half, dec_routes(), (0.5,))
         return grad
 
+    def enc_settle(grad):
+        nonlocal dec_blocks
+        grad, dec_blocks = lax.optimization_barrier((grad, dec_blocks))
+        return grad
+
     enc_out_grad, enc_gain_last, enc_shift_last = norm_back(
         enc_out, enc_gain[2], enc_shift[2], mul_trans(latent_grad, dec_table["embed_w"])
     )
-    def enc_return(pair):
-        nonlocal dec_blocks
-        joined = own_rows(jnp.concatenate(pair, axis=1))
-        joined, dec_blocks = lax.optimization_barrier((joined, dec_blocks))
-        return (joined[:, :D], joined[:, D:])
-
-    enc_start_grad, enc_small, enc_pairs = block_backward(
-        enc_out_grad, enc_table, H, 0, own_ids, group_ids, enc_saved, enc_return, enc_pause
-    )
-    enc_norms = jnp.stack(
-        [
-            enc_small[0],
-            enc_small[2],
-            enc_gain_last,
-            enc_small[1],
-            enc_small[3],
-            enc_shift_last,
-            jnp.zeros_like(enc_shift_last),
-            jnp.zeros_like(enc_shift_last),
-        ]
-    )
-    enc_pairs["patch_w"] = (enc_input, enc_start_grad.astype(jnp.bfloat16))
-    names = ("patch_w", "qkv_w", "out_w", "up_w", "down_w")
-    places = [(3 * D + F, PATCH), (0, D), (D, D), (2 * D, D), (3 * D, F)]
+    enc_grads, enc_small = enc_backward(
+        enc_out_grad, enc_table, enc_start, group_ids, enc_saved, enc_pause, enc_settle
+    )
+    enc_norms = jnp.stack([enc_small[2], enc_gain_last, enc_small[3], enc_shift_last])
+    branch_grad, far_grad, enc_norms = lax.optimization_barrier(
+        (enc_grads[2], enc_grads[3], enc_norms)
+    )
     enc_quarter = enc_grad_quarter(
-        group_inputs,
-        places,
-        [group_rows(enc_pairs[name][1]) for name in names],
+        [enc_input, enc_saved[0], group_inputs],
+        [*enc_grads[:2], branch_grad, group_rows(far_grad)],
         group_rows(enc_norms),
+        jnp.stack([enc_small[0], enc_small[1]]),
         ER,
     )
     enc_blocks = reduce_first(enc_quarter, dp_routes(), (0.5,))
+    dec_blocks = reduce_rest(dec_blocks, dec_routes(), 1, 2)
     enc_sum = reduce_rest(enc_blocks, dp_routes())
-    dec_sum = reduce_rest(dec_blocks, dec_routes())
+    enc_sum, dec_blocks = lax.optimization_barrier((enc_sum, dec_blocks))
+    enc_own = jnp.concatenate(enc_sum, axis=0)
+    enc_across = swap(enc_own, "grp", 2)
+    dec_sum = reduce_rest(dec_blocks, dec_routes(), 2)
     squares = sum(jnp.sum(part * part) for part in enc_sum + dec_sum)
     lane = lax.broadcasted_iota(jnp.int32, (8, 128), 1)
-    enc_own = jnp.concatenate(enc_sum, axis=0)
-    enc_across = swap(enc_own, "grp", 2)
     sums = total(jnp.where(lane == 0, squares, jnp.where(lane == 1, loss_part, 0.0)))
-    enc_across, sums = lax.optimization_barrier((enc_across, sums))
+    dec_wide = [double(piece, 0, "grp", 2).reshape(-1, 128) for piece in dec_sum]
     enc_quarters = (
         enc_own,
         swap(enc_own, "grp", 1),
         enc_across,
         swap(enc_across, "grp", 1),
     )
+    dec_mine = jnp.concatenate(dec_wide, axis=0)
+    dec_halves = dec_mine, swap(dec_mine, "grp", 1)
     loss_total = sums[0, 1]
     grad_norm = jnp.sqrt(sums[0, 0])
     factor = jnp.minimum(1.0, CLIP_LIMIT / (grad_norm + NORM_EPS))
@@ -1148,7 +1230,7 @@
         enc_quarters, (enc_params, enc_first, enc_second, enc_average), factor, steps_done
     )
     dec_new, dec_first_new, dec_second_new, dec_copy_new = adamw(
-        spread_pieces(dec_sum), (dec_params, dec_first, dec_second), factor, steps_done
+        dec_halves, (dec_params, dec_first, dec_second), factor, steps_done
     )
     return (
         enc_new,

time: 823 us -> 775 us (0.942)
  waiting for transfers between devices: 342 us -> 306 us
  local copies, waits for them, and re-layouts: 83.3 us -> 67.4 us
  Pallas kernels: 141 us -> 155 us
  other arithmetic: 97.2 us -> 88.3 us
    ppermute x69 -> x58, waiting for transfers between devices: 246 us -> 214 us  [swap(): return lax.ppermute(block, axis, [(i, i ^ bit) for i in range(count)])]
    pallas_call x5 -> x6, Pallas kernels: 69.5 us -> 82.3 us  [the longest x3 50.2 us: attend_back(): pl.pallas_call(functools.partial(attend_back_kernel, window, stride, colu...]
    ppermute x2, waiting for transfers between devices: 9.54 us -> 0.01 us  [passed_along(): return lax.ppermute(block, axis, route)]
    concatenate x8 -> x5, other arithmetic: 17.1 us -> 7.66 us  [group_rows(): return jnp.concatenate([block, near, across, far], axis=0)]
    concatenate x4 -> x7, other arithmetic: 4.73 us -> 14.1 us  [the longest x1 11 us: attend_back_slots(): return jnp.concatenate([query_grad, middle], axis=1)]
    ppermute x69 -> x58, starting transfers between devices: 61.4 us -> 54.5 us  [swap(): return lax.ppermute(block, axis, [(i, i ^ bit) for i in range(count)])]
    unnamed x281 -> x239, local copies, waits for them, and re-layouts: 29.6 us -> 30.1 us
  transfers between devices with their start and end apart: 77 -> 66, of which waited for: 36 -> 30; matrix products, arithmetic and copies ran while one was open for 18% -> 15% of each run, Pallas kernels for 7% -> 11%
where the time goes in v3:
time: 775 us; the launch traced here: 765 us
  waiting for transfers between devices  306 us (39%)
  Pallas kernels  155 us (20%)
  other arithmetic  88.3 us (11%)
  starting transfers between devices  68.5 us (9%)
  local copies, waits for them, and re-layouts  67.4 us (9%)
  matrix products  57.2 us (7%)
  between operations  22.7 us (3%)
    ppermute x58, waiting for transfers between devices, swap(): return lax.ppermute(block, axis, [(i, i ^ bit) for i in range(count)])  214 us
    all_gather x2, waiting for transfers between devices, gather_quarters(): return lax.all_gather(quarter, ('dp', 'grp'), axis=0, tiled=True)  91.9 us
    ppermute x58, starting transfers between devices, swap(): return lax.ppermute(block, axis, [(i, i ^ bit) for i in range(count)])  54.5 us
    pallas_call x3, Pallas kernels, attend_back(): pl.pallas_call(functools.partial(attend_back_kernel, window, stride, colu...  50.2 us
    unnamed x239, local copies, waits for them, and re-layouts  30.1 us
    dot_general x13, matrix products, matmul(): return jnp.dot(left, right, preferred_element_type=jnp.float32)  28.7 us
    pallas_call x2, Pallas kernels, relayout(): pl.pallas_call(functools.partial(relayout_kernel, plan), in_specs=[anywhe...  28.1 us
    dot_general x10, matrix products, mul_trans(): lax.dot_general(left, right, (((1,), (1,)), ((), ())), preferred_element_...  26.8 us
  transfers between devices with their start and end apart: 66, of which 30 were waited for; matrix products, arithmetic and copies ran while one was open for 15% of the time, Pallas kernels for 11%

profile of v3, /device:TPU:0, one launch (start us, length us, event | category | flops | bytes accessed | tf_op | source)
XLA Modules:
  0.0 764.6 jit_solution(15122527249185234558)
XLA Ops:
  17.9 3.1 multiply_sine_fusion
  26.0 3.5 convolution_convert_fusion.2
  36.6 3.2 collective-permute-start.10
  44.3 13.3 %collective-permute-done.4 = bf16[96,1728]{1,0:T(8,128)(2,1)S(1)} collective-permute-done((bf16[96,1728]{1,0:T(8,128)(2,1)S(1)}, bf16[96,1728]{1,0:T(8,128)(2,1)S(1)}, u32[]{:S(2)}, u32[]{:S(2)}) %collective-permute-start.4) | collective-permute-done | bytes 331808 | tf_op jit(solution)/shard_map/ppermute | solution.py:37
  66.5 7.9 %collective-permute-done.6 = bf16[96,1728]{1,0:T(8,128)(2,1)S(1)} collective-permute-done((bf16[96,1728]{1,0:T(8,128)(2,1)S(1)}, bf16[96,1728]{1,0:T(8,128)(2,1)S(1)}, u32[]{:S(2)}, u32[]{:S(2)}) %collective-permute-start.6) | collective-permute-done | bytes 331808 | tf_op jit(solution)/shard_map/ppermute | solution.py:37
  74.4 3.2 collective-permute-start.16
  80.9 60.5 %all-gather.3.cloned.1.call-done.refs_0_ = bf16[66048,128]{1,0:T(8,128)(2,1)} async-done(((bf16[2064,128]{1,0:T(8,128)(2,1)}), bf16[66048,128]{1,0:T(8,128)(2,1)}) %all-gather.3.cloned.1.call-update) | async-done | bytes 16908304 | tf_op jit(solution)/shard_map/all_gather | solution.py:77
  146.4 18.9 %shard_map.202 = (bf16[1728,768]{1,0:T(8,128)(2,1)S(1)}, bf16[768,2304]{1,0:T(8,128)(2,1)S(1)}, bf16[768,768]{1,0:T(8,128)(2,1)S(1)}, bf16[768,3072]{1,0:T(8,128)(2,1)S(1)}, bf16[3072,768]{1,0:T(8,128)(2,1)}) custom-call(bf16[66048,128]{1,0:T(8,128)(2,1)} %all-gather.3.cloned.1.call-done.refs_0_), custom_call_target="tpu_custom_call" | custom-call | bytes 33816576 | tf_op jit(solution)/shard_map/pallas_call | solution.py:272
  172.7 3.2 fusion.65
  191.1 31.5 %all-gather.5.cloned.1.call-done.refs_0_ = bf16[34816,128]{1,0:T(8,128)(2,1)} async-done(((bf16[1088,128]{1,0:T(8,128)(2,1)}), bf16[34816,128]{1,0:T(8,128)(2,1)}) %all-gather.5.cloned.1.call-update) | async-done | bytes 8912912 | tf_op jit(solution)/shard_map/all_gather | solution.py:77
  223.9 9.2 %shard_map.204 = (bf16[768,512]{1,0:T(8,128)(2,1)S(1)}, bf16[512,1536]{1,0:T(8,128)(2,1)S(1)}, bf16[512,512]{1,0:T(8,128)(2,1)S(1)}, bf16[512,2048]{1,0:T(8,128)(2,1)S(1)}, bf16[2048,512]{1,0:T(8,128)(2,1)S(1)}) custom-call(bf16[34816,128]{1,0:T(8,128)(2,1)} %all-gather.5.cloned.1.call-done.refs_0_), custom_call_target="tpu_custom_call" | custom-call | bytes 17825792 | tf_op jit(solution)/shard_map/pallas_call | solution.py:272
  247.2 4.2 reshape.656
  263.6 3.1 collective-permute-start.23
  268.7 15.1 %shard_map.205 = bf16[896,512]{1,0:T(8,128)(2,1)S(1)} custom-call(bf16[896,512]{1,0:T(8,128)(2,1)S(1)} %pad.43.q_ref.refs_0_, bf16[1280,512]{1,0:T(8,128)(2,1)S(1)} %pad.44.k_ref.refs_2_, bf16[1280,512]{1,0:T(8,128)(2,1)S(1)} %pad.45.v_ref.refs_3_, s32[896,1]{1,0:T(8,128)S(1)} %copy-done.18, s32[1,1280]{1,0:T(1,128)S(1)} %broadcast_in_dim.89.kid_ref), custom_call_target="tpu_custom_call" | custom-call | flops 939524096 | bytes 5242880 | tf_op jit(solution)/shard_map/pallas_call | solution.py:502
  286.6 4.9 fusion.3
  294.6 7.2 collective-permute-start.24
  301.8 4.8 multiply_reduce_fusion
  307.3 3.4 pad_maximum_fusion.refs_2_
  310.7 5.8 divide_convert_fusion.refs_11_
  316.6 4.1 multiply_reduce_fusion.1
  321.7 3.9 multiply_convert_fusion.refs_7_
  325.6 5.1 multiply_reduce_fusion.2
  333.8 20.8 %shard_map.206 = (f32[896,512]{1,0:T(8,128)}, f32[1280,512]{1,0:T(8,128)}, f32[1280,512]{1,0:T(8,128)}) custom-call(bf16[896,512]{1,0:T(8,128)(2,1)S(1)} %pad.43.q_ref.refs_0_, bf16[896,512]{1,0:T(8,128)(2,1)S(1)} %pad.48.refs_1_, bf16[1280,512]{1,0:T(8,128)(2,1)S(1)} %pad.44.k_ref.refs_2_, bf16[1280,512]{1,0:T(8,128)(2,1)S(1)} %pad.45.v_ref.refs_3_, ...), custom_call_target="tpu_custom_call" | custom-call | flops 10737418240 | bytes 13107200 | tf_op jit(solution)/shard_map/pallas_call | solution.py:547
  360.2 4.4 collective-permute-start.25
  364.5 18.9 %shard_map.207 = (f32[896,512]{1,0:T(8,128)}, f32[1280,512]{1,0:T(8,128)}, f32[1280,512]{1,0:T(8,128)}) custom-call(bf16[896,512]{1,0:T(8,128)(2,1)S(1)} %pad.43.q_ref.refs_0_, bf16[896,512]{1,0:T(8,128)(2,1)S(1)} %pad.48.refs_1_, bf16[1280,512]{1,0:T(8,128)(2,1)S(1)} %pad.44.k_ref.refs_2_, bf16[1280,512]{1,0:T(8,128)(2,1)S(1)} %pad.45.v_ref.refs_3_, ...), custom_call_target="tpu_custom_call" | custom-call | flops 8053063680 | bytes 13107200 | tf_op jit(solution)/shard_map/pallas_call | solution.py:547
  390.6 11.0 %maximum_maximum_fusion.refs_3_ = bf16[864,1536]{1,0:T(8,128)(2,1)S(1)} fusion(bf16[192,1024]{1,0:T(8,128)(2,1)S(1)} %get-tuple-element.194, bf16[480,1024]{1,0:T(8,128)(2,1)S(1)} %slice.440, bf16[192,1024]{1,0:T(8,128)(2,1)S(1)} %get-tuple-element.193, bf16[224,512]{1,0:T(8,128)(2,1)S(1)} %slice-done.10, bf16[384,512]{1,0:T(8,128)(2,1)S(1)} %slice.441, ...), kind=kLoop, calls=%fused_computation.26 | loop fusion | flops 15925248 | bytes 5308416 | tf_op jit(solution)/shard_map/concatenate | solution.py:625
  410.6 3.4 collective-permute-done.28
  415.6 24.4 %shard_map.208 = (f32[17408,128]{1,0:T(8,128)}, f32[17408,128]{1,0:T(8,128)}) custom-call(s32[1]{0:T(128)} %bitcast.4.side_ref, bf16[96,768]{1,0:T(8,128)(2,1)} %copy-done.63, bf16[96,512]{1,0:T(8,128)(2,1)} %fusion.24.refs_1_, bf16[864,512]{1,0:T(8,128)(2,1)} %copy-done.59, bf16[864,1536]{1,0:T(8,128)(2,1)} %copy-done.47, bf16[864,512]{1,0:T(8,128)(2,1)} %slice.360.refs_4_, ...), custom_call_target="tpu_custom_call" | custom-call | flops 7700742144 | bytes 17825792 | tf_op jit(solution)/shard_map/pallas_call | solution.py:970
  442.4 4.8 fusion.8
  447.3 7.0 collective-permute-done.29
  454.4 4.5 add.616
  464.1 6.0 collective-permute-done.31
  474.6 10.4 %shard_map.209 = (f32[384,768]{1,0:T(8,128)S(1)}, f32[384,768]{1,0:T(8,128)S(1)}, f32[384,768]{1,0:T(8,128)S(1)}) custom-call(bf16[384,768]{1,0:T(8,128)(2,1)S(1)} %copy-done.15, bf16[384,768]{1,0:T(8,128)(2,1)S(1)} %convolution_convert_fusion.4.refs_1_, bf16[384,768]{1,0:T(8,128)(2,1)S(1)} %get-tuple-element.205.k_ref.refs_2_, ...), custom_call_target="tpu_custom_call" | custom-call | flops 9059696640 | bytes 5898240 | tf_op jit(solution)/shard_map/pallas_call | solution.py:547
  497.8 14.7 %collective-permute-done.33 = f32[2,2,1,1088,128]{4,3,2,1,0:T(8,128)} collective-permute-done((f32[2,2,1,1088,128]{4,3,2,1,0:T(8,128)S(1)}, f32[2,2,1,1088,128]{4,3,2,1,0:T(8,128)}, u32[]{:S(2)}, u32[]{:S(2)}) %collective-permute-start.33) | collective-permute-done | bytes 2228256 | tf_op jit(solution)/shard_map/ppermute | solution.py:37
  512.5 3.2 dynamic-slice_add_fusion.1
  515.7 3.3 dynamic-slice_add_fusion
  519.0 14.5 %shard_map.210 = f32[16512,128]{1,0:T(8,128)} custom-call(s32[2]{0:T(128)S(1)} %pad_add_fusion.4.place_ref, bf16[384,1728]{1,0:T(8,128)(2,1)S(1)} %pad_maximum_fusion.5.refs_0_, bf16[384,768]{1,0:T(8,128)(2,1)S(1)} %copy-done.5, bf16[384,4608]{1,0:T(8,128)(2,1)} %pad_maximum_fusion.refs_2_, bf16[384,768]{1,0:T(8,128)(2,1)S(1)} %add_convert_fusion.4.refs_3_, ...), custom_call_target="tpu_custom_call" | custom-call | flops 3246391296 | bytes 8454144 | tf_op jit(solution)/shard_map/pallas_call | solution.py:862
  540.2 43.9 %collective-permute-done.41 = f32[2,2,1,1024,128]{4,3,2,1,0:T(8,128)} collective-permute-done((f32[2,2,1,1024,128]{4,3,2,1,0:T(8,128)}, f32[2,2,1,1024,128]{4,3,2,1,0:T(8,128)}, u32[]{:S(2)}, u32[]{:S(2)}) %collective-permute-start.41) | collective-permute-done | bytes 2097184 | tf_op jit(solution)/shard_map/ppermute | solution.py:37
  598.6 31.5 %collective-permute-done.42 = f32[2,1,1,1024,128]{4,3,2,1,0:T(8,128)} collective-permute-done((f32[2,1,1,1024,128]{4,3,2,1,0:T(8,128)}, f32[2,1,1,1024,128]{4,3,2,1,0:T(8,128)}, u32[]{:S(2)}, u32[]{:S(2)}) %collective-permute-start.42) | collective-permute-done | bytes 1048608 | tf_op jit(solution)/shard_map/ppermute | solution.py:37
  631.6 22.8 %collective-permute-done.45 = f32[1,1,2,1040,128]{4,3,2,1,0:T(8,128)} collective-permute-done((f32[1,1,2,1040,128]{4,3,2,1,0:T(8,128)}, f32[1,1,2,1040,128]{4,3,2,1,0:T(8,128)}, u32[]{:S(2)}, u32[]{:S(2)}) %collective-permute-start.45) | collective-permute-done | bytes 1064992 | tf_op jit(solution)/shard_map/ppermute | solution.py:37
  657.6 5.5 collective-permute-done.43
  671.1 16.6 %collective-permute-done.51 = f32[1,1,2,544,128]{4,3,2,1,0:T(8,128)S(1)} collective-permute-done((f32[1,1,2,544,128]{4,3,2,1,0:T(8,128)S(1)}, f32[1,1,2,544,128]{4,3,2,1,0:T(8,128)S(1)}, u32[]{:S(2)}, u32[]{:S(2)}) %collective-permute-start.51) | collective-permute-done | bytes 557088 | tf_op jit(solution)/shard_map/ppermute | solution.py:37
  688.5 7.9 %collective-permute-done.52 = f32[1,1,1,544,128]{4,3,2,1,0:T(8,128)S(1)} collective-permute-done((f32[1,1,1,544,128]{4,3,2,1,0:T(8,128)S(1)}, f32[1,1,1,544,128]{4,3,2,1,0:T(8,128)S(1)}, u32[]{:S(2)}, u32[]{:S(2)}) %collective-permute-start.52) | collective-permute-done | bytes 278560 | tf_op jit(solution)/shard_map/ppermute | solution.py:37
  706.9 5.3 collective-permute-done.61
  722.5 3.5 collective-permute-done.56
  727.2 3.3 collective-permute-done.57
  736.4 14.7 %shard_map.211 = (f32[8256,128]{1,0:T(8,128)}, f32[8256,128]{1,0:T(8,128)}, f32[8256,128]{1,0:T(8,128)}, bf16[8256,128]{1,0:T(8,128)(2,1)}, f32[8256,128]{1,0:T(8,128)}) custom-call(s32[4]{0:T(128)S(1)} %pad_add_fusion.3.place_ref, f32[3]{0:T(128)S(1)} %pad_maximum_fusion.21.scalar_ref, f32[2064,128]{1,0:T(8,128)S(1)} %get-tuple-element.214.refs_0_, ...), custom_call_target="tpu_custom_call" | custom-call | tf_op jit(solution)/shard_map/pallas_call | solution.py:1031
  751.1 5.2 shard_map.212
  (589 shorter events, 211.3 us)
Async XLA Ops:
  7.2 134.2 %all-gather.3.cloned.1.call-start = ((), (), s32[]{:S(2)}) async-start(), calls=%async_computation | async-start | bytes 17436672 | tf_op jit(solution)/shard_map/all_gather | solution.py:77
  9.3 213.2 %all-gather.5.cloned.1.call-start = ((), (), s32[]{:S(2)}) async-start(), calls=%async_computation.1 | async-start | bytes 9191424 | tf_op jit(solution)/shard_map/all_gather | solution.py:77
  9.4 15.4 %collective-permute-start.1 = (s32[96]{0:T(128)}, s32[96]{0:T(128)S(1)}, u32[]{:S(2)}, u32[]{:S(2)}) collective-permute-start(s32[96]{0:T(128)} %param.13), channel_id=1, source_target_pairs={{0,2},{1,3},{2,0},{3,1},{4,6},{5,7},{6,4},{7,5},{8,10},{9,11},{10,... | collective-permute-start | bytes 1160 | tf_op jit(solution)/shard_map/ppermute | solution.py:37
  12.4 12.6 %collective-permute-start = (s32[96]{0:T(128)}, s32[96]{0:T(128)S(1)}, u32[]{:S(2)}, u32[]{:S(2)}) collective-permute-start(s32[96]{0:T(128)} %param.13), channel_id=1, source_target_pairs={{0,1},{1,0},{2,3},{3,2},{4,5},{5,4},{6,7},{7,6},{8,9},{9,8},{10,11... | collective-permute-start | bytes 1160 | tf_op jit(solution)/shard_map/ppermute | solution.py:37
  12.4 22.8 %collective-permute-start.8 = (s32[864]{0:T(1024)}, s32[864]{0:T(1024)S(1)}, u32[]{:S(2)}, u32[]{:S(2)}) collective-permute-start(s32[864]{0:T(1024)} %param.12), channel_id=1, source_target_pairs={{0,2},{1,3},{2,0},{3,1},{4,6},{5,7},{6,4},{7,5},{8,10},{9,11},{10,... | collective-permute-start | bytes 10376 | tf_op jit(solution)/shard_map/ppermute | solution.py:37
  15.1 27.7 %collective-permute-start.12 = (f32[8,128]{1,0:T(8,128)S(1)}, f32[8,128]{1,0:T(8,128)S(1)}, u32[]{:S(2)}, u32[]{:S(2)}) collective-permute-start(f32[8,128]{1,0:T(8,128)S(1)} %broadcast_in_dim.83), channel_id=1, source_target_pairs={{0,1},{1,0},{2,3},{3,2},{4,5},{5,4},{6,7},{7,6},{8,9},{9,8},{10,11... | collective-permute-start | bytes 12296 | tf_op jit(solution)/shard_map/ppermute | solution.py:37
  29.7 10.2 %collective-permute-start.3 = (bf16[192,1728]{1,0:T(8,128)(2,1)S(1)}, bf16[192,1728]{1,0:T(8,128)(2,1)S(1)}, u32[]{:S(2)}, u32[]{:S(2)}) collective-permute-start(bf16[192,1728]{1,0:T(8,128)(2,1)S(1)} %pad_maximum_fusion.13), channel_id=1, source_target_pairs={{0,1},{1,0},{2,3},{3,2},{4,5},{5,4},{6,7},{7,6},{8,9},{9,8},{10,11... | collective-permute-start | bytes 1990664 | tf_op jit(solution)/shard_map/ppermute | solution.py:37
  35.3 8.9 %collective-permute-start.11 = (s32[192]{0:T(256)S(1)}, s32[192]{0:T(256)S(1)}, u32[]{:S(2)}, u32[]{:S(2)}) collective-permute-start(s32[192]{0:T(256)S(1)} %get-tuple-element.242), channel_id=1, source_target_pairs={{1,0},{2,1},{3,2},{5,4},{6,5},{7,6},{9,8},{10,9},{11,10},{13,12},{... | collective-permute-start | bytes 2312 | tf_op jit(solution)/shard_map/ppermute | solution.py:176
  36.6 7.6 collective-permute-start.10
  40.8 16.8 %collective-permute-start.4 = (bf16[96,1728]{1,0:T(8,128)(2,1)S(1)}, bf16[96,1728]{1,0:T(8,128)(2,1)S(1)}, u32[]{:S(2)}, u32[]{:S(2)}) collective-permute-start(bf16[96,1728]{1,0:T(8,128)(2,1)S(1)} %slice_add_fusion.2), channel_id=1, source_target_pairs={{0,2},{1,3},{2,0},{3,1},{4,6},{5,7},{6,4},{7,5},{8,10},{9,11},{10,... | collective-permute-start | bytes 995336 | tf_op jit(solution)/shard_map/ppermute | solution.py:37
  42.7 31.7 %collective-permute-start.9 = (s32[2,864]{1,0:T(2,128)S(1)}, s32[2,864]{1,0:T(2,128)S(1)}, u32[]{:S(2)}, u32[]{:S(2)}) collective-permute-start(s32[2,864]{1,0:T(2,128)S(1)} %pad_add_fusion.1), channel_id=1, source_target_pairs={{0,1},{1,0},{2,3},{3,2},{4,5},{5,4},{6,7},{7,6},{8,9},{9,8},{10,11... | collective-permute-start | bytes 20744 | tf_op jit(solution)/shard_map/ppermute | solution.py:37
  42.8 18.4 %collective-permute-start.13 = (f32[8,128]{1,0:T(8,128)S(1)}, f32[8,128]{1,0:T(8,128)S(1)}, u32[]{:S(2)}, u32[]{:S(2)}) collective-permute-start(f32[8,128]{1,0:T(8,128)S(1)} %broadcast_add_fusion.1), channel_id=1, source_target_pairs={{0,2},{1,3},{2,0},{3,1},{4,6},{5,7},{6,4},{7,5},{8,10},{9,11},{10,... | collective-permute-start | bytes 12296 | tf_op jit(solution)/shard_map/ppermute | solution.py:37
  58.6 15.7 %collective-permute-start.6 = (bf16[96,1728]{1,0:T(8,128)(2,1)S(1)}, bf16[96,1728]{1,0:T(8,128)(2,1)S(1)}, u32[]{:S(2)}, u32[]{:S(2)}) collective-permute-start(bf16[96,1728]{1,0:T(8,128)(2,1)S(1)} %fusion.23), channel_id=1, source_target_pairs={{0,2},{1,3},{2,0},{3,1},{4,6},{5,7},{6,4},{7,5},{8,10},{9,11},{10,... | collective-permute-start | bytes 995336 | tf_op jit(solution)/shard_map/ppermute | solution.py:37
  64.8 9.6 %collective-permute-start.15 = (f32[8,128]{1,0:T(8,128)S(1)}, f32[8,128]{1,0:T(8,128)S(1)}, u32[]{:S(2)}, u32[]{:S(2)}) collective-permute-start(f32[8,128]{1,0:T(8,128)S(1)} %add.554), channel_id=1, source_target_pairs={{0,8},{4,12},{8,0},{12,4},{16,24},{20,28},{24,16},{28,20},{1,9},{5... | collective-permute-start | bytes 12296 | tf_op jit(solution)/shard_map/ppermute | solution.py:37
  66.5 14.3 %collective-permute-start.5 = (bf16[96,1728]{1,0:T(8,128)(2,1)S(1)}, bf16[96,1728]{1,0:T(8,128)(2,1)S(1)}, u32[]{:S(2)}, u32[]{:S(2)}) collective-permute-start(bf16[96,1728]{1,0:T(8,128)(2,1)S(1)} %fusion.23), channel_id=1, source_target_pairs={{0,1},{1,0},{2,3},{3,2},{4,5},{5,4},{6,7},{7,6},{8,9},{9,8},{10,11... | collective-permute-start | bytes 995336 | tf_op jit(solution)/shard_map/ppermute | solution.py:37
  239.9 11.5 %collective-permute-start.17 = (bf16[96,512]{1,0:T(8,128)(2,1)}, bf16[96,512]{1,0:T(8,128)(2,1)S(1)}, u32[]{:S(2)}, u32[]{:S(2)}) collective-permute-start(bf16[96,512]{1,0:T(8,128)(2,1)} %fusion.17), channel_id=1, source_target_pairs={{0,1},{1,0},{2,3},{3,2},{4,5},{5,4},{6,7},{7,6},{8,9},{9,8},{10,11... | collective-permute-start | bytes 294920 | tf_op jit(solution)/shard_map/ppermute | solution.py:37
  258.4 8.6 %collective-permute-start.20 = (bf16[192,1024]{1,0:T(8,128)(2,1)S(1)}, bf16[192,1024]{1,0:T(8,128)(2,1)S(1)}, u32[]{:S(2)}, u32[]{:S(2)}) collective-permute-start(bf16[192,1024]{1,0:T(8,128)(2,1)S(1)} %get-tuple-element.195), channel_id=1, source_target_pairs={{0,1},{1,2},{2,3},{4,5},{5,6},{6,7},{8,9},{9,10},{10,11},{12,13},{... | collective-permute-start | bytes 1179656 | tf_op jit(solution)/shard_map/ppermute | solution.py:174
  263.6 31.1 %collective-permute-start.23 = (bf16[96,4608]{1,0:T(8,128)(2,1)S(1)}, bf16[96,4608]{1,0:T(8,128)(2,1)}, u32[]{:S(2)}, u32[]{:S(2)}) collective-permute-start(bf16[96,4608]{1,0:T(8,128)(2,1)S(1)} %copy-done.46), channel_id=1, source_target_pairs={{0,2},{1,3},{2,0},{3,1},{4,6},{5,7},{6,4},{7,5},{8,10},{9,11},{10,... | collective-permute-start | bytes 2654216 | tf_op jit(solution)/shard_map/ppermute | solution.py:37
  266.7 40.6 %collective-permute-start.22 = (bf16[96,4608]{1,0:T(8,128)(2,1)S(1)}, bf16[96,4608]{1,0:T(8,128)(2,1)}, u32[]{:S(2)}, u32[]{:S(2)}) collective-permute-start(bf16[96,4608]{1,0:T(8,128)(2,1)S(1)} %copy-done.46), channel_id=1, source_target_pairs={{0,1},{1,0},{2,3},{3,2},{4,5},{5,4},{6,7},{7,6},{8,9},{9,8},{10,11... | collective-permute-start | bytes 2654216 | tf_op jit(solution)/shard_map/ppermute | solution.py:37
  294.6 12.6 %collective-permute-start.24 = (bf16[96,4608]{1,0:T(8,128)(2,1)}, bf16[96,4608]{1,0:T(8,128)(2,1)S(1)}, u32[]{:S(2)}, u32[]{:S(2)}) collective-permute-start(bf16[96,4608]{1,0:T(8,128)(2,1)} %collective-permute-done.23), channel_id=1, source_target_pairs={{0,1},{1,0},{2,3},{3,2},{4,5},{5,4},{6,7},{7,6},{8,9},{9,8},{10,11... | collective-permute-start | bytes 2654216 | tf_op jit(solution)/shard_map/ppermute | solution.py:37
  357.9 31.0 %collective-permute-start.26 = (f32[192,1024]{1,0:T(8,128)}, f32[192,1024]{1,0:T(8,128)}, u32[]{:S(2)}, u32[]{:S(2)}) collective-permute-start(f32[192,1024]{1,0:T(8,128)} %pad_maximum_fusion.11), channel_id=1, source_target_pairs={{1,0},{2,1},{3,2},{5,4},{6,5},{7,6},{9,8},{10,9},{11,10},{13,12},{... | collective-permute-start | bytes 2359304 | tf_op jit(solution)/shard_map/ppermute | solution.py:185
  360.2 28.8 %collective-permute-start.25 = (f32[192,1024]{1,0:T(8,128)}, f32[192,1024]{1,0:T(8,128)}, u32[]{:S(2)}, u32[]{:S(2)}) collective-permute-start(f32[192,1024]{1,0:T(8,128)} %pad_maximum_fusion.10), channel_id=1, source_target_pairs={{0,1},{1,2},{2,3},{4,5},{5,6},{6,7},{8,9},{9,10},{10,11},{12,13},{... | collective-permute-start | bytes 2359304 | tf_op jit(solution)/shard_map/ppermute | solution.py:185
  440.0 14.3 %collective-permute-start.29 = (f32[17408,128]{1,0:T(8,128)}, f32[17408,128]{1,0:T(8,128)}, u32[]{:S(2)}, u32[]{:S(2)}) collective-permute-start(f32[17408,128]{1,0:T(8,128)} %get-tuple-element.117), channel_id=1, source_target_pairs={{0,1},{1,0},{2,3},{3,2},{4,5},{5,4},{6,7},{7,6},{8,9},{9,8},{10,11... | collective-permute-start | bytes 26738696 | tf_op jit(solution)/shard_map/ppermute | solution.py:37
  461.0 9.1 %collective-permute-start.31 = (f32[96,768]{1,0:T(8,128)S(1)}, f32[96,768]{1,0:T(8,128)S(1)}, u32[]{:S(2)}, u32[]{:S(2)}) collective-permute-start(f32[96,768]{1,0:T(8,128)S(1)} %add_add_fusion.10), channel_id=1, source_target_pairs={{0,2},{1,3},{2,0},{3,1},{4,6},{5,7},{6,4},{7,5},{8,10},{9,11},{10,... | collective-permute-start | bytes 884744 | tf_op jit(solution)/shard_map/ppermute | solution.py:37
  461.3 8.8 %collective-permute-start.30 = (f32[96,768]{1,0:T(8,128)S(1)}, f32[96,768]{1,0:T(8,128)S(1)}, u32[]{:S(2)}, u32[]{:S(2)}) collective-permute-start(f32[96,768]{1,0:T(8,128)S(1)} %add_add_fusion.10), channel_id=1, source_target_pairs={{0,1},{1,0},{2,3},{3,2},{4,5},{5,4},{6,7},{7,6},{8,9},{9,8},{10,11... | collective-permute-start | bytes 884744 | tf_op jit(solution)/shard_map/ppermute | solution.py:37
  461.5 51.0 %collective-permute-start.33 = (f32[2,2,1,1088,128]{4,3,2,1,0:T(8,128)S(1)}, f32[2,2,1,1088,128]{4,3,2,1,0:T(8,128)}, u32[]{:S(2)}, u32[]{:S(2)}) collective-permute-start(f32[2,2,1,1088,128]{4,3,2,1,0:T(8,128)S(1)} %constant_dynamic-slice_fusion.13), channel_id=1, source_target_pairs={{0,4},{4,0},{8,12},{12,8},{16,20},{20,16},{24,28},{28,24},{1,5},{5... | collective-permute-start | bytes 6684680 | tf_op jit(solution)/shard_map/ppermute | solution.py:37
  462.5 53.2 %collective-permute-start.34 = (f32[2,1,2,1088,128]{4,3,2,1,0:T(8,128)S(1)}, f32[2,1,2,1088,128]{4,3,2,1,0:T(8,128)}, u32[]{:S(2)}, u32[]{:S(2)}) collective-permute-start(f32[2,1,2,1088,128]{4,3,2,1,0:T(8,128)S(1)} %constant_dynamic-slice_fusion.12), channel_id=1, source_target_pairs={{0,8},{4,12},{8,0},{12,4},{16,24},{20,28},{24,16},{28,20},{1,9},{5... | collective-permute-start | bytes 6684680 | tf_op jit(solution)/shard_map/ppermute | solution.py:37
  472.5 18.8 %collective-permute-start.36 = (bf16[96,3840]{1,0:T(8,128)(2,1)S(1)}, bf16[96,3840]{1,0:T(8,128)(2,1)}, u32[]{:S(2)}, u32[]{:S(2)}) collective-permute-start(bf16[96,3840]{1,0:T(8,128)(2,1)S(1)} %pad_maximum_fusion.12), channel_id=1, source_target_pairs={{0,2},{1,3},{2,0},{3,1},{4,6},{5,7},{6,4},{7,5},{8,10},{9,11},{10,... | collective-permute-start | bytes 2211848 | tf_op jit(solution)/shard_map/ppermute | solution.py:37
  472.8 21.9 %collective-permute-start.35 = (bf16[96,3840]{1,0:T(8,128)(2,1)S(1)}, bf16[96,3840]{1,0:T(8,128)(2,1)}, u32[]{:S(2)}, u32[]{:S(2)}) collective-permute-start(bf16[96,3840]{1,0:T(8,128)(2,1)S(1)} %pad_maximum_fusion.12), channel_id=1, source_target_pairs={{0,1},{1,0},{2,3},{3,2},{4,5},{5,4},{6,7},{7,6},{8,9},{9,8},{10,11... | collective-permute-start | bytes 2211848 | tf_op jit(solution)/shard_map/ppermute | solution.py:37
  472.8 18.9 %collective-permute-start.39 = (f32[4,768]{1,0:T(4,128)S(1)}, f32[4,768]{1,0:T(4,128)S(1)}, u32[]{:S(2)}, u32[]{:S(2)}) collective-permute-start(f32[4,768]{1,0:T(4,128)S(1)} %pad_maximum_fusion.19), channel_id=1, source_target_pairs={{0,2},{1,3},{2,0},{3,1},{4,6},{5,7},{6,4},{7,5},{8,10},{9,11},{10,... | collective-permute-start | bytes 36872 | tf_op jit(solution)/shard_map/ppermute | solution.py:37
  536.5 47.6 %collective-permute-start.41 = (f32[2,2,1,1024,128]{4,3,2,1,0:T(8,128)}, f32[2,2,1,1024,128]{4,3,2,1,0:T(8,128)}, u32[]{:S(2)}, u32[]{:S(2)}) collective-permute-start(f32[2,2,1,1024,128]{4,3,2,1,0:T(8,128)} %constant_dynamic-slice_fusion.11), channel_id=1, source_target_pairs={{0,4},{4,0},{8,12},{12,8},{16,20},{20,16},{24,28},{28,24},{1,5},{5... | collective-permute-start | bytes 6291464 | tf_op jit(solution)/shard_map/ppermute | solution.py:37
  538.7 50.5 %collective-permute-start.44 = (f32[2,1,2,1040,128]{4,3,2,1,0:T(8,128)S(1)}, f32[2,1,2,1040,128]{4,3,2,1,0:T(8,128)}, u32[]{:S(2)}, u32[]{:S(2)}) collective-permute-start(f32[2,1,2,1040,128]{4,3,2,1,0:T(8,128)S(1)} %constant_dynamic-slice_fusion.8), channel_id=1, source_target_pairs={{0,8},{4,12},{8,0},{12,4},{16,24},{20,28},{24,16},{28,20},{1,9},{5... | collective-permute-start | bytes 6389768 | tf_op jit(solution)/shard_map/ppermute | solution.py:37
  587.7 42.5 %collective-permute-start.42 = (f32[2,1,1,1024,128]{4,3,2,1,0:T(8,128)}, f32[2,1,1,1024,128]{4,3,2,1,0:T(8,128)}, u32[]{:S(2)}, u32[]{:S(2)}) collective-permute-start(f32[2,1,1,1024,128]{4,3,2,1,0:T(8,128)} %constant_dynamic-slice_fusion.10), channel_id=1, source_target_pairs={{0,8},{4,12},{8,0},{12,4},{16,24},{20,28},{24,16},{28,20},{1,9},{5... | collective-permute-start | bytes 3145736 | tf_op jit(solution)/shard_map/ppermute | solution.py:37
  592.7 61.7 %collective-permute-start.45 = (f32[1,1,2,1040,128]{4,3,2,1,0:T(8,128)}, f32[1,1,2,1040,128]{4,3,2,1,0:T(8,128)}, u32[]{:S(2)}, u32[]{:S(2)}) collective-permute-start(f32[1,1,2,1040,128]{4,3,2,1,0:T(8,128)} %constant_dynamic-slice_fusion.7), channel_id=1, source_target_pairs={{0,16},{4,20},{8,24},{12,28},{16,0},{20,4},{24,8},{28,12},{1,17},{... | collective-permute-start | bytes 3194888 | tf_op jit(solution)/shard_map/ppermute | solution.py:37
  595.1 61.1 %collective-permute-start.48 = (f32[2,1,2,544,128]{4,3,2,1,0:T(8,128)S(1)}, f32[2,1,2,544,128]{4,3,2,1,0:T(8,128)S(1)}, u32[]{:S(2)}, u32[]{:S(2)}) collective-permute-start(f32[2,1,2,544,128]{4,3,2,1,0:T(8,128)S(1)} %constant_dynamic-slice_fusion.4), channel_id=1, source_target_pairs={{0,2},{1,3},{2,0},{3,1},{4,6},{5,7},{6,4},{7,5},{8,10},{9,11},{10,... | collective-permute-start | bytes 3342344 | tf_op jit(solution)/shard_map/ppermute | solution.py:37
  598.3 58.1 %collective-permute-start.47 = (f32[2,2,1,544,128]{4,3,2,1,0:T(8,128)S(1)}, f32[2,2,1,544,128]{4,3,2,1,0:T(8,128)S(1)}, u32[]{:S(2)}, u32[]{:S(2)}) collective-permute-start(f32[2,2,1,544,128]{4,3,2,1,0:T(8,128)S(1)} %constant_dynamic-slice_fusion.5), channel_id=1, source_target_pairs={{0,2},{1,3},{2,0},{3,1},{4,6},{5,7},{6,4},{7,5},{8,10},{9,11},{10,... | collective-permute-start | bytes 3342344 | tf_op jit(solution)/shard_map/ppermute | solution.py:37
  631.5 31.6 %collective-permute-start.43 = (f32[1,1,1,1024,128]{4,3,2,1,0:T(8,128)S(1)}, f32[1,1,1,1024,128]{4,3,2,1,0:T(8,128)S(1)}, u32[]{:S(2)}, u32[]{:S(2)}) collective-permute-start(f32[1,1,1,1024,128]{4,3,2,1,0:T(8,128)S(1)} %constant_dynamic-slice_fusion.9), channel_id=1, source_target_pairs={{0,16},{4,20},{8,24},{12,28},{16,0},{20,4},{24,8},{28,12},{1,17},{... | collective-permute-start | bytes 1572872 | tf_op jit(solution)/shard_map/ppermute | solution.py:37
  655.8 9.3 %collective-permute-start.46 = (f32[1,1,1,1040,128]{4,3,2,1,0:T(8,128)S(1)}, f32[1,1,1,1040,128]{4,3,2,1,0:T(8,128)S(1)}, u32[]{:S(2)}, u32[]{:S(2)}) collective-permute-start(f32[1,1,1,1040,128]{4,3,2,1,0:T(8,128)S(1)} %constant_dynamic-slice_fusion.6), channel_id=1, source_target_pairs={{0,4},{4,0},{8,12},{12,8},{16,20},{20,16},{24,28},{28,24},{1,5},{5... | collective-permute-start | bytes 1597448 | tf_op jit(solution)/shard_map/ppermute | solution.py:37
  665.3 22.5 %collective-permute-start.51 = (f32[1,1,2,544,128]{4,3,2,1,0:T(8,128)S(1)}, f32[1,1,2,544,128]{4,3,2,1,0:T(8,128)S(1)}, u32[]{:S(2)}, u32[]{:S(2)}) collective-permute-start(f32[1,1,2,544,128]{4,3,2,1,0:T(8,128)S(1)} %constant_dynamic-slice_fusion.1), channel_id=1, source_target_pairs={{0,16},{4,20},{8,24},{12,28},{16,0},{20,4},{24,8},{28,12},{1,17},{... | collective-permute-start | bytes 1671176 | tf_op jit(solution)/shard_map/ppermute | solution.py:37
  665.4 22.9 %collective-permute-start.49 = (f32[2,1,1,544,128]{4,3,2,1,0:T(8,128)S(1)}, f32[2,1,1,544,128]{4,3,2,1,0:T(8,128)S(1)}, u32[]{:S(2)}, u32[]{:S(2)}) collective-permute-start(f32[2,1,1,544,128]{4,3,2,1,0:T(8,128)S(1)} %constant_dynamic-slice_fusion.3), channel_id=1, source_target_pairs={{0,8},{4,12},{8,0},{12,4},{16,24},{20,28},{24,16},{28,20},{1,9},{5... | collective-permute-start | bytes 1671176 | tf_op jit(solution)/shard_map/ppermute | solution.py:37
  669.4 37.3 %collective-permute-start.59 = (f32[2064,128]{1,0:T(8,128)S(1)}, f32[2064,128]{1,0:T(8,128)}, u32[]{:S(2)}, u32[]{:S(2)}) collective-permute-start(f32[2064,128]{1,0:T(8,128)S(1)} %get-tuple-element.214.refs_0_), channel_id=1, source_target_pairs={{0,2},{1,3},{2,0},{3,1},{4,6},{5,7},{6,4},{7,5},{8,10},{9,11},{10,... | collective-permute-start | bytes 3170312 | tf_op jit(solution)/shard_map/ppermute | solution.py:37
  687.9 8.6 %collective-permute-start.52 = (f32[1,1,1,544,128]{4,3,2,1,0:T(8,128)S(1)}, f32[1,1,1,544,128]{4,3,2,1,0:T(8,128)S(1)}, u32[]{:S(2)}, u32[]{:S(2)}) collective-permute-start(f32[1,1,1,544,128]{4,3,2,1,0:T(8,128)S(1)} %constant_dynamic-slice_fusion), channel_id=1, source_target_pairs={{0,4},{4,0},{8,12},{12,8},{16,20},{20,16},{24,28},{28,24},{1,5},{5... | collective-permute-start | bytes 835592 | tf_op jit(solution)/shard_map/ppermute | solution.py:37
  688.4 14.5 %collective-permute-start.50 = (f32[1,1,1,544,128]{4,3,2,1,0:T(8,128)S(1)}, f32[1,1,1,544,128]{4,3,2,1,0:T(8,128)S(1)}, u32[]{:S(2)}, u32[]{:S(2)}) collective-permute-start(f32[1,1,1,544,128]{4,3,2,1,0:T(8,128)S(1)} %constant_dynamic-slice_fusion.2), channel_id=1, source_target_pairs={{0,16},{4,20},{8,24},{12,28},{16,0},{20,4},{24,8},{28,12},{1,17},{... | collective-permute-start | bytes 835592 | tf_op jit(solution)/shard_map/ppermute | solution.py:37
  697.1 9.6 %collective-permute-start.62 = (f32[544,128]{1,0:T(8,128)S(1)}, f32[544,128]{1,0:T(8,128)S(1)}, u32[]{:S(2)}, u32[]{:S(2)}) collective-permute-start(f32[544,128]{1,0:T(8,128)S(1)} %get-tuple-element.161), channel_id=1, source_target_pairs={{0,2},{1,3},{2,0},{3,1},{4,6},{5,7},{6,4},{7,5},{8,10},{9,11},{10,... | collective-permute-start | bytes 835592 | tf_op jit(solution)/shard_map/ppermute | solution.py:37
  699.5 32.4 %collective-permute-start.58 = (f32[2064,128]{1,0:T(8,128)S(1)}, f32[2064,128]{1,0:T(8,128)}, u32[]{:S(2)}, u32[]{:S(2)}) collective-permute-start(f32[2064,128]{1,0:T(8,128)S(1)} %get-tuple-element.214.refs_0_), channel_id=1, source_target_pairs={{0,1},{1,0},{2,3},{3,2},{4,5},{5,4},{6,7},{7,6},{8,9},{9,8},{10,11... | collective-permute-start | bytes 3170312 | tf_op jit(solution)/shard_map/ppermute | solution.py:37
  703.6 8.6 %collective-permute-start.61 = (f32[544,128]{1,0:T(8,128)S(1)}, f32[544,128]{1,0:T(8,128)S(1)}, u32[]{:S(2)}, u32[]{:S(2)}) collective-permute-start(f32[544,128]{1,0:T(8,128)S(1)} %get-tuple-element.163), channel_id=1, source_target_pairs={{0,2},{1,3},{2,0},{3,1},{4,6},{5,7},{6,4},{7,5},{8,10},{9,11},{10,... | collective-permute-start | bytes 835592 | tf_op jit(solution)/shard_map/ppermute | solution.py:37
  706.7 25.3 %collective-permute-start.60 = (f32[2064,128]{1,0:T(8,128)}, f32[2064,128]{1,0:T(8,128)}, u32[]{:S(2)}, u32[]{:S(2)}) collective-permute-start(f32[2064,128]{1,0:T(8,128)} %collective-permute-done.59.refs_2_), channel_id=1, source_target_pairs={{0,1},{1,0},{2,3},{3,2},{4,5},{5,4},{6,7},{7,6},{8,9},{9,8},{10,11... | collective-permute-start | bytes 3170312 | tf_op jit(solution)/shard_map/ppermute | solution.py:37
  712.4 38.7 %collective-permute-start.63 = (f32[2176,128]{1,0:T(8,128)S(1)}, f32[2176,128]{1,0:T(8,128)S(1)}, u32[]{:S(2)}, u32[]{:S(2)}) collective-permute-start(f32[2176,128]{1,0:T(8,128)S(1)} %pad_maximum_fusion.8.refs_0_), channel_id=1, source_target_pairs={{0,1},{1,0},{2,3},{3,2},{4,5},{5,4},{6,7},{7,6},{8,9},{9,8},{10,11... | collective-permute-start | bytes 3342344 | tf_op jit(solution)/shard_map/ppermute | solution.py:37
  (140 other events, 1019.7 us)
Sparse Core Ops, SparseCore 0:
  11.5 129.7 all-gather.2
  144.7 77.7 all-gather.4

commit v4 on v3

--- a/solution.py
+++ b/solution.py
@@ -419,8 +419,9 @@
 
 def attend_back_kernel(window, stride, width, pick, *refs):
     q_ref, g_ref, k_ref, v_ref, qid_ref, kid_ref = refs[:6]
-    dq_ref, dk_ref, dv_ref, bias_ref, score_ref, grad_ref, prob_ref, back_ref = refs[-8:]
-    before = refs[6:-8]
+    dq_ref, both_ref, bias_ref, score_ref, grad_ref, prob_ref, back_ref = refs[-7:]
+    before = refs[6:-7]
+    columns = q_ref.shape[1]
     step = pl.program_id(0)
     start = pl.multiple_of(pick(step) * stride, BLOCK)
     scale = width ** (-0.5)
@@ -428,8 +429,7 @@
 
     @pl.when(step == 0)
     def _():
-        dk_ref[...] = before[0][...] if before else jnp.zeros_like(dk_ref)
-        dv_ref[...] = before[1][...] if before else jnp.zeros_like(dv_ref)
+        both_ref[...] = before[0][...] if before else jnp.zeros_like(both_ref)
 
     near = pl.ds(start, window)
     bias_ref[...] = jnp.where(kid_ref[near, :] == qid_ref[...], 0.0, MASK_FILL)
@@ -469,8 +469,9 @@
                     probs * (grad_ref[slot, tile, head] - shared)
                 ).astype(jnp.bfloat16)
         back = back_ref[slot]
-        dv_ref[near, lanes] += matmul(prob_ref[slot], outs)
-        dk_ref[near, lanes] += matmul(back, queries) * scale
+        far_lanes = slice(columns + group * 128, columns + (group + 1) * 128)
+        both_ref[near, far_lanes] += matmul(prob_ref[slot], outs)
+        both_ref[near, lanes] += matmul(back, queries) * scale
         dq_ref[:, lanes] = pick_heads(trans_mul(back, keys), masks) * scale
 
 
@@ -555,13 +556,13 @@
             pl.BlockSpec((1, BLOCK), lambda i: (0, pick(i))),
             whole_spec((span, 1)),
         ]
-        + [whole_spec((span, columns))] * len(before),
-        out_specs=[block, whole_spec((span, columns)), whole_spec((span, columns))],
+        + ([whole_spec((span, 2 * columns)), pl.BlockSpec(memory_space=pl.ANY)] if before else []),
+        out_specs=[block, whole_spec((span, 2 * columns))],
         out_shape=[
             jax.ShapeDtypeStruct((all_steps * BLOCK, columns), jnp.float32),
-            jax.ShapeDtypeStruct((span, columns), jnp.float32),
-            jax.ShapeDtypeStruct((span, columns), jnp.float32),
+            jax.ShapeDtypeStruct((span, 2 * columns), jnp.float32),
         ],
+        input_output_aliases={7: 0} if before else {},
         scratch_shapes=[
             pltpu.VMEM((window, BLOCK), jnp.float32),
             pltpu.VMEM((2, window, stack), jnp.float32),
@@ -595,33 +596,16 @@
     edges = attend_back(
         *args, steps=low + steps - high, pick=lambda i: i + (i // low) * (high - low)
     )
-    ends = slice(rim + count, 2 * rim + count)
-    from_upper = passed_along(
-        jnp.concatenate([edges[1][:rim], edges[2][:rim]], axis=1), "grp", -1
-    )
-    from_lower = passed_along(
-        jnp.concatenate([edges[1][ends], edges[2][ends]], axis=1), "grp", 1
-    )
+    from_upper = passed_along(edges[1][:rim], "grp", -1)
+    from_lower = passed_along(edges[1][rim + count : 2 * rim + count], "grp", 1)
     inner = attend_back(
-        *args, steps=high - low, pick=lambda i: i + low, before=(edges[1], edges[2])
-    )
-    query_grad = jnp.concatenate(
-        [
-            edges[0][: low * BLOCK],
-            inner[0][low * BLOCK : high * BLOCK],
-            edges[0][high * BLOCK : count],
-        ],
-        axis=0,
-    )
-    middle = jnp.concatenate([inner[1], inner[2]], axis=1)[rim : rim + count]
-    middle = jnp.concatenate(
-        [
-            middle[:rim] + from_lower,
-            middle[rim : count - rim],
-            middle[count - rim :] + from_upper,
-        ],
-        axis=0,
-    )
+        *args, steps=high - low, pick=lambda i: i + low, before=(edges[1], edges[0])
+    )
+    rims = jnp.pad(from_lower, ((0, count - rim), (0, 0))) + jnp.pad(
+        from_upper, ((count - rim, 0), (0, 0))
+    )
+    middle = (inner[1][rim : rim + count] + rims).astype(jnp.bfloat16)
+    query_grad = inner[0][:count].astype(jnp.bfloat16)
     return jnp.concatenate([query_grad, middle], axis=1)
 
 
@@ -694,7 +678,7 @@
     attended_grad = mul_trans(branch_grad, table["out_w"]).astype(jnp.bfloat16)
     qkv_grad = attend_back_slots(
         query, all_keys, all_values, query_ids, key_ids, heads, rim, attended_grad
-    ).astype(jnp.bfloat16)
+    )
     pairs["qkv_w"] = (normed_one, qkv_grad)
     input_part, gain_one, shift_one = norm_back(
         inputs, gains[0], shifts[0], mul_trans(qkv_grad, table["qkv_w"])
@@ -718,7 +702,7 @@
     return result, (normed_one, qkv, attended, mixed, normed_two, slope, activated)
 
 
-def enc_backward(grad_out, table, inputs, ids, saved, pause, settle):
+def enc_backward(grad_out, table, inputs, ids, saved, pause):
     normed_one, qkv, attended, mixed, normed_two, slope, activated = saved
     gains = table["norm_g"].astype(jnp.float32)
     shifts = table["norm_b"].astype(jnp.float32)
@@ -738,7 +722,7 @@
     input_part, gain_one, shift_one = norm_back(
         inputs, gains[0], shifts[0], mul_trans(qkv_grad, table["qkv_w"])
     )
-    patch_grad = settle((mixed_grad + input_part).astype(jnp.bfloat16))
+    patch_grad = (mixed_grad + input_part).astype(jnp.bfloat16)
     return (
         (patch_grad, qkv_grad, branch_grad, jnp.concatenate([hidden_grad, down_grad], axis=1)),
         (gain_one, shift_one, gain_two, shift_two),
@@ -1181,16 +1165,11 @@
         dec_blocks = reduce_first(dec_half, dec_routes(), (0.5,))
         return grad
 
-    def enc_settle(grad):
-        nonlocal dec_blocks
-        grad, dec_blocks = lax.optimization_barrier((grad, dec_blocks))
-        return grad
-
     enc_out_grad, enc_gain_last, enc_shift_last = norm_back(
         enc_out, enc_gain[2], enc_shift[2], mul_trans(latent_grad, dec_table["embed_w"])
     )
     enc_grads, enc_small = enc_backward(
-        enc_out_grad, enc_table, enc_start, group_ids, enc_saved, enc_pause, enc_settle
+        enc_out_grad, enc_table, enc_start, group_ids, enc_saved, enc_pause
     )
     enc_norms = jnp.stack([enc_small[2], enc_gain_last, enc_small[3], enc_shift_last])
     branch_grad, far_grad, enc_norms = lax.optimization_barrier(
@@ -1203,6 +1182,7 @@
         jnp.stack([enc_small[0], enc_small[1]]),
         ER,
     )
+    enc_quarter, dec_blocks = lax.optimization_barrier((enc_quarter, dec_blocks))
     enc_blocks = reduce_first(enc_quarter, dp_routes(), (0.5,))
     dec_blocks = reduce_rest(dec_blocks, dec_routes(), 1, 2)
     enc_sum = reduce_rest(enc_blocks, dp_routes())

time: 775 us -> 747 us (0.964)
  other arithmetic: 88.3 us -> 78.7 us
  local copies, waits for them, and re-layouts: 67.4 us -> 58.9 us
    ppermute x58, waiting for transfers between devices: 214 us -> 202 us  [swap(): return lax.ppermute(block, axis, [(i, i ^ bit) for i in range(count)])]
    concatenate x1, other arithmetic: 11 us -> 1.69 us  [attend_back_slots(): return jnp.concatenate([query_grad, middle], axis=1)]
    unnamed x239 -> x208, local copies, waits for them, and re-layouts: 30.1 us -> 21.6 us
  transfers between devices with their start and end apart: 66 -> 66, of which waited for: 30 -> 30; matrix products, arithmetic and copies ran while one was open for 15% -> 15% of each run, Pallas kernels for 11% -> 13%
where the time goes in v4:
time: 747 us; the launch traced here: 737 us
  waiting for transfers between devices  301 us (40%)
  Pallas kernels  156 us (21%)
  other arithmetic  78.7 us (11%)
  starting transfers between devices  61.9 us (8%)
  local copies, waits for them, and re-layouts  58.9 us (8%)
  matrix products  58.6 us (8%)
  between operations  22.2 us (3%)
    ppermute x58, waiting for transfers between devices, swap(): return lax.ppermute(block, axis, [(i, i ^ bit) for i in range(count)])  202 us
    all_gather x2, waiting for transfers between devices, gather_quarters(): return lax.all_gather(quarter, ('dp', 'grp'), axis=0, tiled=True)  98.5 us
    pallas_call x3, Pallas kernels, attend_back(): pl.pallas_call(functools.partial(attend_back_kernel, window, stride, colu...  51.1 us
    ppermute x58, starting transfers between devices, swap(): return lax.ppermute(block, axis, [(i, i ^ bit) for i in range(count)])  50.3 us
    dot_general x13, matrix products, matmul(): return jnp.dot(left, right, preferred_element_type=jnp.float32)  30.1 us
    pallas_call x2, Pallas kernels, relayout(): pl.pallas_call(functools.partial(relayout_kernel, plan), in_specs=[anywhe...  27.9 us
    dot_general x10, matrix products, mul_trans(): lax.dot_general(left, right, (((1,), (1,)), ((), ())), preferred_element_...  26.9 us
    pallas_call x1, Pallas kernels, dec_grad_halves(): pl.pallas_call(functools.partial(dec_grad_kernel, plan), in_specs=[pl.Blo...  24.8 us
  transfers between devices with their start and end apart: 66, of which 30 were waited for; matrix products, arithmetic and copies ran while one was open for 15% of the time, Pallas kernels for 13%

profile of v4, /device:TPU:0, one launch (start us, length us, event | category | flops | bytes accessed | tf_op | source)
XLA Modules:
  0.0 736.8 jit_solution(7054659528397077067)
XLA Ops:
  9.4 3.0 collective-permute-start.1
  18.0 3.1 multiply_sine_fusion
  52.3 11.0 %collective-permute-done.6 = bf16[96,1728]{1,0:T(8,128)(2,1)S(1)} collective-permute-done((bf16[96,1728]{1,0:T(8,128)(2,1)S(1)}, bf16[96,1728]{1,0:T(8,128)(2,1)S(1)}, u32[]{:S(2)}, u32[]{:S(2)}) %collective-permute-start.6) | collective-permute-done | bytes 331808 | tf_op jit(solution)/shard_map/ppermute | solution.py:37
  63.4 2.9 collective-permute-start.16
  69.6 67.7 %all-gather.3.cloned.1.call-done.refs_0_ = bf16[66048,128]{1,0:T(8,128)(2,1)} async-done(((bf16[2064,128]{1,0:T(8,128)(2,1)}), bf16[66048,128]{1,0:T(8,128)(2,1)}) %all-gather.3.cloned.1.call-update) | async-done | bytes 16908304 | tf_op jit(solution)/shard_map/all_gather | solution.py:77
  141.2 18.7 %shard_map.202 = (bf16[1728,768]{1,0:T(8,128)(2,1)S(1)}, bf16[768,2304]{1,0:T(8,128)(2,1)S(1)}, bf16[768,768]{1,0:T(8,128)(2,1)S(1)}, bf16[768,3072]{1,0:T(8,128)(2,1)S(1)}, bf16[3072,768]{1,0:T(8,128)(2,1)}) custom-call(bf16[66048,128]{1,0:T(8,128)(2,1)} %all-gather.3.cloned.1.call-done.refs_0_), custom_call_target="tpu_custom_call" | custom-call | bytes 33816576 | tf_op jit(solution)/shard_map/pallas_call | solution.py:272
  176.0 4.9 fusion.14
  182.2 3.6 fusion.65
  187.8 30.7 %all-gather.5.cloned.1.call-done.refs_0_ = bf16[34816,128]{1,0:T(8,128)(2,1)} async-done(((bf16[1088,128]{1,0:T(8,128)(2,1)}), bf16[34816,128]{1,0:T(8,128)(2,1)}) %all-gather.5.cloned.1.call-update) | async-done | bytes 8912912 | tf_op jit(solution)/shard_map/all_gather | solution.py:77
  218.5 9.3 %shard_map.204 = (bf16[768,512]{1,0:T(8,128)(2,1)S(1)}, bf16[512,1536]{1,0:T(8,128)(2,1)S(1)}, bf16[512,512]{1,0:T(8,128)(2,1)S(1)}, bf16[512,2048]{1,0:T(8,128)(2,1)S(1)}, bf16[2048,512]{1,0:T(8,128)(2,1)S(1)}) custom-call(bf16[34816,128]{1,0:T(8,128)(2,1)} %all-gather.5.cloned.1.call-done.refs_0_), custom_call_target="tpu_custom_call" | custom-call | bytes 17825792 | tf_op jit(solution)/shard_map/pallas_call | solution.py:272
  236.8 3.0 collective-permute-done.18
  243.2 4.2 reshape.656
  259.2 3.1 collective-permute-start.23
  265.4 15.1 %shard_map.205 = bf16[896,512]{1,0:T(8,128)(2,1)S(1)} custom-call(bf16[896,512]{1,0:T(8,128)(2,1)S(1)} %pad.51.q_ref.refs_0_, bf16[1280,512]{1,0:T(8,128)(2,1)S(1)} %pad.52.k_ref.refs_2_, bf16[1280,512]{1,0:T(8,128)(2,1)S(1)} %pad.53.v_ref.refs_3_, s32[896,1]{1,0:T(8,128)S(1)} %copy-done.18, s32[1,1280]{1,0:T(1,128)S(1)} %broadcast_in_dim.89.kid_ref), custom_call_target="tpu_custom_call" | custom-call | flops 939524096 | bytes 5242880 | tf_op jit(solution)/shard_map/pallas_call | solution.py:503
  283.4 4.9 fusion.3
  291.4 5.8 collective-permute-start.24
  297.3 4.7 multiply_reduce_fusion
  302.7 3.6 pad_maximum_fusion.refs_2_
  306.3 5.8 divide_convert_fusion.refs_11_
  312.1 4.1 multiply_reduce_fusion.1
  317.3 3.8 multiply_convert_fusion.refs_7_
  321.1 5.1 multiply_reduce_fusion.2
  329.9 21.4 %shard_map.206 = (f32[896,512]{1,0:T(8,128)}, f32[1280,1024]{1,0:T(8,128)}) custom-call(bf16[896,512]{1,0:T(8,128)(2,1)S(1)} %pad.51.q_ref.refs_0_, bf16[896,512]{1,0:T(8,128)(2,1)S(1)} %pad.56.refs_1_, bf16[1280,512]{1,0:T(8,128)(2,1)S(1)} %pad.52.k_ref.refs_2_, bf16[1280,512]{1,0:T(8,128)(2,1)S(1)} %pad.53.v_ref.refs_3_, ...), custom_call_target="tpu_custom_call" | custom-call | flops 10737418240 | bytes 13107200 | tf_op jit(solution)/shard_map/pallas_call | solution.py:548
  358.0 19.3 %shard_map.207 = (f32[896,512]{1,0:T(8,128)}, f32[1280,1024]{1,0:T(8,128)}) custom-call(bf16[896,512]{1,0:T(8,128)(2,1)S(1)} %pad.51.q_ref.refs_0_, bf16[896,512]{1,0:T(8,128)(2,1)S(1)} %pad.56.refs_1_, bf16[1280,512]{1,0:T(8,128)(2,1)S(1)} %pad.52.k_ref.refs_2_, bf16[1280,512]{1,0:T(8,128)(2,1)S(1)} %pad.53.v_ref.refs_3_, ...), custom_call_target="tpu_custom_call", output_to_operand_aliasing={{0}: (7, {})} | custom-call | flops 8053063680 | bytes 13107200 | tf_op jit(solution)/shard_map/pallas_call | solution.py:548
  396.4 24.8 %shard_map.208 = (f32[17408,128]{1,0:T(8,128)}, f32[17408,128]{1,0:T(8,128)}) custom-call(s32[1]{0:T(128)} %bitcast.4.side_ref, bf16[96,768]{1,0:T(8,128)(2,1)} %add_convert_fusion.7.refs_0_, bf16[96,512]{1,0:T(8,128)(2,1)} %fusion.22.refs_1_, bf16[864,512]{1,0:T(8,128)(2,1)} %copy-done.53, bf16[864,1536]{1,0:T(8,128)(2,1)} %pad_maximum_fusion.2.refs_3_, ...), custom_call_target="tpu_custom_call" | custom-call | flops 7700742144 | bytes 17825792 | tf_op jit(solution)/shard_map/pallas_call | solution.py:954
  423.6 4.8 fusion.8
  428.5 7.0 collective-permute-done.29
  435.5 4.5 add.620
  455.2 10.4 %shard_map.209 = (f32[384,768]{1,0:T(8,128)S(1)}, f32[384,1536]{1,0:T(8,128)S(1)}) custom-call(bf16[384,768]{1,0:T(8,128)(2,1)S(1)} %copy-done.15, bf16[384,768]{1,0:T(8,128)(2,1)S(1)} %convolution_convert_fusion.4.refs_1_, bf16[384,768]{1,0:T(8,128)(2,1)S(1)} %get-tuple-element.195.k_ref.refs_2_, bf16[384,768]{1,0:T(8,128)(2,1)S(1)} %get-tuple-element.194.v_ref.refs_3_, ...), custom_call_target="tpu_custom_call" | custom-call | flops 9059696640 | bytes 5898240 | tf_op jit(solution)/shard_map/pallas_call | solution.py:548
  475.8 2.9 pad_maximum_fusion.1.refs_6_
  478.7 14.5 %shard_map.210 = f32[16512,128]{1,0:T(8,128)} custom-call(s32[2]{0:T(128)S(1)} %pad_add_fusion.4.place_ref, bf16[384,1728]{1,0:T(8,128)(2,1)S(1)} %pad_maximum_fusion.6.refs_0_, bf16[384,768]{1,0:T(8,128)(2,1)S(1)} %copy-done.5, bf16[384,4608]{1,0:T(8,128)(2,1)} %pad_maximum_fusion.refs_2_, bf16[384,768]{1,0:T(8,128)(2,1)S(1)} %add_convert_fusion.5.refs_3_, ...), custom_call_target="tpu_custom_call" | custom-call | flops 3246391296 | bytes 8454144 | tf_op jit(solution)/shard_map/pallas_call | solution.py:846
  493.2 3.2 collective-permute-done.40
  496.5 4.0 dynamic-slice_add_fusion
  500.5 3.0 dynamic-slice_add_fusion.1
  508.4 44.2 %collective-permute-done.41 = f32[2,2,1,1024,128]{4,3,2,1,0:T(8,128)} collective-permute-done((f32[2,2,1,1024,128]{4,3,2,1,0:T(8,128)}, f32[2,2,1,1024,128]{4,3,2,1,0:T(8,128)}, u32[]{:S(2)}, u32[]{:S(2)}) %collective-permute-start.41) | collective-permute-done | bytes 2097184 | tf_op jit(solution)/shard_map/ppermute | solution.py:37
  566.3 32.1 %collective-permute-done.42 = f32[2,1,1,1024,128]{4,3,2,1,0:T(8,128)} collective-permute-done((f32[2,1,1,1024,128]{4,3,2,1,0:T(8,128)}, f32[2,1,1,1024,128]{4,3,2,1,0:T(8,128)}, u32[]{:S(2)}, u32[]{:S(2)}) %collective-permute-start.42) | collective-permute-done | bytes 1048608 | tf_op jit(solution)/shard_map/ppermute | solution.py:37
  599.9 23.2 %collective-permute-done.45 = f32[1,1,2,1040,128]{4,3,2,1,0:T(8,128)} collective-permute-done((f32[1,1,2,1040,128]{4,3,2,1,0:T(8,128)S(1)}, f32[1,1,2,1040,128]{4,3,2,1,0:T(8,128)}, u32[]{:S(2)}, u32[]{:S(2)}) %collective-permute-start.45) | collective-permute-done | bytes 1064992 | tf_op jit(solution)/shard_map/ppermute | solution.py:37
  625.2 6.5 collective-permute-done.43
  638.3 17.0 %collective-permute-done.49 = f32[2,1,1,544,128]{4,3,2,1,0:T(8,128)S(1)} collective-permute-done((f32[2,1,1,544,128]{4,3,2,1,0:T(8,128)S(1)}, f32[2,1,1,544,128]{4,3,2,1,0:T(8,128)S(1)}, u32[]{:S(2)}, u32[]{:S(2)}) %collective-permute-start.49) | collective-permute-done | bytes 557088 | tf_op jit(solution)/shard_map/ppermute | solution.py:37
  657.8 11.5 %collective-permute-done.50 = f32[1,1,1,544,128]{4,3,2,1,0:T(8,128)S(1)} collective-permute-done((f32[1,1,1,544,128]{4,3,2,1,0:T(8,128)S(1)}, f32[1,1,1,544,128]{4,3,2,1,0:T(8,128)S(1)}, u32[]{:S(2)}, u32[]{:S(2)}) %collective-permute-start.50) | collective-permute-done | bytes 278560 | tf_op jit(solution)/shard_map/ppermute | solution.py:37
  676.4 3.1 collective-permute-done.61
  679.6 4.9 collective-permute-done.62
  687.8 3.3 collective-permute-done.54
  691.5 3.2 collective-permute-done.55
  694.9 3.5 collective-permute-done.56
  699.6 3.3 collective-permute-done.57
  708.7 14.7 %shard_map.211 = (f32[8256,128]{1,0:T(8,128)}, f32[8256,128]{1,0:T(8,128)}, f32[8256,128]{1,0:T(8,128)}, bf16[8256,128]{1,0:T(8,128)(2,1)}, f32[8256,128]{1,0:T(8,128)}) custom-call(s32[4]{0:T(128)S(1)} %pad_add_fusion.3.place_ref, f32[3]{0:T(128)S(1)} %pad_maximum_fusion.20.scalar_ref, f32[2064,128]{1,0:T(8,128)S(1)} %get-tuple-element.204.refs_0_, ...), custom_call_target="tpu_custom_call" | custom-call | tf_op jit(solution)/shard_map/pallas_call | solution.py:1015
  723.4 5.3 shard_map.212
  (545 shorter events, 200.8 us)
Async XLA Ops:
  7.2 130.1 %all-gather.3.cloned.1.call-start = ((), (), s32[]{:S(2)}) async-start(), calls=%async_computation | async-start | bytes 17436672 | tf_op jit(solution)/shard_map/all_gather | solution.py:77
  9.3 209.2 %all-gather.5.cloned.1.call-start = ((), (), s32[]{:S(2)}) async-start(), calls=%async_computation.1 | async-start | bytes 9191424 | tf_op jit(solution)/shard_map/all_gather | solution.py:77
  9.4 15.4 %collective-permute-start.1 = (s32[96]{0:T(128)}, s32[96]{0:T(128)S(1)}, u32[]{:S(2)}, u32[]{:S(2)}) collective-permute-start(s32[96]{0:T(128)} %param.13), channel_id=1, source_target_pairs={{0,2},{1,3},{2,0},{3,1},{4,6},{5,7},{6,4},{7,5},{8,10},{9,11},{10,... | collective-permute-start | bytes 1160 | tf_op jit(solution)/shard_map/ppermute | solution.py:37
  12.4 12.7 %collective-permute-start = (s32[96]{0:T(128)}, s32[96]{0:T(128)S(1)}, u32[]{:S(2)}, u32[]{:S(2)}) collective-permute-start(s32[96]{0:T(128)} %param.13), channel_id=1, source_target_pairs={{0,1},{1,0},{2,3},{3,2},{4,5},{5,4},{6,7},{7,6},{8,9},{9,8},{10,11... | collective-permute-start | bytes 1160 | tf_op jit(solution)/shard_map/ppermute | solution.py:37
  12.4 20.9 %collective-permute-start.8 = (s32[864]{0:T(1024)}, s32[864]{0:T(1024)S(1)}, u32[]{:S(2)}, u32[]{:S(2)}) collective-permute-start(s32[864]{0:T(1024)} %param.12), channel_id=1, source_target_pairs={{0,2},{1,3},{2,0},{3,1},{4,6},{5,7},{6,4},{7,5},{8,10},{9,11},{10,... | collective-permute-start | bytes 10376 | tf_op jit(solution)/shard_map/ppermute | solution.py:37
  15.1 24.3 %collective-permute-start.12 = (f32[8,128]{1,0:T(8,128)S(1)}, f32[8,128]{1,0:T(8,128)S(1)}, u32[]{:S(2)}, u32[]{:S(2)}) collective-permute-start(f32[8,128]{1,0:T(8,128)S(1)} %broadcast_in_dim.83), channel_id=1, source_target_pairs={{0,1},{1,0},{2,3},{3,2},{4,5},{5,4},{6,7},{7,6},{8,9},{9,8},{10,11... | collective-permute-start | bytes 12296 | tf_op jit(solution)/shard_map/ppermute | solution.py:37
  33.4 29.9 %collective-permute-start.9 = (s32[2,864]{1,0:T(2,128)S(1)}, s32[2,864]{1,0:T(2,128)S(1)}, u32[]{:S(2)}, u32[]{:S(2)}) collective-permute-start(s32[2,864]{1,0:T(2,128)S(1)} %pad_add_fusion.1), channel_id=1, source_target_pairs={{0,1},{1,0},{2,3},{3,2},{4,5},{5,4},{6,7},{7,6},{8,9},{9,8},{10,11... | collective-permute-start | bytes 20744 | tf_op jit(solution)/shard_map/ppermute | solution.py:37
  33.8 10.4 %collective-permute-start.4 = (bf16[96,1728]{1,0:T(8,128)(2,1)S(1)}, bf16[96,1728]{1,0:T(8,128)(2,1)S(1)}, u32[]{:S(2)}, u32[]{:S(2)}) collective-permute-start(bf16[96,1728]{1,0:T(8,128)(2,1)S(1)} %slice_add_fusion), channel_id=1, source_target_pairs={{0,2},{1,3},{2,0},{3,1},{4,6},{5,7},{6,4},{7,5},{8,10},{9,11},{10,... | collective-permute-start | bytes 995336 | tf_op jit(solution)/shard_map/ppermute | solution.py:37
  35.7 6.4 collective-permute-start.10
  39.4 7.6 %collective-permute-start.13 = (f32[8,128]{1,0:T(8,128)S(1)}, f32[8,128]{1,0:T(8,128)S(1)}, u32[]{:S(2)}, u32[]{:S(2)}) collective-permute-start(f32[8,128]{1,0:T(8,128)S(1)} %broadcast_add_fusion.1), channel_id=1, source_target_pairs={{0,2},{1,3},{2,0},{3,1},{4,6},{5,7},{6,4},{7,5},{8,10},{9,11},{10,... | collective-permute-start | bytes 12296 | tf_op jit(solution)/shard_map/ppermute | solution.py:37
  45.2 18.1 %collective-permute-start.6 = (bf16[96,1728]{1,0:T(8,128)(2,1)S(1)}, bf16[96,1728]{1,0:T(8,128)(2,1)S(1)}, u32[]{:S(2)}, u32[]{:S(2)}) collective-permute-start(bf16[96,1728]{1,0:T(8,128)(2,1)S(1)} %fusion.21), channel_id=1, source_target_pairs={{0,2},{1,3},{2,0},{3,1},{4,6},{5,7},{6,4},{7,5},{8,10},{9,11},{10,... | collective-permute-start | bytes 995336 | tf_op jit(solution)/shard_map/ppermute | solution.py:37
  50.7 12.6 %collective-permute-start.15 = (f32[8,128]{1,0:T(8,128)S(1)}, f32[8,128]{1,0:T(8,128)S(1)}, u32[]{:S(2)}, u32[]{:S(2)}) collective-permute-start(f32[8,128]{1,0:T(8,128)S(1)} %add.558), channel_id=1, source_target_pairs={{0,8},{4,12},{8,0},{12,4},{16,24},{20,28},{24,16},{28,20},{1,9},{5... | collective-permute-start | bytes 12296 | tf_op jit(solution)/shard_map/ppermute | solution.py:37
  52.3 17.2 %collective-permute-start.5 = (bf16[96,1728]{1,0:T(8,128)(2,1)S(1)}, bf16[96,1728]{1,0:T(8,128)(2,1)S(1)}, u32[]{:S(2)}, u32[]{:S(2)}) collective-permute-start(bf16[96,1728]{1,0:T(8,128)(2,1)S(1)} %fusion.21), channel_id=1, source_target_pairs={{0,1},{1,0},{2,3},{3,2},{4,5},{5,4},{6,7},{7,6},{8,9},{9,8},{10,11... | collective-permute-start | bytes 995336 | tf_op jit(solution)/shard_map/ppermute | solution.py:37
  63.3 6.1 collective-permute-start.7
  235.8 11.5 %collective-permute-start.17 = (bf16[96,512]{1,0:T(8,128)(2,1)}, bf16[96,512]{1,0:T(8,128)(2,1)S(1)}, u32[]{:S(2)}, u32[]{:S(2)}) collective-permute-start(bf16[96,512]{1,0:T(8,128)(2,1)} %fusion.17), channel_id=1, source_target_pairs={{0,1},{1,0},{2,3},{3,2},{4,5},{5,4},{6,7},{7,6},{8,9},{9,8},{10,11... | collective-permute-start | bytes 294920 | tf_op jit(solution)/shard_map/ppermute | solution.py:37
  239.8 7.6 %collective-permute-start.19 = (bf16[96,512]{1,0:T(8,128)(2,1)S(1)}, bf16[96,512]{1,0:T(8,128)(2,1)}, u32[]{:S(2)}, u32[]{:S(2)}) collective-permute-start(bf16[96,512]{1,0:T(8,128)(2,1)S(1)} %collective-permute-done.18), channel_id=1, source_target_pairs={{0,1},{1,0},{2,3},{3,2},{4,5},{5,4},{6,7},{7,6},{8,9},{9,8},{10,11... | collective-permute-start | bytes 294920 | tf_op jit(solution)/shard_map/ppermute | solution.py:37
  254.1 8.4 %collective-permute-start.20 = (bf16[192,1024]{1,0:T(8,128)(2,1)S(1)}, bf16[192,1024]{1,0:T(8,128)(2,1)S(1)}, u32[]{:S(2)}, u32[]{:S(2)}) collective-permute-start(bf16[192,1024]{1,0:T(8,128)(2,1)S(1)} %get-tuple-element.189), channel_id=1, source_target_pairs={{0,1},{1,2},{2,3},{4,5},{5,6},{6,7},{8,9},{9,10},{10,11},{12,13},{... | collective-permute-start | bytes 1179656 | tf_op jit(solution)/shard_map/ppermute | solution.py:174
  259.2 32.2 %collective-permute-start.23 = (bf16[96,4608]{1,0:T(8,128)(2,1)}, bf16[96,4608]{1,0:T(8,128)(2,1)}, u32[]{:S(2)}, u32[]{:S(2)}) collective-permute-start(bf16[96,4608]{1,0:T(8,128)(2,1)} %pad_maximum_fusion.10), channel_id=1, source_target_pairs={{0,2},{1,3},{2,0},{3,1},{4,6},{5,7},{6,4},{7,5},{8,10},{9,11},{10,... | collective-permute-start | bytes 2654216 | tf_op jit(solution)/shard_map/ppermute | solution.py:37
  262.3 40.4 %collective-permute-start.22 = (bf16[96,4608]{1,0:T(8,128)(2,1)}, bf16[96,4608]{1,0:T(8,128)(2,1)}, u32[]{:S(2)}, u32[]{:S(2)}) collective-permute-start(bf16[96,4608]{1,0:T(8,128)(2,1)} %pad_maximum_fusion.10), channel_id=1, source_target_pairs={{0,1},{1,0},{2,3},{3,2},{4,5},{5,4},{6,7},{7,6},{8,9},{9,8},{10,11... | collective-permute-start | bytes 2654216 | tf_op jit(solution)/shard_map/ppermute | solution.py:37
  291.4 11.3 %collective-permute-start.24 = (bf16[96,4608]{1,0:T(8,128)(2,1)}, bf16[96,4608]{1,0:T(8,128)(2,1)S(1)}, u32[]{:S(2)}, u32[]{:S(2)}) collective-permute-start(bf16[96,4608]{1,0:T(8,128)(2,1)} %collective-permute-done.23), channel_id=1, source_target_pairs={{0,1},{1,0},{2,3},{3,2},{4,5},{5,4},{6,7},{7,6},{8,9},{9,8},{10,11... | collective-permute-start | bytes 2654216 | tf_op jit(solution)/shard_map/ppermute | solution.py:37
  352.8 26.0 %collective-permute-start.25 = (f32[192,1024]{1,0:T(8,128)S(1)}, f32[192,1024]{1,0:T(8,128)S(1)}, u32[]{:S(2)}, u32[]{:S(2)}) collective-permute-start(f32[192,1024]{1,0:T(8,128)S(1)} %get-tuple-element.187), channel_id=1, source_target_pairs={{0,1},{1,2},{2,3},{4,5},{5,6},{6,7},{8,9},{9,10},{10,11},{12,13},{... | collective-permute-start | bytes 2359304 | tf_op jit(solution)/shard_map/ppermute | solution.py:185
  355.7 23.1 %collective-permute-start.26 = (f32[192,1024]{1,0:T(8,128)S(1)}, f32[192,1024]{1,0:T(8,128)S(1)}, u32[]{:S(2)}, u32[]{:S(2)}) collective-permute-start(f32[192,1024]{1,0:T(8,128)S(1)} %get-tuple-element.188), channel_id=1, source_target_pairs={{1,0},{2,1},{3,2},{5,4},{6,5},{7,6},{9,8},{10,9},{11,10},{13,12},{... | collective-permute-start | bytes 2359304 | tf_op jit(solution)/shard_map/ppermute | solution.py:185
  421.2 14.3 %collective-permute-start.29 = (f32[17408,128]{1,0:T(8,128)}, f32[17408,128]{1,0:T(8,128)}, u32[]{:S(2)}, u32[]{:S(2)}) collective-permute-start(f32[17408,128]{1,0:T(8,128)} %get-tuple-element.112), channel_id=1, source_target_pairs={{0,1},{1,0},{2,3},{3,2},{4,5},{5,4},{6,7},{7,6},{8,9},{9,8},{10,11... | collective-permute-start | bytes 26738696 | tf_op jit(solution)/shard_map/ppermute | solution.py:37
  442.1 9.1 %collective-permute-start.31 = (f32[96,768]{1,0:T(8,128)S(1)}, f32[96,768]{1,0:T(8,128)S(1)}, u32[]{:S(2)}, u32[]{:S(2)}) collective-permute-start(f32[96,768]{1,0:T(8,128)S(1)} %add_add_fusion.10), channel_id=1, source_target_pairs={{0,2},{1,3},{2,0},{3,1},{4,6},{5,7},{6,4},{7,5},{8,10},{9,11},{10,... | collective-permute-start | bytes 884744 | tf_op jit(solution)/shard_map/ppermute | solution.py:37
  443.8 7.5 %collective-permute-start.30 = (f32[96,768]{1,0:T(8,128)S(1)}, f32[96,768]{1,0:T(8,128)S(1)}, u32[]{:S(2)}, u32[]{:S(2)}) collective-permute-start(f32[96,768]{1,0:T(8,128)S(1)} %add_add_fusion.10), channel_id=1, source_target_pairs={{0,1},{1,0},{2,3},{3,2},{4,5},{5,4},{6,7},{7,6},{8,9},{9,8},{10,11... | collective-permute-start | bytes 884744 | tf_op jit(solution)/shard_map/ppermute | solution.py:37
  445.3 51.2 %collective-permute-start.40 = (f32[2,1,2,1088,128]{4,3,2,1,0:T(8,128)}, f32[2,1,2,1088,128]{4,3,2,1,0:T(8,128)}, u32[]{:S(2)}, u32[]{:S(2)}) collective-permute-start(f32[2,1,2,1088,128]{4,3,2,1,0:T(8,128)} %constant_dynamic-slice_fusion.12), channel_id=1, source_target_pairs={{0,8},{4,12},{8,0},{12,4},{16,24},{20,28},{24,16},{28,20},{1,9},{5... | collective-permute-start | bytes 6684680 | tf_op jit(solution)/shard_map/ppermute | solution.py:37
  448.3 52.2 %collective-permute-start.39 = (f32[2,2,1,1088,128]{4,3,2,1,0:T(8,128)}, f32[2,2,1,1088,128]{4,3,2,1,0:T(8,128)}, u32[]{:S(2)}, u32[]{:S(2)}) collective-permute-start(f32[2,2,1,1088,128]{4,3,2,1,0:T(8,128)} %constant_dynamic-slice_fusion.13), channel_id=1, source_target_pairs={{0,4},{4,0},{8,12},{12,8},{16,20},{20,16},{24,28},{28,24},{1,5},{5... | collective-permute-start | bytes 6684680 | tf_op jit(solution)/shard_map/ppermute | solution.py:37
  453.6 18.7 %collective-permute-start.34 = (bf16[96,3840]{1,0:T(8,128)(2,1)S(1)}, bf16[96,3840]{1,0:T(8,128)(2,1)S(1)}, u32[]{:S(2)}, u32[]{:S(2)}) collective-permute-start(bf16[96,3840]{1,0:T(8,128)(2,1)S(1)} %pad_maximum_fusion.11), channel_id=1, source_target_pairs={{0,2},{1,3},{2,0},{3,1},{4,6},{5,7},{6,4},{7,5},{8,10},{9,11},{10,... | collective-permute-start | bytes 2211848 | tf_op jit(solution)/shard_map/ppermute | solution.py:37
  455.2 20.5 %collective-permute-start.33 = (bf16[96,3840]{1,0:T(8,128)(2,1)S(1)}, bf16[96,3840]{1,0:T(8,128)(2,1)}, u32[]{:S(2)}, u32[]{:S(2)}) collective-permute-start(bf16[96,3840]{1,0:T(8,128)(2,1)S(1)} %pad_maximum_fusion.11), channel_id=1, source_target_pairs={{0,1},{1,0},{2,3},{3,2},{4,5},{5,4},{6,7},{7,6},{8,9},{9,8},{10,11... | collective-permute-start | bytes 2211848 | tf_op jit(solution)/shard_map/ppermute | solution.py:37
  465.9 6.9 collective-permute-start.37
  505.0 47.6 %collective-permute-start.41 = (f32[2,2,1,1024,128]{4,3,2,1,0:T(8,128)}, f32[2,2,1,1024,128]{4,3,2,1,0:T(8,128)}, u32[]{:S(2)}, u32[]{:S(2)}) collective-permute-start(f32[2,2,1,1024,128]{4,3,2,1,0:T(8,128)} %constant_dynamic-slice_fusion.11), channel_id=1, source_target_pairs={{0,4},{4,0},{8,12},{12,8},{16,20},{20,16},{24,28},{28,24},{1,5},{5... | collective-permute-start | bytes 6291464 | tf_op jit(solution)/shard_map/ppermute | solution.py:37
  506.8 50.8 %collective-permute-start.44 = (f32[2,1,2,1040,128]{4,3,2,1,0:T(8,128)}, f32[2,1,2,1040,128]{4,3,2,1,0:T(8,128)}, u32[]{:S(2)}, u32[]{:S(2)}) collective-permute-start(f32[2,1,2,1040,128]{4,3,2,1,0:T(8,128)} %constant_dynamic-slice_fusion.8), channel_id=1, source_target_pairs={{0,8},{4,12},{8,0},{12,4},{16,24},{20,28},{24,16},{28,20},{1,9},{5... | collective-permute-start | bytes 6389768 | tf_op jit(solution)/shard_map/ppermute | solution.py:37
  556.1 42.2 %collective-permute-start.42 = (f32[2,1,1,1024,128]{4,3,2,1,0:T(8,128)}, f32[2,1,1,1024,128]{4,3,2,1,0:T(8,128)}, u32[]{:S(2)}, u32[]{:S(2)}) collective-permute-start(f32[2,1,1,1024,128]{4,3,2,1,0:T(8,128)} %constant_dynamic-slice_fusion.10), channel_id=1, source_target_pairs={{0,8},{4,12},{8,0},{12,4},{16,24},{20,28},{24,16},{28,20},{1,9},{5... | collective-permute-start | bytes 3145736 | tf_op jit(solution)/shard_map/ppermute | solution.py:37
  561.5 61.6 %collective-permute-start.45 = (f32[1,1,2,1040,128]{4,3,2,1,0:T(8,128)S(1)}, f32[1,1,2,1040,128]{4,3,2,1,0:T(8,128)}, u32[]{:S(2)}, u32[]{:S(2)}) collective-permute-start(f32[1,1,2,1040,128]{4,3,2,1,0:T(8,128)S(1)} %constant_dynamic-slice_fusion.7), channel_id=1, source_target_pairs={{0,16},{4,20},{8,24},{12,28},{16,0},{20,4},{24,8},{28,12},{1,17},{... | collective-permute-start | bytes 3194888 | tf_op jit(solution)/shard_map/ppermute | solution.py:37
  564.0 60.9 %collective-permute-start.48 = (f32[2,1,2,544,128]{4,3,2,1,0:T(8,128)S(1)}, f32[2,1,2,544,128]{4,3,2,1,0:T(8,128)S(1)}, u32[]{:S(2)}, u32[]{:S(2)}) collective-permute-start(f32[2,1,2,544,128]{4,3,2,1,0:T(8,128)S(1)} %constant_dynamic-slice_fusion.4), channel_id=1, source_target_pairs={{0,2},{1,3},{2,0},{3,1},{4,6},{5,7},{6,4},{7,5},{8,10},{9,11},{10,... | collective-permute-start | bytes 3342344 | tf_op jit(solution)/shard_map/ppermute | solution.py:37
  564.5 60.6 %collective-permute-start.47 = (f32[2,2,1,544,128]{4,3,2,1,0:T(8,128)S(1)}, f32[2,2,1,544,128]{4,3,2,1,0:T(8,128)S(1)}, u32[]{:S(2)}, u32[]{:S(2)}) collective-permute-start(f32[2,2,1,544,128]{4,3,2,1,0:T(8,128)S(1)} %constant_dynamic-slice_fusion.5), channel_id=1, source_target_pairs={{0,2},{1,3},{2,0},{3,1},{4,6},{5,7},{6,4},{7,5},{8,10},{9,11},{10,... | collective-permute-start | bytes 3342344 | tf_op jit(solution)/shard_map/ppermute | solution.py:37
  599.8 32.0 %collective-permute-start.43 = (f32[1,1,1,1024,128]{4,3,2,1,0:T(8,128)S(1)}, f32[1,1,1,1024,128]{4,3,2,1,0:T(8,128)S(1)}, u32[]{:S(2)}, u32[]{:S(2)}) collective-permute-start(f32[1,1,1,1024,128]{4,3,2,1,0:T(8,128)S(1)} %constant_dynamic-slice_fusion.9), channel_id=1, source_target_pairs={{0,16},{4,20},{8,24},{12,28},{16,0},{20,4},{24,8},{28,12},{1,17},{... | collective-permute-start | bytes 1572872 | tf_op jit(solution)/shard_map/ppermute | solution.py:37
  624.5 9.3 %collective-permute-start.46 = (f32[1,1,1,1040,128]{4,3,2,1,0:T(8,128)S(1)}, f32[1,1,1,1040,128]{4,3,2,1,0:T(8,128)S(1)}, u32[]{:S(2)}, u32[]{:S(2)}) collective-permute-start(f32[1,1,1,1040,128]{4,3,2,1,0:T(8,128)S(1)} %constant_dynamic-slice_fusion.6), channel_id=1, source_target_pairs={{0,4},{4,0},{8,12},{12,8},{16,20},{20,16},{24,28},{28,24},{1,5},{5... | collective-permute-start | bytes 1597448 | tf_op jit(solution)/shard_map/ppermute | solution.py:37
  634.0 21.4 %collective-permute-start.49 = (f32[2,1,1,544,128]{4,3,2,1,0:T(8,128)S(1)}, f32[2,1,1,544,128]{4,3,2,1,0:T(8,128)S(1)}, u32[]{:S(2)}, u32[]{:S(2)}) collective-permute-start(f32[2,1,1,544,128]{4,3,2,1,0:T(8,128)S(1)} %constant_dynamic-slice_fusion.3), channel_id=1, source_target_pairs={{0,8},{4,12},{8,0},{12,4},{16,24},{20,28},{24,16},{28,20},{1,9},{5... | collective-permute-start | bytes 1671176 | tf_op jit(solution)/shard_map/ppermute | solution.py:37
  634.1 23.2 %collective-permute-start.51 = (f32[1,1,2,544,128]{4,3,2,1,0:T(8,128)S(1)}, f32[1,1,2,544,128]{4,3,2,1,0:T(8,128)S(1)}, u32[]{:S(2)}, u32[]{:S(2)}) collective-permute-start(f32[1,1,2,544,128]{4,3,2,1,0:T(8,128)S(1)} %constant_dynamic-slice_fusion.1), channel_id=1, source_target_pairs={{0,16},{4,20},{8,24},{12,28},{16,0},{20,4},{24,8},{28,12},{1,17},{... | collective-permute-start | bytes 1671176 | tf_op jit(solution)/shard_map/ppermute | solution.py:37
  638.1 38.0 %collective-permute-start.59 = (f32[2064,128]{1,0:T(8,128)S(1)}, f32[2064,128]{1,0:T(8,128)}, u32[]{:S(2)}, u32[]{:S(2)}) collective-permute-start(f32[2064,128]{1,0:T(8,128)S(1)} %get-tuple-element.204.refs_0_), channel_id=1, source_target_pairs={{0,2},{1,3},{2,0},{3,1},{4,6},{5,7},{6,4},{7,5},{8,10},{9,11},{10,... | collective-permute-start | bytes 3170312 | tf_op jit(solution)/shard_map/ppermute | solution.py:37
  655.5 13.8 %collective-permute-start.50 = (f32[1,1,1,544,128]{4,3,2,1,0:T(8,128)S(1)}, f32[1,1,1,544,128]{4,3,2,1,0:T(8,128)S(1)}, u32[]{:S(2)}, u32[]{:S(2)}) collective-permute-start(f32[1,1,1,544,128]{4,3,2,1,0:T(8,128)S(1)} %constant_dynamic-slice_fusion.2), channel_id=1, source_target_pairs={{0,16},{4,20},{8,24},{12,28},{16,0},{20,4},{24,8},{28,12},{1,17},{... | collective-permute-start | bytes 835592 | tf_op jit(solution)/shard_map/ppermute | solution.py:37
  657.4 14.7 %collective-permute-start.52 = (f32[1,1,1,544,128]{4,3,2,1,0:T(8,128)S(1)}, f32[1,1,1,544,128]{4,3,2,1,0:T(8,128)S(1)}, u32[]{:S(2)}, u32[]{:S(2)}) collective-permute-start(f32[1,1,1,544,128]{4,3,2,1,0:T(8,128)S(1)} %constant_dynamic-slice_fusion), channel_id=1, source_target_pairs={{0,4},{4,0},{8,12},{12,8},{16,20},{20,16},{24,28},{28,24},{1,5},{5... | collective-permute-start | bytes 835592 | tf_op jit(solution)/shard_map/ppermute | solution.py:37
  670.0 9.5 %collective-permute-start.61 = (f32[544,128]{1,0:T(8,128)S(1)}, f32[544,128]{1,0:T(8,128)S(1)}, u32[]{:S(2)}, u32[]{:S(2)}) collective-permute-start(f32[544,128]{1,0:T(8,128)S(1)} %get-tuple-element.157), channel_id=1, source_target_pairs={{0,2},{1,3},{2,0},{3,1},{4,6},{5,7},{6,4},{7,5},{8,10},{9,11},{10,... | collective-permute-start | bytes 835592 | tf_op jit(solution)/shard_map/ppermute | solution.py:37
  670.7 33.6 %collective-permute-start.58 = (f32[2064,128]{1,0:T(8,128)S(1)}, f32[2064,128]{1,0:T(8,128)}, u32[]{:S(2)}, u32[]{:S(2)}) collective-permute-start(f32[2064,128]{1,0:T(8,128)S(1)} %get-tuple-element.204.refs_0_), channel_id=1, source_target_pairs={{0,1},{1,0},{2,3},{3,2},{4,5},{5,4},{6,7},{7,6},{8,9},{9,8},{10,11... | collective-permute-start | bytes 3170312 | tf_op jit(solution)/shard_map/ppermute | solution.py:37
  672.7 11.8 %collective-permute-start.62 = (f32[544,128]{1,0:T(8,128)S(1)}, f32[544,128]{1,0:T(8,128)S(1)}, u32[]{:S(2)}, u32[]{:S(2)}) collective-permute-start(f32[544,128]{1,0:T(8,128)S(1)} %get-tuple-element.155), channel_id=1, source_target_pairs={{0,2},{1,3},{2,0},{3,1},{4,6},{5,7},{6,4},{7,5},{8,10},{9,11},{10,... | collective-permute-start | bytes 835592 | tf_op jit(solution)/shard_map/ppermute | solution.py:37
  676.1 28.2 %collective-permute-start.60 = (f32[2064,128]{1,0:T(8,128)}, f32[2064,128]{1,0:T(8,128)}, u32[]{:S(2)}, u32[]{:S(2)}) collective-permute-start(f32[2064,128]{1,0:T(8,128)} %collective-permute-done.59.refs_2_), channel_id=1, source_target_pairs={{0,1},{1,0},{2,3},{3,2},{4,5},{5,4},{6,7},{7,6},{8,9},{9,8},{10,11... | collective-permute-start | bytes 3170312 | tf_op jit(solution)/shard_map/ppermute | solution.py:37
  684.7 38.7 %collective-permute-start.63 = (f32[2176,128]{1,0:T(8,128)S(1)}, f32[2176,128]{1,0:T(8,128)S(1)}, u32[]{:S(2)}, u32[]{:S(2)}) collective-permute-start(f32[2176,128]{1,0:T(8,128)S(1)} %pad_maximum_fusion.9.refs_0_), channel_id=1, source_target_pairs={{0,1},{1,0},{2,3},{3,2},{4,5},{5,4},{6,7},{7,6},{8,9},{9,8},{10,11... | collective-permute-start | bytes 3342344 | tf_op jit(solution)/shard_map/ppermute | solution.py:37
  (124 other events, 969.1 us)
Sparse Core Ops, SparseCore 0:
  11.5 125.7 all-gather.2
  140.7 77.7 all-gather.4

commit v5 on v4

--- a/solution.py
+++ b/solution.py
@@ -1185,8 +1185,9 @@
     enc_quarter, dec_blocks = lax.optimization_barrier((enc_quarter, dec_blocks))
     enc_blocks = reduce_first(enc_quarter, dp_routes(), (0.5,))
     dec_blocks = reduce_rest(dec_blocks, dec_routes(), 1, 2)
-    enc_sum = reduce_rest(enc_blocks, dp_routes())
-    enc_sum, dec_blocks = lax.optimization_barrier((enc_sum, dec_blocks))
+    enc_blocks = reduce_rest(enc_blocks, dp_routes(), 1, 2)
+    enc_blocks, dec_blocks = lax.optimization_barrier((enc_blocks, dec_blocks))
+    enc_sum = reduce_rest(enc_blocks, dp_routes(), 2)
     enc_own = jnp.concatenate(enc_sum, axis=0)
     enc_across = swap(enc_own, "grp", 2)
     dec_sum = reduce_rest(dec_blocks, dec_routes(), 2)

time: 747 us -> 773 us (1.035)
  waiting for transfers between devices: 301 us -> 320 us
    ppermute x58, waiting for transfers between devices: 202 us -> 221 us  [swap(): return lax.ppermute(block, axis, [(i, i ^ bit) for i in range(count)])]
    unnamed x208 -> x212, local copies, waits for them, and re-layouts: 21.6 us -> 24.3 us
  transfers between devices with their start and end apart: 66 -> 66, of which waited for: 30 -> 28; matrix products, arithmetic and copies ran while one was open for 15% -> 15% of each run, Pallas kernels for 13% -> 11%
where the time goes in v5:
time: 773 us; the launch traced here: 763 us
  waiting for transfers between devices  320 us (41%)
  Pallas kernels  154 us (20%)
  other arithmetic  81.2 us (11%)
  starting transfers between devices  63.6 us (8%)
  local copies, waits for them, and re-layouts  63.4 us (8%)
  matrix products  58.8 us (8%)
  between operations  22.2 us (3%)
    ppermute x58, waiting for transfers between devices, swap(): return lax.ppermute(block, axis, [(i, i ^ bit) for i in range(count)])  221 us
    all_gather x2, waiting for transfers between devices, gather_quarters(): return lax.all_gather(quarter, ('dp', 'grp'), axis=0, tiled=True)  98.4 us
    ppermute x58, starting transfers between devices, swap(): return lax.ppermute(block, axis, [(i, i ^ bit) for i in range(count)])  51.1 us
    pallas_call x3, Pallas kernels, attend_back(): pl.pallas_call(functools.partial(attend_back_kernel, window, stride, colu...  51 us
    dot_general x13, matrix products, matmul(): return jnp.dot(left, right, preferred_element_type=jnp.float32)  30.1 us
    pallas_call x2, Pallas kernels, relayout(): pl.pallas_call(functools.partial(relayout_kernel, plan), in_specs=[anywhe...  28 us
    dot_general x10, matrix products, mul_trans(): lax.dot_general(left, right, (((1,), (1,)), ((), ())), preferred_element_...  27 us
    pallas_call x1, Pallas kernels, dec_grad_halves(): pl.pallas_call(functools.partial(dec_grad_kernel, plan), in_specs=[pl.Blo...  24.7 us
  transfers between devices with their start and end apart: 66, of which 28 were waited for; matrix products, arithmetic and copies ran while one was open for 15% of the time, Pallas kernels for 11%

profile of v5, /device:TPU:0, one launch (start us, length us, event | category | flops | bytes accessed | tf_op | source)
XLA Modules:
  0.0 763.1 jit_solution(13707882401445213615)
XLA Ops:
  9.4 3.0 collective-permute-start.1
  18.0 3.1 multiply_sine_fusion
  52.3 11.0 %collective-permute-done.6 = bf16[96,1728]{1,0:T(8,128)(2,1)S(1)} collective-permute-done((bf16[96,1728]{1,0:T(8,128)(2,1)S(1)}, bf16[96,1728]{1,0:T(8,128)(2,1)S(1)}, u32[]{:S(2)}, u32[]{:S(2)}) %collective-permute-start.6) | collective-permute-done | bytes 331808 | tf_op jit(solution)/shard_map/ppermute | solution.py:37
  69.5 67.8 %all-gather.3.cloned.1.call-done.refs_0_ = bf16[66048,128]{1,0:T(8,128)(2,1)} async-done(((bf16[2064,128]{1,0:T(8,128)(2,1)}), bf16[66048,128]{1,0:T(8,128)(2,1)}) %all-gather.3.cloned.1.call-update) | async-done | bytes 16908304 | tf_op jit(solution)/shard_map/all_gather | solution.py:77
  141.2 18.7 %shard_map.202 = (bf16[1728,768]{1,0:T(8,128)(2,1)S(1)}, bf16[768,2304]{1,0:T(8,128)(2,1)S(1)}, bf16[768,768]{1,0:T(8,128)(2,1)S(1)}, bf16[768,3072]{1,0:T(8,128)(2,1)S(1)}, bf16[3072,768]{1,0:T(8,128)(2,1)}) custom-call(bf16[66048,128]{1,0:T(8,128)(2,1)} %all-gather.3.cloned.1.call-done.refs_0_), custom_call_target="tpu_custom_call" | custom-call | bytes 33816576 | tf_op jit(solution)/shard_map/pallas_call | solution.py:272
  176.1 4.9 fusion.14
  182.3 3.6 fusion.65
  187.8 30.6 %all-gather.5.cloned.1.call-done.refs_0_ = bf16[34816,128]{1,0:T(8,128)(2,1)} async-done(((bf16[1088,128]{1,0:T(8,128)(2,1)}), bf16[34816,128]{1,0:T(8,128)(2,1)}) %all-gather.5.cloned.1.call-update) | async-done | bytes 8912912 | tf_op jit(solution)/shard_map/all_gather | solution.py:77
  218.5 9.3 %shard_map.204 = (bf16[768,512]{1,0:T(8,128)(2,1)S(1)}, bf16[512,1536]{1,0:T(8,128)(2,1)S(1)}, bf16[512,512]{1,0:T(8,128)(2,1)S(1)}, bf16[512,2048]{1,0:T(8,128)(2,1)S(1)}, bf16[2048,512]{1,0:T(8,128)(2,1)S(1)}) custom-call(bf16[34816,128]{1,0:T(8,128)(2,1)} %all-gather.5.cloned.1.call-done.refs_0_), custom_call_target="tpu_custom_call" | custom-call | bytes 17825792 | tf_op jit(solution)/shard_map/pallas_call | solution.py:272
  236.8 3.0 collective-permute-done.18
  243.2 4.2 reshape.656
  259.6 3.1 collective-permute-start.23
  265.8 14.8 %shard_map.205 = bf16[896,512]{1,0:T(8,128)(2,1)S(1)} custom-call(bf16[896,512]{1,0:T(8,128)(2,1)S(1)} %pad.51.q_ref.refs_0_, bf16[1280,512]{1,0:T(8,128)(2,1)S(1)} %pad.52.k_ref.refs_2_, bf16[1280,512]{1,0:T(8,128)(2,1)S(1)} %pad.53.v_ref.refs_3_, s32[896,1]{1,0:T(8,128)S(1)} %copy-done.17, s32[1,1280]{1,0:T(1,128)S(1)} %broadcast_in_dim.89.kid_ref), custom_call_target="tpu_custom_call" | custom-call | flops 939524096 | bytes 5242880 | tf_op jit(solution)/shard_map/pallas_call | solution.py:503
  283.4 4.9 fusion.3
  291.5 5.9 collective-permute-start.24
  297.4 4.7 multiply_reduce_fusion
  302.8 3.6 pad_maximum_fusion.refs_2_
  306.4 5.9 divide_convert_fusion.refs_11_
  312.3 4.1 multiply_reduce_fusion.1
  317.4 3.9 multiply_convert_fusion.refs_7_
  321.3 5.2 multiply_reduce_fusion.2
  329.6 21.4 %shard_map.206 = (f32[896,512]{1,0:T(8,128)}, f32[1280,1024]{1,0:T(8,128)}) custom-call(bf16[896,512]{1,0:T(8,128)(2,1)S(1)} %pad.51.q_ref.refs_0_, bf16[896,512]{1,0:T(8,128)(2,1)S(1)} %pad.56.refs_1_, bf16[1280,512]{1,0:T(8,128)(2,1)S(1)} %pad.52.k_ref.refs_2_, bf16[1280,512]{1,0:T(8,128)(2,1)S(1)} %pad.53.v_ref.refs_3_, ...), custom_call_target="tpu_custom_call" | custom-call | flops 10737418240 | bytes 13107200 | tf_op jit(solution)/shard_map/pallas_call | solution.py:548
  352.5 3.7 collective-permute-start.25
  358.5 19.2 %shard_map.207 = (f32[896,512]{1,0:T(8,128)}, f32[1280,1024]{1,0:T(8,128)}) custom-call(bf16[896,512]{1,0:T(8,128)(2,1)S(1)} %pad.51.q_ref.refs_0_, bf16[896,512]{1,0:T(8,128)(2,1)S(1)} %pad.56.refs_1_, bf16[1280,512]{1,0:T(8,128)(2,1)S(1)} %pad.52.k_ref.refs_2_, bf16[1280,512]{1,0:T(8,128)(2,1)S(1)} %pad.53.v_ref.refs_3_, ...), custom_call_target="tpu_custom_call", output_to_operand_aliasing={{0}: (7, {})} | custom-call | flops 8053063680 | bytes 13107200 | tf_op jit(solution)/shard_map/pallas_call | solution.py:548
  379.3 3.0 add_convert_fusion
  392.3 3.1 collective-permute-done.28
  397.0 24.7 %shard_map.208 = (f32[17408,128]{1,0:T(8,128)}, f32[17408,128]{1,0:T(8,128)}) custom-call(s32[1]{0:T(128)} %bitcast.4.side_ref, bf16[96,768]{1,0:T(8,128)(2,1)} %add_convert_fusion.7.refs_0_, bf16[96,512]{1,0:T(8,128)(2,1)} %fusion.22.refs_1_, bf16[864,512]{1,0:T(8,128)(2,1)} %copy-done.52, bf16[864,1536]{1,0:T(8,128)(2,1)} %pad_maximum_fusion.2.refs_3_, ...), custom_call_target="tpu_custom_call" | custom-call | flops 7700742144 | bytes 17825792 | tf_op jit(solution)/shard_map/pallas_call | solution.py:954
  424.1 4.8 fusion.8
  429.0 7.0 collective-permute-done.29
  436.0 4.5 add.620
  448.4 3.4 collective-permute-done.31
  454.9 10.4 %shard_map.209 = (f32[384,768]{1,0:T(8,128)S(1)}, f32[384,1536]{1,0:T(8,128)S(1)}) custom-call(bf16[384,768]{1,0:T(8,128)(2,1)S(1)} %copy-done.14, bf16[384,768]{1,0:T(8,128)(2,1)S(1)} %convolution_convert_fusion.4.refs_1_, bf16[384,768]{1,0:T(8,128)(2,1)S(1)} %get-tuple-element.199.k_ref.refs_2_, bf16[384,768]{1,0:T(8,128)(2,1)S(1)} %get-tuple-element.198.v_ref.refs_3_, ...), custom_call_target="tpu_custom_call" | custom-call | flops 9059696640 | bytes 5898240 | tf_op jit(solution)/shard_map/pallas_call | solution.py:548
  469.7 3.2 collective-permute-done.34
  479.2 14.5 %shard_map.210 = f32[16512,128]{1,0:T(8,128)} custom-call(s32[2]{0:T(128)S(1)} %pad_add_fusion.4.place_ref, bf16[384,1728]{1,0:T(8,128)(2,1)S(1)} %pad_maximum_fusion.6.refs_0_, bf16[384,768]{1,0:T(8,128)(2,1)S(1)} %copy-done.4, bf16[384,4608]{1,0:T(8,128)(2,1)} %pad_maximum_fusion.refs_2_, bf16[384,768]{1,0:T(8,128)(2,1)S(1)} %add_convert_fusion.5.refs_3_, ...), custom_call_target="tpu_custom_call" | custom-call | flops 3246391296 | bytes 8454144 | tf_op jit(solution)/shard_map/pallas_call | solution.py:846
  496.2 4.0 dynamic-slice_add_fusion
  500.2 3.0 dynamic-slice_add_fusion.1
  512.5 39.8 %collective-permute-done.41 = f32[2,2,1,1024,128]{4,3,2,1,0:T(8,128)} collective-permute-done((f32[2,2,1,1024,128]{4,3,2,1,0:T(8,128)}, f32[2,2,1,1024,128]{4,3,2,1,0:T(8,128)}, u32[]{:S(2)}, u32[]{:S(2)}) %collective-permute-start.41) | collective-permute-done | bytes 2097184 | tf_op jit(solution)/shard_map/ppermute | solution.py:37
  566.5 30.5 %collective-permute-done.42 = f32[2,1,1,1024,128]{4,3,2,1,0:T(8,128)} collective-permute-done((f32[2,1,1,1024,128]{4,3,2,1,0:T(8,128)}, f32[2,1,1,1024,128]{4,3,2,1,0:T(8,128)}, u32[]{:S(2)}, u32[]{:S(2)}) %collective-permute-start.42) | collective-permute-done | bytes 1048608 | tf_op jit(solution)/shard_map/ppermute | solution.py:37
  598.4 11.9 %collective-permute-done.44 = f32[1,1,2,1040,128]{4,3,2,1,0:T(8,128)} collective-permute-done((f32[1,1,2,1040,128]{4,3,2,1,0:T(8,128)}, f32[1,1,2,1040,128]{4,3,2,1,0:T(8,128)}, u32[]{:S(2)}, u32[]{:S(2)}) %collective-permute-start.44) | collective-permute-done | bytes 1064992 | tf_op jit(solution)/shard_map/ppermute | solution.py:37
  616.1 21.1 %collective-permute-done.47 = f32[1,1,1,1024,128]{4,3,2,1,0:T(8,128)S(1)} collective-permute-done((f32[1,1,1,1024,128]{4,3,2,1,0:T(8,128)S(1)}, f32[1,1,1,1024,128]{4,3,2,1,0:T(8,128)S(1)}, u32[]{:S(2)}, u32[]{:S(2)}) %collective-permute-start.47) | collective-permute-done | bytes 524320 | tf_op jit(solution)/shard_map/ppermute | solution.py:37
  639.2 25.5 %collective-permute-done.51 = f32[1,1,2,544,128]{4,3,2,1,0:T(8,128)S(1)} collective-permute-done((f32[1,1,2,544,128]{4,3,2,1,0:T(8,128)S(1)}, f32[1,1,2,544,128]{4,3,2,1,0:T(8,128)S(1)}, u32[]{:S(2)}, u32[]{:S(2)}) %collective-permute-start.51) | collective-permute-done | bytes 557088 | tf_op jit(solution)/shard_map/ppermute | solution.py:37
  665.2 5.3 collective-permute-done.50
  680.8 27.6 %collective-permute-done.62 = f32[544,128]{1,0:T(8,128)S(1)} collective-permute-done((f32[544,128]{1,0:T(8,128)S(1)}, f32[544,128]{1,0:T(8,128)S(1)}, u32[]{:S(2)}, u32[]{:S(2)}) %collective-permute-start.62) | collective-permute-done | bytes 278560 | tf_op jit(solution)/shard_map/ppermute | solution.py:37
  716.1 3.2 collective-permute-done.55
  719.4 3.5 collective-permute-done.56
  724.2 3.2 collective-permute-done.57
  734.0 5.2 shard_map.212
  741.5 13.5 %shard_map.211 = (f32[8256,128]{1,0:T(8,128)}, f32[8256,128]{1,0:T(8,128)}, f32[8256,128]{1,0:T(8,128)}, bf16[8256,128]{1,0:T(8,128)(2,1)}, f32[8256,128]{1,0:T(8,128)}) custom-call(s32[4]{0:T(128)S(1)} %pad_add_fusion.3.place_ref, f32[3]{0:T(128)S(1)} %pad_maximum_fusion.21.scalar_ref, f32[2064,128]{1,0:T(8,128)S(1)} %pad_maximum_fusion.10.refs_0_, ...), custom_call_target="tpu_custom_call" | custom-call | tf_op jit(solution)/shard_map/pallas_call | solution.py:1015
  (549 shorter events, 205.7 us)
Async XLA Ops:
  7.2 130.1 %all-gather.3.cloned.1.call-start = ((), (), s32[]{:S(2)}) async-start(), calls=%async_computation | async-start | bytes 17436672 | tf_op jit(solution)/shard_map/all_gather | solution.py:77
  9.3 209.2 %all-gather.5.cloned.1.call-start = ((), (), s32[]{:S(2)}) async-start(), calls=%async_computation.1 | async-start | bytes 9191424 | tf_op jit(solution)/shard_map/all_gather | solution.py:77
  9.4 15.4 %collective-permute-start.1 = (s32[96]{0:T(128)}, s32[96]{0:T(128)S(1)}, u32[]{:S(2)}, u32[]{:S(2)}) collective-permute-start(s32[96]{0:T(128)} %param.13), channel_id=1, source_target_pairs={{0,2},{1,3},{2,0},{3,1},{4,6},{5,7},{6,4},{7,5},{8,10},{9,11},{10,... | collective-permute-start | bytes 1160 | tf_op jit(solution)/shard_map/ppermute | solution.py:37
  12.4 12.7 %collective-permute-start = (s32[96]{0:T(128)}, s32[96]{0:T(128)S(1)}, u32[]{:S(2)}, u32[]{:S(2)}) collective-permute-start(s32[96]{0:T(128)} %param.13), channel_id=1, source_target_pairs={{0,1},{1,0},{2,3},{3,2},{4,5},{5,4},{6,7},{7,6},{8,9},{9,8},{10,11... | collective-permute-start | bytes 1160 | tf_op jit(solution)/shard_map/ppermute | solution.py:37
  12.4 20.9 %collective-permute-start.8 = (s32[864]{0:T(1024)}, s32[864]{0:T(1024)S(1)}, u32[]{:S(2)}, u32[]{:S(2)}) collective-permute-start(s32[864]{0:T(1024)} %param.12), channel_id=1, source_target_pairs={{0,2},{1,3},{2,0},{3,1},{4,6},{5,7},{6,4},{7,5},{8,10},{9,11},{10,... | collective-permute-start | bytes 10376 | tf_op jit(solution)/shard_map/ppermute | solution.py:37
  15.1 24.3 %collective-permute-start.12 = (f32[8,128]{1,0:T(8,128)S(1)}, f32[8,128]{1,0:T(8,128)S(1)}, u32[]{:S(2)}, u32[]{:S(2)}) collective-permute-start(f32[8,128]{1,0:T(8,128)S(1)} %broadcast_in_dim.83), channel_id=1, source_target_pairs={{0,1},{1,0},{2,3},{3,2},{4,5},{5,4},{6,7},{7,6},{8,9},{9,8},{10,11... | collective-permute-start | bytes 12296 | tf_op jit(solution)/shard_map/ppermute | solution.py:37
  33.4 29.9 %collective-permute-start.9 = (s32[2,864]{1,0:T(2,128)S(1)}, s32[2,864]{1,0:T(2,128)S(1)}, u32[]{:S(2)}, u32[]{:S(2)}) collective-permute-start(s32[2,864]{1,0:T(2,128)S(1)} %pad_add_fusion.1), channel_id=1, source_target_pairs={{0,1},{1,0},{2,3},{3,2},{4,5},{5,4},{6,7},{7,6},{8,9},{9,8},{10,11... | collective-permute-start | bytes 20744 | tf_op jit(solution)/shard_map/ppermute | solution.py:37
  33.8 10.4 %collective-permute-start.4 = (bf16[96,1728]{1,0:T(8,128)(2,1)S(1)}, bf16[96,1728]{1,0:T(8,128)(2,1)S(1)}, u32[]{:S(2)}, u32[]{:S(2)}) collective-permute-start(bf16[96,1728]{1,0:T(8,128)(2,1)S(1)} %slice_add_fusion), channel_id=1, source_target_pairs={{0,2},{1,3},{2,0},{3,1},{4,6},{5,7},{6,4},{7,5},{8,10},{9,11},{10,... | collective-permute-start | bytes 995336 | tf_op jit(solution)/shard_map/ppermute | solution.py:37
  35.7 6.4 collective-permute-start.10
  39.4 7.6 %collective-permute-start.13 = (f32[8,128]{1,0:T(8,128)S(1)}, f32[8,128]{1,0:T(8,128)S(1)}, u32[]{:S(2)}, u32[]{:S(2)}) collective-permute-start(f32[8,128]{1,0:T(8,128)S(1)} %broadcast_add_fusion.1), channel_id=1, source_target_pairs={{0,2},{1,3},{2,0},{3,1},{4,6},{5,7},{6,4},{7,5},{8,10},{9,11},{10,... | collective-permute-start | bytes 12296 | tf_op jit(solution)/shard_map/ppermute | solution.py:37
  45.2 18.1 %collective-permute-start.6 = (bf16[96,1728]{1,0:T(8,128)(2,1)S(1)}, bf16[96,1728]{1,0:T(8,128)(2,1)S(1)}, u32[]{:S(2)}, u32[]{:S(2)}) collective-permute-start(bf16[96,1728]{1,0:T(8,128)(2,1)S(1)} %fusion.21), channel_id=1, source_target_pairs={{0,2},{1,3},{2,0},{3,1},{4,6},{5,7},{6,4},{7,5},{8,10},{9,11},{10,... | collective-permute-start | bytes 995336 | tf_op jit(solution)/shard_map/ppermute | solution.py:37
  50.7 12.6 %collective-permute-start.15 = (f32[8,128]{1,0:T(8,128)S(1)}, f32[8,128]{1,0:T(8,128)S(1)}, u32[]{:S(2)}, u32[]{:S(2)}) collective-permute-start(f32[8,128]{1,0:T(8,128)S(1)} %add.558), channel_id=1, source_target_pairs={{0,8},{4,12},{8,0},{12,4},{16,24},{20,28},{24,16},{28,20},{1,9},{5... | collective-permute-start | bytes 12296 | tf_op jit(solution)/shard_map/ppermute | solution.py:37
  52.3 17.2 %collective-permute-start.5 = (bf16[96,1728]{1,0:T(8,128)(2,1)S(1)}, bf16[96,1728]{1,0:T(8,128)(2,1)S(1)}, u32[]{:S(2)}, u32[]{:S(2)}) collective-permute-start(bf16[96,1728]{1,0:T(8,128)(2,1)S(1)} %fusion.21), channel_id=1, source_target_pairs={{0,1},{1,0},{2,3},{3,2},{4,5},{5,4},{6,7},{7,6},{8,9},{9,8},{10,11... | collective-permute-start | bytes 995336 | tf_op jit(solution)/shard_map/ppermute | solution.py:37
  63.3 6.1 collective-permute-start.7
  235.9 11.5 %collective-permute-start.17 = (bf16[96,512]{1,0:T(8,128)(2,1)}, bf16[96,512]{1,0:T(8,128)(2,1)S(1)}, u32[]{:S(2)}, u32[]{:S(2)}) collective-permute-start(bf16[96,512]{1,0:T(8,128)(2,1)} %fusion.17), channel_id=1, source_target_pairs={{0,1},{1,0},{2,3},{3,2},{4,5},{5,4},{6,7},{7,6},{8,9},{9,8},{10,11... | collective-permute-start | bytes 294920 | tf_op jit(solution)/shard_map/ppermute | solution.py:37
  239.8 7.6 collective-permute-start.19
  254.5 8.4 %collective-permute-start.20 = (bf16[192,1024]{1,0:T(8,128)(2,1)S(1)}, bf16[192,1024]{1,0:T(8,128)(2,1)S(1)}, u32[]{:S(2)}, u32[]{:S(2)}) collective-permute-start(bf16[192,1024]{1,0:T(8,128)(2,1)S(1)} %get-tuple-element.193), channel_id=1, source_target_pairs={{0,1},{1,2},{2,3},{4,5},{5,6},{6,7},{8,9},{9,10},{10,11},{12,13},{... | collective-permute-start | bytes 1179656 | tf_op jit(solution)/shard_map/ppermute | solution.py:174
  259.6 31.9 %collective-permute-start.23 = (bf16[96,4608]{1,0:T(8,128)(2,1)}, bf16[96,4608]{1,0:T(8,128)(2,1)}, u32[]{:S(2)}, u32[]{:S(2)}) collective-permute-start(bf16[96,4608]{1,0:T(8,128)(2,1)} %pad_maximum_fusion.11), channel_id=1, source_target_pairs={{0,2},{1,3},{2,0},{3,1},{4,6},{5,7},{6,4},{7,5},{8,10},{9,11},{10,... | collective-permute-start | bytes 2654216 | tf_op jit(solution)/shard_map/ppermute | solution.py:37
  262.7 40.1 %collective-permute-start.22 = (bf16[96,4608]{1,0:T(8,128)(2,1)}, bf16[96,4608]{1,0:T(8,128)(2,1)}, u32[]{:S(2)}, u32[]{:S(2)}) collective-permute-start(bf16[96,4608]{1,0:T(8,128)(2,1)} %pad_maximum_fusion.11), channel_id=1, source_target_pairs={{0,1},{1,0},{2,3},{3,2},{4,5},{5,4},{6,7},{7,6},{8,9},{9,8},{10,11... | collective-permute-start | bytes 2654216 | tf_op jit(solution)/shard_map/ppermute | solution.py:37
  291.5 11.3 %collective-permute-start.24 = (bf16[96,4608]{1,0:T(8,128)(2,1)}, bf16[96,4608]{1,0:T(8,128)(2,1)S(1)}, u32[]{:S(2)}, u32[]{:S(2)}) collective-permute-start(bf16[96,4608]{1,0:T(8,128)(2,1)} %collective-permute-done.23), channel_id=1, source_target_pairs={{0,1},{1,0},{2,3},{3,2},{4,5},{5,4},{6,7},{7,6},{8,9},{9,8},{10,11... | collective-permute-start | bytes 2654216 | tf_op jit(solution)/shard_map/ppermute | solution.py:37
  352.5 26.8 %collective-permute-start.25 = (f32[192,1024]{1,0:T(8,128)S(1)}, f32[192,1024]{1,0:T(8,128)}, u32[]{:S(2)}, u32[]{:S(2)}) collective-permute-start(f32[192,1024]{1,0:T(8,128)S(1)} %get-tuple-element.191), channel_id=1, source_target_pairs={{0,1},{1,2},{2,3},{4,5},{5,6},{6,7},{8,9},{9,10},{10,11},{12,13},{... | collective-permute-start | bytes 2359304 | tf_op jit(solution)/shard_map/ppermute | solution.py:185
  356.2 23.1 %collective-permute-start.26 = (f32[192,1024]{1,0:T(8,128)S(1)}, f32[192,1024]{1,0:T(8,128)}, u32[]{:S(2)}, u32[]{:S(2)}) collective-permute-start(f32[192,1024]{1,0:T(8,128)S(1)} %get-tuple-element.192), channel_id=1, source_target_pairs={{1,0},{2,1},{3,2},{5,4},{6,5},{7,6},{9,8},{10,9},{11,10},{13,12},{... | collective-permute-start | bytes 2359304 | tf_op jit(solution)/shard_map/ppermute | solution.py:185
  421.7 14.3 %collective-permute-start.29 = (f32[17408,128]{1,0:T(8,128)}, f32[17408,128]{1,0:T(8,128)}, u32[]{:S(2)}, u32[]{:S(2)}) collective-permute-start(f32[17408,128]{1,0:T(8,128)} %get-tuple-element.112), channel_id=1, source_target_pairs={{0,1},{1,0},{2,3},{3,2},{4,5},{5,4},{6,7},{7,6},{8,9},{9,8},{10,11... | collective-permute-start | bytes 26738696 | tf_op jit(solution)/shard_map/ppermute | solution.py:37
  442.7 9.1 %collective-permute-start.31 = (f32[96,768]{1,0:T(8,128)S(1)}, f32[96,768]{1,0:T(8,128)S(1)}, u32[]{:S(2)}, u32[]{:S(2)}) collective-permute-start(f32[96,768]{1,0:T(8,128)S(1)} %add_add_fusion.10), channel_id=1, source_target_pairs={{0,2},{1,3},{2,0},{3,1},{4,6},{5,7},{6,4},{7,5},{8,10},{9,11},{10,... | collective-permute-start | bytes 884744 | tf_op jit(solution)/shard_map/ppermute | solution.py:37
  443.5 8.3 %collective-permute-start.30 = (f32[96,768]{1,0:T(8,128)S(1)}, f32[96,768]{1,0:T(8,128)S(1)}, u32[]{:S(2)}, u32[]{:S(2)}) collective-permute-start(f32[96,768]{1,0:T(8,128)S(1)} %add_add_fusion.10), channel_id=1, source_target_pairs={{0,1},{1,0},{2,3},{3,2},{4,5},{5,4},{6,7},{7,6},{8,9},{9,8},{10,11... | collective-permute-start | bytes 884744 | tf_op jit(solution)/shard_map/ppermute | solution.py:37
  445.0 51.2 %collective-permute-start.40 = (f32[2,1,2,1088,128]{4,3,2,1,0:T(8,128)}, f32[2,1,2,1088,128]{4,3,2,1,0:T(8,128)}, u32[]{:S(2)}, u32[]{:S(2)}) collective-permute-start(f32[2,1,2,1088,128]{4,3,2,1,0:T(8,128)} %constant_dynamic-slice_fusion.12), channel_id=1, source_target_pairs={{0,8},{4,12},{8,0},{12,4},{16,24},{20,28},{24,16},{28,20},{1,9},{5... | collective-permute-start | bytes 6684680 | tf_op jit(solution)/shard_map/ppermute | solution.py:37
  448.0 52.2 %collective-permute-start.39 = (f32[2,2,1,1088,128]{4,3,2,1,0:T(8,128)}, f32[2,2,1,1088,128]{4,3,2,1,0:T(8,128)}, u32[]{:S(2)}, u32[]{:S(2)}) collective-permute-start(f32[2,2,1,1088,128]{4,3,2,1,0:T(8,128)} %constant_dynamic-slice_fusion.13), channel_id=1, source_target_pairs={{0,4},{4,0},{8,12},{12,8},{16,20},{20,16},{24,28},{28,24},{1,5},{5... | collective-permute-start | bytes 6684680 | tf_op jit(solution)/shard_map/ppermute | solution.py:37
  454.1 18.7 %collective-permute-start.34 = (bf16[96,3840]{1,0:T(8,128)(2,1)S(1)}, bf16[96,3840]{1,0:T(8,128)(2,1)S(1)}, u32[]{:S(2)}, u32[]{:S(2)}) collective-permute-start(bf16[96,3840]{1,0:T(8,128)(2,1)S(1)} %pad_maximum_fusion.12), channel_id=1, source_target_pairs={{0,2},{1,3},{2,0},{3,1},{4,6},{5,7},{6,4},{7,5},{8,10},{9,11},{10,... | collective-permute-start | bytes 2211848 | tf_op jit(solution)/shard_map/ppermute | solution.py:37
  454.9 21.4 %collective-permute-start.33 = (bf16[96,3840]{1,0:T(8,128)(2,1)S(1)}, bf16[96,3840]{1,0:T(8,128)(2,1)}, u32[]{:S(2)}, u32[]{:S(2)}) collective-permute-start(bf16[96,3840]{1,0:T(8,128)(2,1)S(1)} %pad_maximum_fusion.12), channel_id=1, source_target_pairs={{0,1},{1,0},{2,3},{3,2},{4,5},{5,4},{6,7},{7,6},{8,9},{9,8},{10,11... | collective-permute-start | bytes 2211848 | tf_op jit(solution)/shard_map/ppermute | solution.py:37
  465.6 7.7 %collective-permute-start.37 = (f32[4,768]{1,0:T(4,128)S(1)}, f32[4,768]{1,0:T(4,128)S(1)}, u32[]{:S(2)}, u32[]{:S(2)}) collective-permute-start(f32[4,768]{1,0:T(4,128)S(1)} %pad_maximum_fusion.19), channel_id=1, source_target_pairs={{0,2},{1,3},{2,0},{3,1},{4,6},{5,7},{6,4},{7,5},{8,10},{9,11},{10,... | collective-permute-start | bytes 36872 | tf_op jit(solution)/shard_map/ppermute | solution.py:37
  504.7 47.6 %collective-permute-start.41 = (f32[2,2,1,1024,128]{4,3,2,1,0:T(8,128)}, f32[2,2,1,1024,128]{4,3,2,1,0:T(8,128)}, u32[]{:S(2)}, u32[]{:S(2)}) collective-permute-start(f32[2,2,1,1024,128]{4,3,2,1,0:T(8,128)} %constant_dynamic-slice_fusion.11), channel_id=1, source_target_pairs={{0,4},{4,0},{8,12},{12,8},{16,20},{20,16},{24,28},{28,24},{1,5},{5... | collective-permute-start | bytes 6291464 | tf_op jit(solution)/shard_map/ppermute | solution.py:37
  506.6 50.8 %collective-permute-start.43 = (f32[2,1,2,1040,128]{4,3,2,1,0:T(8,128)}, f32[2,1,2,1040,128]{4,3,2,1,0:T(8,128)}, u32[]{:S(2)}, u32[]{:S(2)}) collective-permute-start(f32[2,1,2,1040,128]{4,3,2,1,0:T(8,128)} %constant_dynamic-slice_fusion.9), channel_id=1, source_target_pairs={{0,8},{4,12},{8,0},{12,4},{16,24},{20,28},{24,16},{28,20},{1,9},{5... | collective-permute-start | bytes 6389768 | tf_op jit(solution)/shard_map/ppermute | solution.py:37
  510.4 52.9 %collective-permute-start.46 = (f32[2,1,2,544,128]{4,3,2,1,0:T(8,128)}, f32[2,1,2,544,128]{4,3,2,1,0:T(8,128)}, u32[]{:S(2)}, u32[]{:S(2)}) collective-permute-start(f32[2,1,2,544,128]{4,3,2,1,0:T(8,128)} %constant_dynamic-slice_fusion.6), channel_id=1, source_target_pairs={{0,2},{1,3},{2,0},{3,1},{4,6},{5,7},{6,4},{7,5},{8,10},{9,11},{10,... | collective-permute-start | bytes 3342344 | tf_op jit(solution)/shard_map/ppermute | solution.py:37
  511.7 53.3 %collective-permute-start.45 = (f32[2,2,1,544,128]{4,3,2,1,0:T(8,128)S(1)}, f32[2,2,1,544,128]{4,3,2,1,0:T(8,128)}, u32[]{:S(2)}, u32[]{:S(2)}) collective-permute-start(f32[2,2,1,544,128]{4,3,2,1,0:T(8,128)S(1)} %constant_dynamic-slice_fusion.7), channel_id=1, source_target_pairs={{0,2},{1,3},{2,0},{3,1},{4,6},{5,7},{6,4},{7,5},{8,10},{9,11},{10,... | collective-permute-start | bytes 3342344 | tf_op jit(solution)/shard_map/ppermute | solution.py:37
  555.9 41.1 %collective-permute-start.42 = (f32[2,1,1,1024,128]{4,3,2,1,0:T(8,128)}, f32[2,1,1,1024,128]{4,3,2,1,0:T(8,128)}, u32[]{:S(2)}, u32[]{:S(2)}) collective-permute-start(f32[2,1,1,1024,128]{4,3,2,1,0:T(8,128)} %constant_dynamic-slice_fusion.10), channel_id=1, source_target_pairs={{0,8},{4,12},{8,0},{12,4},{16,24},{20,28},{24,16},{28,20},{1,9},{5... | collective-permute-start | bytes 3145736 | tf_op jit(solution)/shard_map/ppermute | solution.py:37
  562.2 48.1 %collective-permute-start.44 = (f32[1,1,2,1040,128]{4,3,2,1,0:T(8,128)}, f32[1,1,2,1040,128]{4,3,2,1,0:T(8,128)}, u32[]{:S(2)}, u32[]{:S(2)}) collective-permute-start(f32[1,1,2,1040,128]{4,3,2,1,0:T(8,128)} %constant_dynamic-slice_fusion.8), channel_id=1, source_target_pairs={{0,16},{4,20},{8,24},{12,28},{16,0},{20,4},{24,8},{28,12},{1,17},{... | collective-permute-start | bytes 3194888 | tf_op jit(solution)/shard_map/ppermute | solution.py:37
  611.7 25.5 %collective-permute-start.47 = (f32[1,1,1,1024,128]{4,3,2,1,0:T(8,128)S(1)}, f32[1,1,1,1024,128]{4,3,2,1,0:T(8,128)S(1)}, u32[]{:S(2)}, u32[]{:S(2)}) collective-permute-start(f32[1,1,1,1024,128]{4,3,2,1,0:T(8,128)S(1)} %constant_dynamic-slice_fusion.5), channel_id=1, source_target_pairs={{0,16},{4,20},{8,24},{12,28},{16,0},{20,4},{24,8},{28,12},{1,17},{... | collective-permute-start | bytes 1572872 | tf_op jit(solution)/shard_map/ppermute | solution.py:37
  611.8 26.1 %collective-permute-start.48 = (f32[1,1,1,1040,128]{4,3,2,1,0:T(8,128)S(1)}, f32[1,1,1,1040,128]{4,3,2,1,0:T(8,128)S(1)}, u32[]{:S(2)}, u32[]{:S(2)}) collective-permute-start(f32[1,1,1,1040,128]{4,3,2,1,0:T(8,128)S(1)} %constant_dynamic-slice_fusion.4), channel_id=1, source_target_pairs={{0,4},{4,0},{8,12},{12,8},{16,20},{20,16},{24,28},{28,24},{1,5},{5... | collective-permute-start | bytes 1597448 | tf_op jit(solution)/shard_map/ppermute | solution.py:37
  613.0 25.7 %collective-permute-start.49 = (f32[2,1,1,544,128]{4,3,2,1,0:T(8,128)S(1)}, f32[2,1,1,544,128]{4,3,2,1,0:T(8,128)S(1)}, u32[]{:S(2)}, u32[]{:S(2)}) collective-permute-start(f32[2,1,1,544,128]{4,3,2,1,0:T(8,128)S(1)} %constant_dynamic-slice_fusion.3), channel_id=1, source_target_pairs={{0,8},{4,12},{8,0},{12,4},{16,24},{20,28},{24,16},{28,20},{1,9},{5... | collective-permute-start | bytes 1671176 | tf_op jit(solution)/shard_map/ppermute | solution.py:37
  615.6 49.1 %collective-permute-start.51 = (f32[1,1,2,544,128]{4,3,2,1,0:T(8,128)S(1)}, f32[1,1,2,544,128]{4,3,2,1,0:T(8,128)S(1)}, u32[]{:S(2)}, u32[]{:S(2)}) collective-permute-start(f32[1,1,2,544,128]{4,3,2,1,0:T(8,128)S(1)} %constant_dynamic-slice_fusion.1), channel_id=1, source_target_pairs={{0,16},{4,20},{8,24},{12,28},{16,0},{20,4},{24,8},{28,12},{1,17},{... | collective-permute-start | bytes 1671176 | tf_op jit(solution)/shard_map/ppermute | solution.py:37
  638.9 31.7 %collective-permute-start.50 = (f32[1,1,1,544,128]{4,3,2,1,0:T(8,128)S(1)}, f32[1,1,1,544,128]{4,3,2,1,0:T(8,128)S(1)}, u32[]{:S(2)}, u32[]{:S(2)}) collective-permute-start(f32[1,1,1,544,128]{4,3,2,1,0:T(8,128)S(1)} %constant_dynamic-slice_fusion.2), channel_id=1, source_target_pairs={{0,16},{4,20},{8,24},{12,28},{16,0},{20,4},{24,8},{28,12},{1,17},{... | collective-permute-start | bytes 835592 | tf_op jit(solution)/shard_map/ppermute | solution.py:37
  664.8 9.9 %collective-permute-start.52 = (f32[1,1,1,544,128]{4,3,2,1,0:T(8,128)S(1)}, f32[1,1,1,544,128]{4,3,2,1,0:T(8,128)S(1)}, u32[]{:S(2)}, u32[]{:S(2)}) collective-permute-start(f32[1,1,1,544,128]{4,3,2,1,0:T(8,128)S(1)} %constant_dynamic-slice_fusion), channel_id=1, source_target_pairs={{0,4},{4,0},{8,12},{12,8},{16,20},{20,16},{24,28},{28,24},{1,5},{5... | collective-permute-start | bytes 835592 | tf_op jit(solution)/shard_map/ppermute | solution.py:37
  671.2 9.5 %collective-permute-start.61 = (f32[544,128]{1,0:T(8,128)S(1)}, f32[544,128]{1,0:T(8,128)S(1)}, u32[]{:S(2)}, u32[]{:S(2)}) collective-permute-start(f32[544,128]{1,0:T(8,128)S(1)} %get-tuple-element.157), channel_id=1, source_target_pairs={{0,2},{1,3},{2,0},{3,1},{4,6},{5,7},{6,4},{7,5},{8,10},{9,11},{10,... | collective-permute-start | bytes 835592 | tf_op jit(solution)/shard_map/ppermute | solution.py:37
  672.5 36.1 %collective-permute-start.59 = (f32[2064,128]{1,0:T(8,128)S(1)}, f32[2064,128]{1,0:T(8,128)}, u32[]{:S(2)}, u32[]{:S(2)}) collective-permute-start(f32[2064,128]{1,0:T(8,128)S(1)} %pad_maximum_fusion.10.refs_0_), channel_id=1, source_target_pairs={{0,2},{1,3},{2,0},{3,1},{4,6},{5,7},{6,4},{7,5},{8,10},{9,11},{10,... | collective-permute-start | bytes 3170312 | tf_op jit(solution)/shard_map/ppermute | solution.py:37
  673.4 65.9 %collective-permute-start.58 = (f32[2064,128]{1,0:T(8,128)S(1)}, f32[2064,128]{1,0:T(8,128)}, u32[]{:S(2)}, u32[]{:S(2)}) collective-permute-start(f32[2064,128]{1,0:T(8,128)S(1)} %pad_maximum_fusion.10.refs_0_), channel_id=1, source_target_pairs={{0,1},{1,0},{2,3},{3,2},{4,5},{5,4},{6,7},{7,6},{8,9},{9,8},{10,11... | collective-permute-start | bytes 3170312 | tf_op jit(solution)/shard_map/ppermute | solution.py:37
  675.4 33.0 %collective-permute-start.62 = (f32[544,128]{1,0:T(8,128)S(1)}, f32[544,128]{1,0:T(8,128)S(1)}, u32[]{:S(2)}, u32[]{:S(2)}) collective-permute-start(f32[544,128]{1,0:T(8,128)S(1)} %get-tuple-element.155), channel_id=1, source_target_pairs={{0,2},{1,3},{2,0},{3,1},{4,6},{5,7},{6,4},{7,5},{8,10},{9,11},{10,... | collective-permute-start | bytes 835592 | tf_op jit(solution)/shard_map/ppermute | solution.py:37
  708.6 20.3 %collective-permute-start.63 = (f32[2176,128]{1,0:T(8,128)S(1)}, f32[2176,128]{1,0:T(8,128)S(1)}, u32[]{:S(2)}, u32[]{:S(2)}) collective-permute-start(f32[2176,128]{1,0:T(8,128)S(1)} %pad_maximum_fusion.9.refs_0_), channel_id=1, source_target_pairs={{0,1},{1,0},{2,3},{3,2},{4,5},{5,4},{6,7},{7,6},{8,9},{9,8},{10,11... | collective-permute-start | bytes 3342344 | tf_op jit(solution)/shard_map/ppermute | solution.py:37
  708.7 30.6 %collective-permute-start.60 = (f32[2064,128]{1,0:T(8,128)}, f32[2064,128]{1,0:T(8,128)}, u32[]{:S(2)}, u32[]{:S(2)}) collective-permute-start(f32[2064,128]{1,0:T(8,128)} %collective-permute-done.59.refs_2_), channel_id=1, source_target_pairs={{0,1},{1,0},{2,3},{3,2},{4,5},{5,4},{6,7},{7,6},{8,9},{9,8},{10,11... | collective-permute-start | bytes 3170312 | tf_op jit(solution)/shard_map/ppermute | solution.py:37
  (126 other events, 993.9 us)
Sparse Core Ops, SparseCore 0:
  11.5 125.7 all-gather.2
  140.7 77.7 all-gather.4
